TPU v7x, 32 devices: a whole 2x2x4 slice. The times are simulated.
32 devices in a mesh: dp: 4 (over z), expert: 8 (over y, x, core).
Axes of the slice: x: 2, y: 2, z: 4, core: 2. Of those that a mesh axis runs over, the one named last changes fastest.
Arguments:
- block_input_vectors: bfloat16 [8, 1024, 1280], P('expert', 'dp'), may hold values from -6 to 6
- output_sensitivity: bfloat16 [8, 1024, 1280], P('expert', 'dp'), may hold values from -6 to 6
- rotary_offsets: int32 [8, 1024], P('expert'), may hold values from 0 to 895, as said below
- dispatched_specialist_ids: int32 [8, 1024, 7], P('expert', 'dp'), may hold values from 0 to 15, all different within a row; in each aligned block of 256 rows (0 to 255, 256 to 511, ..., all dimensions but the last counted through in order) at most 224 rows name the same one
- specialist_quotas: int32 [16], replicated, may hold values from 112 to 224
- storage_holder: int32 [16], replicated, may hold values from 0 to 15, each once
- mixer_projection_matrices: float32 [4, 1280, 1280], P(None, ('dp', 'expert'))
- mixer_mean_estimate: float32 [4, 1280, 1280], P(None, ('dp', 'expert'))
- mixer_variance_estimate: float32 [4, 1280, 1280], P(None, ('dp', 'expert'))
- common_projection_matrices: float32 [3, 1280, 896], P(None, ('dp', 'expert'))
- common_mean_estimate: float32 [3, 1280, 896], P(None, ('dp', 'expert'))
- common_variance_estimate: float32 [3, 1280, 896], P(None, ('dp', 'expert'))
- gating_projection_matrix: float32 [1280, 16], P(('dp', 'expert')), may hold values from -0.078125 to 0.078125
- gating_mean_estimate: float32 [1280, 16], P(('dp', 'expert'))
- gating_variance_estimate: float32 [1280, 16], P(('dp', 'expert'))
- scaling_factors: float32 [2, 1280], P(None, ('dp', 'expert'))
- scaling_mean_estimate: float32 [2, 1280], P(None, ('dp', 'expert'))
- scaling_variance_estimate: float32 [2, 1280], P(None, ('dp', 'expert'))
- dispatched_projection_matrices: float32 [16, 3, 1280, 896], P('expert', None, 'dp')
- dispatched_mean_estimate: float32 [16, 3, 1280, 896], P('expert', None, 'dp')
- dispatched_variance_estimate: float32 [16, 3, 1280, 896], P('expert', None, 'dp')
Outputs:
- block_out: bfloat16 [8, 1024, 1280], P('expert', 'dp')
- input_grad: float32 [8, 1024, 1280], P('expert', 'dp')
- grad_norm: float32 [], replicated
- attn_new: float32 [4, 1280, 1280], P(None, ('dp', 'expert'))
- attn_moment: float32 [4, 1280, 1280], P(None, ('dp', 'expert'))
- attn_square: float32 [4, 1280, 1280], P(None, ('dp', 'expert'))
- attn_copy: bfloat16 [4, 1280, 1280], P(None, ('dp', 'expert'))
- shared_new: float32 [3, 1280, 896], P(None, ('dp', 'expert'))
- shared_moment: float32 [3, 1280, 896], P(None, ('dp', 'expert'))
- shared_square: float32 [3, 1280, 896], P(None, ('dp', 'expert'))
- shared_copy: bfloat16 [3, 1280, 896], P(None, ('dp', 'expert'))
- router_new: float32 [1280, 16], P(('dp', 'expert'))
- router_moment: float32 [1280, 16], P(('dp', 'expert'))
- router_square: float32 [1280, 16], P(('dp', 'expert'))
- router_copy: bfloat16 [1280, 16], P(('dp', 'expert'))
- gain_new: float32 [2, 1280], P(None, ('dp', 'expert'))
- gain_moment: float32 [2, 1280], P(None, ('dp', 'expert'))
- gain_square: float32 [2, 1280], P(None, ('dp', 'expert'))
- expert_new: float32 [16, 3, 1280, 896], P('expert', None, 'dp')
- expert_moment: float32 [16, 3, 1280, 896], P('expert', None, 'dp')
- expert_square: float32 [16, 3, 1280, 896], P('expert', None, 'dp')
- expert_copy: bfloat16 [16, 3, 1280, 896], P('expert', None, 'dp')
Inputs may be any that keep to these rules, and one draw needn't show every extreme that they name: `rotary_offsets`: each sequence holds three documents; positions count from 0 at each document's start; the middle document holds exactly 896 tokens, begins within the first 128 tokens and ends within the last 128. `dispatched_specialist_ids`: within the rows of one device no expert is named more than 224 times. `storage_holder`: A permutation; storage row r lies on index r // 2 of the expert axis.
All inputs are finite; a program needn't handle non-finite values.
Results may differ from a plain program's by a relative error of at most 0.02.
The roundings to bfloat16 on the way count: a program that leaves them out, or rounds other values in their place, can miss the bound.
Values may be sent and summed in bfloat16 or wider, within the bound.
No kernel may reach another device: no remote copies, remote signals or barrier semaphores. Data moves between devices by JAX's collectives and lax.ppermute only.
A program may use at most 384 MiB of HBM per device.

v0:
```python
import jax
import jax.numpy as jnp
from jax import lax
from jax.sharding import PartitionSpec as P

HEAD_DIM = 128
STEP = 10


NORM_EPS = 1e-06
THETA = 10000.0
CLIP_VALUE = 1.0
BETA_ONE = 0.9
BETA_TWO = 0.999
ADAM_EPS = 1e-08
DECAY = 0.1
RATE_MATRIX = 0.02
RATE_EXPERT = 0.1
RATE_GAIN = 0.3
MASKED = -1e30


def contract(left, right, left_dim, right_dim):
    return lax.dot_general(
        left, right, (((left_dim,), (right_dim,)), ((), ())), preferred_element_type=jnp.float32
    )


def rotary_tables(places, head_dim):
    half = head_dim // 2
    freq = THETA ** (-2.0 * jnp.arange(half, dtype=jnp.float32) / head_dim)
    angle = places.astype(jnp.float32)[:, None] * freq
    cosine = jnp.concatenate([jnp.cos(angle), jnp.cos(angle)], -1)[:, None, :]
    sine = jnp.concatenate([jnp.sin(angle), jnp.sin(angle)], -1)[:, None, :]
    return (cosine, sine)


def turn(values, cosine, sine):
    half = values.shape[-1] // 2
    turned = jnp.concatenate([-values[..., half:], values[..., :half]], -1)
    return values * cosine + turned * sine


def norm_forward(values, gain):
    inverse = lax.rsqrt(jnp.mean(values * values, axis=-1, keepdims=True) + NORM_EPS)
    scaled = values * inverse
    return ((scaled * gain).astype(jnp.bfloat16), scaled, inverse)


def norm_backward(grad, scaled, inverse, gain):
    gain_grad = jnp.sum(grad * scaled, axis=0)
    local = grad * gain
    return (
        inverse * (local - scaled * jnp.mean(local * scaled, axis=-1, keepdims=True)),
        gain_grad,
    )


def assignment_place_number(
    linear_specialist_position, specialist_quotas, storage_holder, block_ordinal
):
    specialist_total = specialist_quotas.shape[0]
    specialist_indicator = (
        linear_specialist_position[:, None]
        == jnp.arange(specialist_total, dtype=jnp.int32)[None, :]
    ).astype(jnp.int32)
    earlier = jnp.cumsum(specialist_indicator, axis=0) - specialist_indicator
    rank = jnp.sum(earlier * specialist_indicator, axis=1)
    quota_ceiling = jnp.sum(specialist_indicator * specialist_quotas[None, :], axis=1)
    storage = jnp.sum(specialist_indicator * storage_holder[None, :], axis=1)
    retained_indicator = rank < quota_ceiling
    place_number = jnp.where(
        retained_indicator, storage * block_ordinal + rank, specialist_total * block_ordinal
    )
    return (place_number, retained_indicator, specialist_indicator)


def slot_owners(place_number, specialist_total, block_ordinal):
    count = place_number.shape[0]
    table = jnp.full((specialist_total * block_ordinal + 1,), count, jnp.int32)
    table = table.at[place_number].set(jnp.arange(count, dtype=jnp.int32))
    return table[: specialist_total * block_ordinal]


def adam(master, first, second, grad, scale, rate):
    clipped = grad * scale
    first_new = BETA_ONE * first + (1.0 - BETA_ONE) * clipped
    second_new = BETA_TWO * second + (1.0 - BETA_TWO) * clipped * clipped
    first_hat = first_new / (1.0 - BETA_ONE**STEP)
    second_hat = second_new / (1.0 - BETA_TWO**STEP)
    master_new = master - rate * (first_hat / (jnp.sqrt(second_hat) + ADAM_EPS) + DECAY * master)
    return (master_new, first_new, second_new)


def body(
    block_input_vectors,
    output_sensitivity,
    rotary_offsets,
    dispatched_specialist_ids,
    specialist_quotas,
    storage_holder,
    mixer_projection_matrices,
    mixer_mean_estimate,
    mixer_variance_estimate,
    common_projection_matrices,
    common_mean_estimate,
    common_variance_estimate,
    gating_projection_matrix,
    gating_mean_estimate,
    gating_variance_estimate,
    scaling_factors,
    scaling_mean_estimate,
    scaling_variance_estimate,
    dispatched_projection_matrices,
    dispatched_mean_estimate,
    dispatched_variance_estimate,
):
    token_rows = block_input_vectors.shape[1]
    width = block_input_vectors.shape[2]
    head_dim = HEAD_DIM
    heads = width // head_dim
    length = rotary_offsets.shape[1]
    top_choice_count = dispatched_specialist_ids.shape[2]
    specialist_total = specialist_quotas.shape[0]
    expert_local = dispatched_projection_matrices.shape[0]
    groups = lax.axis_size("expert")
    block_ordinal = min(token_rows, 2 * token_rows * top_choice_count // specialist_total)
    block = min(512, length)
    scale_attn = head_dim ** (-0.5)
    attn_low, shared_low, router_low, gain_low = (
        lax.all_gather(
            mixer_projection_matrices.astype(jnp.bfloat16), ("dp", "expert"), axis=1, tiled=True
        ),
        lax.all_gather(
            common_projection_matrices.astype(jnp.bfloat16), ("dp", "expert"), axis=1, tiled=True
        ),
        lax.all_gather(
            gating_projection_matrix.astype(jnp.bfloat16), ("dp", "expert"), axis=0, tiled=True
        ),
        lax.all_gather(scaling_factors.astype(jnp.bfloat16), ("dp", "expert"), axis=1, tiled=True),
    )
    expert_low = lax.all_gather(
        dispatched_projection_matrices.astype(jnp.bfloat16), "dp", axis=2, tiled=True
    )
    gain_one = gain_low[0].astype(jnp.float32)
    gain_two = gain_low[1].astype(jnp.float32)
    inputs = block_input_vectors[0].astype(jnp.float32)
    normed, scaled_one, inverse_one = norm_forward(inputs, gain_one)
    place = lax.axis_index("dp") * token_rows
    own_positions = lax.dynamic_slice_in_dim(rotary_offsets[0], place, token_rows)
    cosine, sine = rotary_tables(own_positions, head_dim)
    query = turn(
        contract(normed, attn_low[0], 1, 0).reshape(token_rows, heads, head_dim), cosine, sine
    ).astype(jnp.bfloat16)
    key_part = turn(
        contract(normed, attn_low[1], 1, 0).reshape(token_rows, heads, head_dim), cosine, sine
    ).astype(jnp.bfloat16)
    value_part = (
        contract(normed, attn_low[2], 1, 0)
        .astype(jnp.bfloat16)
        .reshape(token_rows, heads, head_dim)
    )
    keys_all, values_all = (
        lax.all_gather(key_part, "dp", axis=0, tiled=True),
        lax.all_gather(value_part, "dp", axis=0, tiled=True),
    )
    starts = jnp.arange(length, dtype=jnp.int32) - rotary_offsets[0]
    query_index = place + jnp.arange(token_rows, dtype=jnp.int32)
    query_start = lax.dynamic_slice_in_dim(starts, place, token_rows)
    blocks_used = (place + token_rows + block - 1) // block

    def block_scores(number):
        begin = number * block
        keys = lax.dynamic_slice_in_dim(keys_all, begin, block, 0)
        raw = (
            jnp.einsum("qhd,khd->hqk", query, keys, preferred_element_type=jnp.float32) * scale_attn
        )
        key_index = begin + jnp.arange(block, dtype=jnp.int32)
        key_start = lax.dynamic_slice_in_dim(starts, begin, block)
        allowed = (query_start[:, None] == key_start[None, :]) & (
            key_index[None, :] <= query_index[:, None]
        )
        return (jnp.where(allowed[None], raw, MASKED), allowed[None])

    def stats_step(number, carry):
        peak, total = carry
        scores, allowed = block_scores(number)
        peak_new = jnp.maximum(peak, jnp.max(scores, axis=-1))
        total = total * jnp.exp(peak - peak_new) + jnp.sum(
            jnp.where(allowed, jnp.exp(scores - peak_new[..., None]), 0.0), axis=-1
        )
        return (peak_new, total)

    peak, total = lax.fori_loop(
        0,
        blocks_used,
        stats_step,
        (
            jnp.full((heads, token_rows), MASKED, jnp.float32),
            jnp.zeros((heads, token_rows), jnp.float32),
        ),
    )
    log_total = peak + jnp.log(total)

    def value_step(number, mixed):
        scores, allowed = block_scores(number)
        weights = jnp.exp(scores - log_total[..., None]).astype(jnp.bfloat16)
        values = lax.dynamic_slice_in_dim(values_all, number * block, block, 0)
        return mixed + jnp.einsum(
            "hqk,khd->qhd", weights, values, preferred_element_type=jnp.float32
        )

    mixed = lax.fori_loop(
        0, blocks_used, value_step, jnp.zeros((token_rows, heads, head_dim), jnp.float32)
    )
    mixed_low = mixed.reshape(token_rows, width).astype(jnp.bfloat16)
    middle = inputs + contract(mixed_low, attn_low[3], 1, 0)
    second, scaled_two, inverse_two = norm_forward(middle, gain_two)
    probs = jax.nn.softmax(contract(second, router_low, 1, 0), axis=-1)
    gate_shared = contract(second, shared_low[0], 1, 0)
    up_shared = contract(second, shared_low[1], 1, 0)
    hidden_shared = (jax.nn.silu(gate_shared) * up_shared).astype(jnp.bfloat16)
    shared_out = contract(hidden_shared, shared_low[2], 1, 1)
    place_number, retained_indicator, specialist_indicator = assignment_place_number(
        dispatched_specialist_ids[0].reshape(token_rows * top_choice_count),
        specialist_quotas,
        storage_holder,
        block_ordinal,
    )
    owners_of_slots = slot_owners(place_number, specialist_total, block_ordinal)
    padded = jnp.concatenate([second, jnp.zeros((1, width), jnp.bfloat16)], 0)
    outgoing = padded[owners_of_slots // top_choice_count].reshape(
        groups, expert_local, block_ordinal, width
    )
    received = lax.all_to_all(outgoing, "expert", split_axis=0, concat_axis=0, tiled=True)
    gate_part = jnp.einsum(
        "sepd,edf->sepf", received, expert_low[:, 0], preferred_element_type=jnp.float32
    )
    up_part = jnp.einsum(
        "sepd,edf->sepf", received, expert_low[:, 1], preferred_element_type=jnp.float32
    )
    hidden = (jax.nn.silu(gate_part) * up_part).astype(jnp.bfloat16)
    result = jnp.einsum(
        "sepf,edf->sepd", hidden, expert_low[:, 2], preferred_element_type=jnp.float32
    ).astype(jnp.bfloat16)
    returned = lax.all_to_all(result, "expert", split_axis=0, concat_axis=0, tiled=True)
    returned, received, gate_part, up_part, hidden = (
        returned,
        received,
        gate_part,
        up_part,
        hidden,
    )
    result_pad = jnp.concatenate(
        [
            returned.reshape(specialist_total * block_ordinal, width),
            jnp.zeros((1, width), jnp.bfloat16),
        ],
        0,
    )
    pair_result = result_pad[place_number].reshape(token_rows, top_choice_count, width)
    pair_onehot = specialist_indicator.reshape(token_rows, top_choice_count, specialist_total)
    pair_prob = jnp.sum(pair_onehot * probs[:, None, :], axis=-1)
    kept = retained_indicator.reshape(token_rows, top_choice_count)
    gate = jnp.where(kept, pair_prob, 0.0)
    routed = jnp.sum(gate[..., None] * pair_result.astype(jnp.float32), axis=1)
    block_out = (middle + shared_out + routed).astype(jnp.bfloat16)
    grad_out = output_sensitivity[0].astype(jnp.float32)
    grad_low = output_sensitivity[0]
    grad_gate = jnp.where(
        kept, jnp.sum(grad_out[:, None, :] * pair_result.astype(jnp.float32), axis=-1), 0.0
    )
    grad_pair = (
        (gate[..., None] * grad_out[:, None, :])
        .astype(jnp.bfloat16)
        .reshape(token_rows * top_choice_count, width)
    )
    grad_pad = jnp.concatenate([grad_pair, jnp.zeros((1, width), jnp.bfloat16)], 0)
    grad_outgoing = grad_pad[owners_of_slots].reshape(groups, expert_local, block_ordinal, width)
    grad_received = lax.all_to_all(grad_outgoing, "expert", split_axis=0, concat_axis=0, tiled=True)
    grad_hidden = jnp.einsum(
        "sepd,edf->sepf", grad_received, expert_low[:, 2], preferred_element_type=jnp.float32
    )
    down_grad = jnp.einsum(
        "sepd,sepf->edf", grad_received, hidden, preferred_element_type=jnp.float32
    )
    sigma = jax.nn.sigmoid(gate_part)
    grad_gate_part = (grad_hidden * up_part * sigma * (1.0 + gate_part * (1.0 - sigma))).astype(
        jnp.bfloat16
    )
    grad_up_part = (grad_hidden * gate_part * sigma).astype(jnp.bfloat16)
    gate_weight_grad = jnp.einsum(
        "sepd,sepf->edf", received, grad_gate_part, preferred_element_type=jnp.float32
    )
    up_weight_grad = jnp.einsum(
        "sepd,sepf->edf", received, grad_up_part, preferred_element_type=jnp.float32
    )
    grad_entry = (
        jnp.einsum(
            "sepf,edf->sepd", grad_gate_part, expert_low[:, 0], preferred_element_type=jnp.float32
        )
        + jnp.einsum(
            "sepf,edf->sepd", grad_up_part, expert_low[:, 1], preferred_element_type=jnp.float32
        )
    ).astype(jnp.bfloat16)
    grad_back = lax.all_to_all(grad_entry, "expert", split_axis=0, concat_axis=0, tiled=True)
    back_pad = jnp.concatenate(
        [
            grad_back.reshape(specialist_total * block_ordinal, width),
            jnp.zeros((1, width), jnp.bfloat16),
        ],
        0,
    )
    grad_second = jnp.sum(
        back_pad[place_number].reshape(token_rows, top_choice_count, width).astype(jnp.float32),
        axis=1,
    )
    grad_prob = jnp.sum(grad_gate[..., None] * pair_onehot, axis=1)
    grad_logit = (probs * (grad_prob - jnp.sum(probs * grad_prob, axis=-1, keepdims=True))).astype(
        jnp.bfloat16
    )
    router_grad = contract(second, grad_logit, 0, 0)
    grad_second = grad_second + contract(grad_logit, router_low, 1, 1)
    shared_down_grad = contract(grad_low, hidden_shared, 0, 0)
    grad_hidden_shared = contract(grad_low, shared_low[2], 1, 0)
    sigma_shared = jax.nn.sigmoid(gate_shared)
    grad_gate_shared = (
        grad_hidden_shared * up_shared * sigma_shared * (1.0 + gate_shared * (1.0 - sigma_shared))
    ).astype(jnp.bfloat16)
    grad_up_shared = (grad_hidden_shared * gate_shared * sigma_shared).astype(jnp.bfloat16)
    shared_gate_grad = contract(second, grad_gate_shared, 0, 0)
    shared_up_grad = contract(second, grad_up_shared, 0, 0)
    grad_second = (
        grad_second
        + contract(grad_gate_shared, shared_low[0], 1, 1)
        + contract(grad_up_shared, shared_low[1], 1, 1)
    )
    grad_middle, gain_two_grad = norm_backward(grad_second, scaled_two, inverse_two, gain_two)
    grad_middle = grad_middle + grad_out
    grad_attn_out = grad_middle.astype(jnp.bfloat16)
    out_grad = contract(mixed_low, grad_attn_out, 0, 0)
    grad_mixed = (
        contract(grad_attn_out, attn_low[3], 1, 1)
        .astype(jnp.bfloat16)
        .reshape(token_rows, heads, head_dim)
    )
    correction = jnp.sum(grad_mixed.astype(jnp.float32) * mixed, axis=-1).T

    def grad_step(number, carry):
        grad_query, grad_keys, grad_values = carry
        begin = number * block
        scores, allowed = block_scores(number)
        weights = jnp.exp(scores - log_total[..., None])
        keys = lax.dynamic_slice_in_dim(keys_all, begin, block, 0)
        values = lax.dynamic_slice_in_dim(values_all, begin, block, 0)
        grad_weights = jnp.einsum(
            "qhd,khd->hqk", grad_mixed, values, preferred_element_type=jnp.float32
        )
        grad_scores = (weights * (grad_weights - correction[..., None])).astype(jnp.bfloat16)
        grad_query = (
            grad_query
            + jnp.einsum("hqk,khd->qhd", grad_scores, keys, preferred_element_type=jnp.float32)
            * scale_attn
        )
        key_term = (
            jnp.einsum("hqk,qhd->khd", grad_scores, query, preferred_element_type=jnp.float32)
            * scale_attn
        )
        value_term = jnp.einsum(
            "hqk,qhd->khd",
            weights.astype(jnp.bfloat16),
            grad_mixed,
            preferred_element_type=jnp.float32,
        )
        grad_keys = lax.dynamic_update_slice_in_dim(grad_keys, key_term, begin, 0)
        grad_values = lax.dynamic_update_slice_in_dim(grad_values, value_term, begin, 0)
        return (grad_query, grad_keys, grad_values)

    empty_keys = jnp.zeros((length, heads, head_dim), jnp.float32)
    grad_query, grad_keys, grad_values = lax.fori_loop(
        0,
        blocks_used,
        grad_step,
        (jnp.zeros((token_rows, heads, head_dim), jnp.float32), empty_keys, empty_keys),
    )
    grad_keys_own, grad_values_own = (
        lax.psum_scatter(
            grad_keys.astype(jnp.bfloat16), "dp", scatter_dimension=0, tiled=True
        ).astype(jnp.float32),
        lax.psum_scatter(
            grad_values.astype(jnp.bfloat16), "dp", scatter_dimension=0, tiled=True
        ).astype(jnp.float32),
    )
    grad_query_low = turn(grad_query, cosine, -sine).reshape(token_rows, width).astype(jnp.bfloat16)
    grad_key_low = (
        turn(grad_keys_own, cosine, -sine).reshape(token_rows, width).astype(jnp.bfloat16)
    )
    grad_value_low = grad_values_own.reshape(token_rows, width).astype(jnp.bfloat16)
    query_grad = contract(normed, grad_query_low, 0, 0)
    key_grad = contract(normed, grad_key_low, 0, 0)
    value_grad = contract(normed, grad_value_low, 0, 0)
    grad_normed = (
        contract(grad_query_low, attn_low[0], 1, 1)
        + contract(grad_key_low, attn_low[1], 1, 1)
        + contract(grad_value_low, attn_low[2], 1, 1)
    )
    grad_inputs, gain_one_grad = norm_backward(grad_normed, scaled_one, inverse_one, gain_one)
    grad_inputs = grad_inputs + grad_middle
    attn_grad = jnp.stack([query_grad, key_grad, value_grad, out_grad])
    shared_grad = jnp.stack([shared_gate_grad, shared_up_grad, shared_down_grad])
    gain_grad = jnp.stack([gain_one_grad, gain_two_grad])
    expert_grad = jnp.stack([gate_weight_grad, up_weight_grad, down_grad], axis=1)
    attn_sum, shared_sum, router_sum, gain_sum = (
        lax.psum_scatter(attn_grad, ("dp", "expert"), scatter_dimension=1, tiled=True),
        lax.psum_scatter(shared_grad, ("dp", "expert"), scatter_dimension=1, tiled=True),
        lax.psum_scatter(router_grad, ("dp", "expert"), scatter_dimension=0, tiled=True),
        lax.psum_scatter(gain_grad, ("dp", "expert"), scatter_dimension=1, tiled=True),
    )
    expert_sum = lax.psum_scatter(
        expert_grad.astype(jnp.bfloat16), "dp", scatter_dimension=2, tiled=True
    ).astype(jnp.float32)
    local_squares = (
        jnp.sum(attn_sum * attn_sum)
        + jnp.sum(shared_sum * shared_sum)
        + jnp.sum(router_sum * router_sum)
        + jnp.sum(gain_sum * gain_sum)
        + jnp.sum(expert_sum * expert_sum)
    )
    grad_norm = jnp.sqrt(lax.psum(local_squares, ("dp", "expert")))
    scale = jnp.minimum(1.0, CLIP_VALUE / (grad_norm + 1e-06))
    attn_new, attn_moment, attn_square = adam(
        mixer_projection_matrices,
        mixer_mean_estimate,
        mixer_variance_estimate,
        attn_sum,
        scale,
        RATE_MATRIX,
    )
    shared_new, shared_moment, shared_square = adam(
        common_projection_matrices,
        common_mean_estimate,
        common_variance_estimate,
        shared_sum,
        scale,
        RATE_MATRIX,
    )
    router_new, router_moment, router_square = adam(
        gating_projection_matrix,
        gating_mean_estimate,
        gating_variance_estimate,
        router_sum,
        scale,
        RATE_MATRIX,
    )
    gain_new, gain_moment, gain_square = adam(
        scaling_factors,
        scaling_mean_estimate,
        scaling_variance_estimate,
        gain_sum,
        scale,
        RATE_GAIN,
    )
    expert_new, expert_moment, expert_square = adam(
        dispatched_projection_matrices,
        dispatched_mean_estimate,
        dispatched_variance_estimate,
        expert_sum,
        scale,
        RATE_EXPERT,
    )
    return (
        block_out[None],
        grad_inputs[None],
        grad_norm,
        attn_new,
        attn_moment,
        attn_square,
        attn_new.astype(jnp.bfloat16),
        shared_new,
        shared_moment,
        shared_square,
        shared_new.astype(jnp.bfloat16),
        router_new,
        router_moment,
        router_square,
        router_new.astype(jnp.bfloat16),
        gain_new,
        gain_moment,
        gain_square,
        expert_new,
        expert_moment,
        expert_square,
        expert_new.astype(jnp.bfloat16),
    )


def solution(mesh):
    placed = (
        P("expert", "dp", None),
        P("expert", "dp", None),
        P("expert", None),
        P("expert", "dp", None),
        P(),
        P(),
        P(None, ("dp", "expert"), None),
        P(None, ("dp", "expert"), None),
        P(None, ("dp", "expert"), None),
        P(None, ("dp", "expert"), None),
        P(None, ("dp", "expert"), None),
        P(None, ("dp", "expert"), None),
        P(("dp", "expert"), None),
        P(("dp", "expert"), None),
        P(("dp", "expert"), None),
        P(None, ("dp", "expert")),
        P(None, ("dp", "expert")),
        P(None, ("dp", "expert")),
        P("expert", None, "dp", None),
        P("expert", None, "dp", None),
        P("expert", None, "dp", None),
    )
    return jax.shard_map(
        body,
        mesh=mesh,
        in_specs=placed,
        out_specs=(
            P("expert", "dp", None),
            P("expert", "dp", None),
            P(),
            P(None, ("dp", "expert"), None),
            P(None, ("dp", "expert"), None),
            P(None, ("dp", "expert"), None),
            P(None, ("dp", "expert"), None),
            P(None, ("dp", "expert"), None),
            P(None, ("dp", "expert"), None),
            P(None, ("dp", "expert"), None),
            P(None, ("dp", "expert"), None),
            P(("dp", "expert"), None),
            P(("dp", "expert"), None),
            P(("dp", "expert"), None),
            P(("dp", "expert"), None),
            P(None, ("dp", "expert")),
            P(None, ("dp", "expert")),
            P(None, ("dp", "expert")),
            P("expert", None, "dp", None),
            P("expert", None, "dp", None),
            P("expert", None, "dp", None),
            P("expert", None, "dp", None),
        ),
        check_vma=False,
    )
```

profile of v0, /device:TPU:0, one launch (start us, length us, event | category | flops | bytes accessed | tf_op | source)
XLA Modules:
  0.0 1895.0 jit_solution(13469565512051409354)
XLA Ops:
  9.9 43.1 %all-gather = bf16[32,40,2]{1,2,0:T(2,128)(2,1)S(1)} all-gather(bf16[1,40,2]{1,2,0:T(2,128)(2,1)S(1)} %convert_bitcast_fusion.2), channel_id=1, replica_groups=mesh['dp'=4,'expert'=8] {'dp','expert'}, dimensions={0}, use_global_device_ids=true | all-gather | bytes 5280 | tf_op jit(solution)/shard_map/all_gather | solution.py:140
  56.9 55.5 %all-gather.8.cloned.1.call-done = bf16[4,1280,1280]{2,1,0:T(8,128)(2,1)} async-done(((bf16[4,40,1280]{2,1,0:T(8,128)(2,1)}), bf16[4,1280,1280]{2,1,0:T(8,128)(2,1)}) %all-gather.8.cloned.1.call-update) | async-done | bytes 13107216 | tf_op jit(solution)/shard_map/all_gather | solution.py:131
  120.8 5.7 copy.195
  136.8 5.6 copy.305
  143.1 39.8 %all-gather.1 = bf16[32,40,16]{1,2,0:T(8,128)(2,1)S(1)} all-gather(bf16[1,40,16]{1,2,0:T(8,128)(2,1)S(1)} %convert_bitcast_fusion.1), channel_id=1, replica_groups=mesh['dp'=4,'expert'=8] {'dp','expert'}, dimensions={0}, use_global_device_ids=true | all-gather | bytes 42240 | tf_op jit(solution)/shard_map/all_gather | solution.py:137
  194.8 48.5 %all-gather.10.cloned.1.call-done = bf16[1024,10,128]{0,2,1:T(8,128)(2,1)} async-done(((bf16[256,10,128]{0,2,1:T(8,128)(2,1)}), bf16[1024,10,128]{0,2,1:T(8,128)(2,1)}) %all-gather.10.cloned.1.call-update) | async-done | bytes 2621456 | tf_op jit(solution)/shard_map/all_gather | solution.py:165
  244.5 5.2 while.40
  260.1 7.1 scatter_custom_fusion
  267.3 12.5 gather_fusion
  279.8 5.2 all-to-all-start
  290.9 10.0 mul.631
  307.6 22.0 %gather_fusion.2 = bf16[3584,1280]{1,0:T(8,128)(2,1)} fusion(bf16[1793,1280]{1,0:T(8,128)(2,1)} %concatenate.40, s32[4096]{0:T(1024)S(1)} %pad_clamp_fusion), kind=kCustom, calls=%fused_computation.2 | custom fusion | bytes 18364416 | tf_op jit(solution)/shard_map/gather | solution.py:279
  329.6 57.9 %all-to-all-done = bf16[8,2,224,1280]{3,2,1,0:T(8,128)(2,1)} async-done(((bf16[8,2,224,1280]{3,2,1,0:T(8,128)(2,1)}), bf16[8,2,224,1280]{3,2,1,0:T(8,128)(2,1)}, u32[]{:S(2)}, u32[]{:S(2)}) %all-to-all-start) | async-done | bytes 9175072 | tf_op jit(solution)/shard_map/all_to_all | solution.py:235
  387.6 5.4 all-to-all-start.2
  393.0 86.4 %all-gather.16.cloned.1.call-done = bf16[2,3,1280,896]{3,2,0,1:T(8,128)(2,1)} async-done(((bf16[2,3,320,896]{3,2,0,1:T(8,128)(2,1)}), bf16[2,3,1280,896]{3,2,0,1:T(8,128)(2,1)}) %all-gather.16.cloned.1.call-update) | async-done | bytes 13762576 | tf_op jit(solution)/shard_map/all_gather | solution.py:142
  479.4 16.1 fusion.73
  495.6 16.2 fusion.75
  511.8 22.3 %fusion.62 = (bf16[8,2,224,896]{3,2,0,1:T(8,128)(2,1)}, bf16[8,2,224,896]{3,2,0,1:T(8,128)(2,1)}, bf16[8,2,224,896]{3,2,0,1:T(8,128)(2,1)S(1)}) fusion(f32[2,8,224,896]{3,2,1,0:T(8,128)} %fusion.75, f32[2,8,224,896]{3,2,1,0:T(8,128)} %fusion.73, bf16[2,3,1280,896]{3,2,0,1:T(8,128)(2,1)} %all-gather.16.cloned.1.call-done, ...), kind=kOutput, calls=%fused_computation.78 | convolution fusion | flops 8272216064 | bytes 58720256 | tf_op jit(solution)/shard_map/sepd,edf->sepf/dot_general | solution.py:281
  536.8 14.1 fusion.71
  550.9 7.7 copy.209
  564.8 16.6 fusion.101
  581.4 18.0 fusion.72
  599.4 7.7 copy.212
  607.2 78.9 %all-to-all-done.1 = bf16[8,2,224,1280]{3,2,1,0:T(8,128)(2,1)} async-done(((bf16[8,2,224,1280]{3,2,1,0:T(8,128)(2,1)}), bf16[8,2,224,1280]{3,2,1,0:T(8,128)(2,1)}, u32[]{:S(2)}, u32[]{:S(2)}) %all-to-all-start.1) | async-done | bytes 9175072 | tf_op jit(solution)/shard_map/all_to_all | solution.py:246
  700.5 8.1 concatenate.39
  708.7 15.1 gather_fusion.1
  723.7 8.2 reshape.544
  731.9 8.8 multiply_reduce_fusion
  741.0 52.6 %all-to-all-done.3 = bf16[8,2,224,1280]{3,2,1,0:T(8,128)(2,1)} async-done(((bf16[8,2,224,1280]{3,2,1,0:T(8,128)(2,1)}), bf16[8,2,224,1280]{3,2,1,0:T(8,128)(2,1)}, u32[]{:S(2)}, u32[]{:S(2)}) %all-to-all-start.3) | async-done | bytes 9175072 | tf_op jit(solution)/shard_map/all_to_all | solution.py:306
  793.6 7.8 concatenate.41
  801.4 15.1 gather_fusion.3
  816.4 8.5 reshape.545
  824.9 7.1 reduce_sum.218
  852.8 23.8 %while.41 = (s32[]{:T(128)}, f32[256,10,128]{0,2,1:T(8,128)}, bf16[1024,10,128]{0,2,1:T(8,128)(2,1)}, bf16[1024,10,128]{0,2,1:T(8,128)(2,1)}, s32[]{:T(128)}, /*...) while((s32[]{:T(128)}, f32[256,10,128]{0,2,1:T(8,128)}, ...), condition=%wide.region_25.26_spmd.clone, body=%wide.region_24.25_spmd.clone.sunk | while | flops 1693188864 | bytes 101375352 | solution.py:380
  887.7 10.8 pad_maximum_fusion.1
  898.7 14.2 fusion.98
  912.9 14.2 fusion.92
  927.1 14.4 fusion.95
  941.6 6.6 pad_maximum_fusion.2
  968.9 34.2 %reduce-scatter.10.cloned.1.call-done = bf16[256,10,128]{0,2,1:T(8,128)(2,1)} async-done(((bf16[1024,10,128]{0,2,1:T(8,128)(2,1)}), bf16[256,10,128]{0,2,1:T(8,128)(2,1)}) %reduce-scatter.10.cloned.1.call-update) | async-done | bytes 655376 | tf_op jit(solution)/shard_map/reduce_scatter | solution.py:390
  1006.2 14.5 pad_maximum_fusion
  1026.0 102.5 %all-reduce.8.cloned.1.call-done = f32[1280,16]{0,1:T(8,128)} async-done(((f32[1280,16]{0,1:T(8,128)}), f32[1280,16]{0,1:T(8,128)}) %all-reduce.8.cloned.1.call-update) | async-done | bytes 81936
  1139.6 48.0 %all-reduce.5 = f32[2,1280]{1,0:T(2,128)S(1)} all-reduce(f32[2,1280]{1,0:T(2,128)S(1)} %pad_maximum_fusion.5), channel_id=7, replica_groups=mesh['dp'=4,'expert'=8] {'dp','expert'}, use_global_device_ids=true, to_apply=%region_37.38.clone | all-reduce | flops 2560 | bytes 20480
  1188.3 103.7 %reduce-scatter.14.cloned.1.call-done = f32[3,40,896]{2,1,0:T(8,128)} async-done(((f32[3,1280,896]{2,1,0:T(8,128)}), f32[3,40,896]{2,1,0:T(8,128)}) %reduce-scatter.14.cloned.1.call-update) | async-done | bytes 430096 | tf_op jit(solution)/shard_map/reduce_scatter | solution.py:415
  1293.7 229.2 %reduce-scatter.16.cloned.1.call-done = bf16[2,3,320,896]{3,2,0,1:T(8,128)(2,1)} async-done(((bf16[2,3,1280,896]{3,2,0,1:T(8,128)(2,1)}), bf16[2,3,320,896]{3,2,0,1:T(8,128)(2,1)}) %reduce-scatter.16.cloned.1.call-update) | async-done | bytes 3440656 | tf_op jit(solution)/shard_map/reduce_scatter | solution.py:419
  1527.2 277.7 %reduce-scatter.12.cloned.1.call-done = f32[4,40,1280]{2,1,0:T(8,128)} async-done(((f32[4,1280,1280]{2,1,0:T(8,128)}), f32[4,40,1280]{2,1,0:T(8,128)}) %reduce-scatter.12.cloned.1.call-update) | async-done | bytes 819216 | tf_op jit(solution)/shard_map/reduce_scatter | solution.py:414
  1811.5 46.1 %psum.7 = f32[]{:T(128)} all-reduce(f32[]{:T(128)S(6)} %add.348), channel_id=1, replica_groups=mesh['dp'=4,'expert'=8] {'dp','expert'}, use_global_device_ids=true, to_apply=%region_41.42 | all-reduce | flops 1 | bytes 8 | tf_op jit(solution)/shard_map/psum | solution.py:429
  1858.4 10.6 fusion.182
  (367 shorter events, 215.5 us)
Async XLA Ops:
  7.2 105.2 %all-gather.8.cloned.1.call-start = ((), (), s32[]{:S(2)}) async-start(), calls=%async_computation.9 | async-start | bytes 13516800 | tf_op jit(solution)/shard_map/all_gather | solution.py:131
  9.2 179.8 %all-gather.12.cloned.1.call-start = ((), (), s32[]{:S(2)}) async-start(), calls=%async_computation.11 | async-start | bytes 3276800 | tf_op jit(solution)/shard_map/all_gather | solution.py:164
  53.9 78.7 %copy-start.58 = (f32[1280]{0:T(1024)}, f32[1280]{0:T(1024)S(1)}, u32[]{:S(2)}) copy-start(f32[1280]{0:T(1024)S(1)} %get-tuple-element.568) | copy-start | bytes 15364
  53.9 202.4 %copy-start.60 = (f32[1280]{0:T(1024)}, f32[1280]{0:T(1024)S(1)}, u32[]{:S(2)}) copy-start(f32[1280]{0:T(1024)S(1)} %get-tuple-element.567) | copy-start | bytes 15364
  54.3 76.9 %copy-start.41 = (f32[256,128]{0,1:T(8,128)}, f32[256,128]{0,1:T(8,128)S(1)}, u32[]{:S(2)}) copy-start(f32[256,128]{0,1:T(8,128)S(1)} %pad_maximum_fusion.3) | copy-start | bytes 393220
  132.6 110.8 %all-gather.10.cloned.1.call-start = ((), (), s32[]{:S(2)}) async-start(), calls=%async_computation.10 | async-start | bytes 3276800 | tf_op jit(solution)/shard_map/all_gather | solution.py:165
  136.7 342.7 %all-gather.16.cloned.1.call-start = ((), (), s32[]{:S(2)}) async-start(), calls=%async_computation.13 | async-start | bytes 17203200 | tf_op jit(solution)/shard_map/all_gather | solution.py:142
  142.4 46.1 %copy-start.90 = (s32[16]{0:T(128)S(1)}, s32[16]{0:T(128)}, u32[]{:S(2)}) copy-start(s32[16]{0:T(128)} %param.32) | copy-start | bytes 196
  142.4 46.1 %copy-start.91 = (s32[16]{0:T(128)S(1)}, s32[16]{0:T(128)}, u32[]{:S(2)}) copy-start(s32[16]{0:T(128)} %param.31) | copy-start | bytes 196
  142.4 115.6 %copy-start.64 = (s32[1,256,7]{1,2,0:T(8,128)}, s32[1,256,7]{1,2,0:T(8,128)S(1)}, u32[]{:S(2)}) copy-start(s32[1,256,7]{1,2,0:T(8,128)S(1)} %copy.311) | copy-start | bytes 21508
  183.2 74.4 %copy-start.52 = (bf16[1280,16]{0,1:T(8,128)(2,1)}, bf16[1280,16]{0,1:T(8,128)(2,1)S(1)}, u32[]{:S(2)}) copy-start(bf16[1280,16]{0,1:T(8,128)(2,1)S(1)} %reshape.591) | copy-start | bytes 122884
  249.7 6.6 copy-start
  249.7 6.6 copy-start.3
  249.7 6.6 copy-start.54
  249.7 6.6 copy-start.56
  249.7 6.6 copy-start.78
  257.6 22.2 %copy-start.7 = (bf16[256,1280]{1,0:T(8,128)(2,1)}, bf16[256,1280]{1,0:T(8,128)(2,1)S(1)}, u32[]{:S(2)}) copy-start(bf16[256,1280]{1,0:T(8,128)(2,1)S(1)} %multiply_convert_fusion.1) | copy-start | bytes 1966084
  257.9 21.9 %copy-start.74 = (f32[256]{0:T(256)}, f32[256]{0:T(256)S(1)}, u32[]{:S(2)}) copy-start(f32[256]{0:T(256)S(1)} %get-tuple-element.686) | copy-start | bytes 3076
  259.4 20.4 %copy-start.76 = (pred[1792]{0:T(1024)(128)(4,1)}, pred[1792]{0:T(1024)(128)(4,1)S(1)}, u32[]{:S(2)}) copy-start(pred[1792]{0:T(1024)(128)(4,1)S(1)} %get-tuple-element.655) | copy-start | bytes 5380
  279.8 107.7 %all-to-all-start = ((bf16[8,2,224,1280]{3,2,1,0:T(8,128)(2,1)}), bf16[8,2,224,1280]{3,2,1,0:T(8,128)(2,1)}, u32[]{:S(2)}, u32[]{:S(2)}) async-start(bf16[8,2,224,1280]{3,2,1,0:T(8,128)(2,1)} %bitcast.383), calls=%async_computation | async-start | bytes 18350080 | tf_op jit(solution)/shard_map/all_to_all | solution.py:235
  387.6 124.2 %all-to-all-start.2 = ((bf16[8,2,224,1280]{3,2,1,0:T(8,128)(2,1)}), bf16[8,2,224,1280]{3,2,1,0:T(8,128)(2,1)}, u32[]{:S(2)}, u32[]{:S(2)}) async-start(bf16[8,2,224,1280]{3,2,1,0:T(8,128)(2,1)} %bitcast.384), calls=%async_computation.2 | async-start | bytes 18350080 | tf_op jit(solution)/shard_map/all_to_all | solution.py:280
  558.6 127.4 %all-to-all-start.1 = ((bf16[8,2,224,1280]{3,2,1,0:T(8,128)(2,1)}), bf16[8,2,224,1280]{3,2,1,0:T(8,128)(2,1)}, u32[]{:S(2)}, u32[]{:S(2)}) async-start(bf16[8,2,224,1280]{3,2,1,0:T(8,128)(2,1)} %copy.209), calls=%async_computation.1 | async-start | bytes 18350080 | tf_op jit(solution)/shard_map/all_to_all | solution.py:246
  563.8 128.1 %all-gather.14.cloned.1.call-start = ((), (), s32[]{:S(2)}) async-start(), calls=%async_computation.12 | async-start | bytes 7096320 | tf_op jit(solution)/shard_map/all_gather | solution.py:134
  607.2 84.2 %copy-start.77 = (pred[1792]{0:T(1024)(128)(4,1)S(1)}, pred[1792]{0:T(1024)(128)(4,1)}, u32[]{:S(2)}) copy-start(pred[1792]{0:T(1024)(128)(4,1)} %copy-done.76) | copy-start | bytes 5380
  607.2 84.5 %copy-start.63 = (f32[256,7]{0,1:T(8,128)S(1)}, f32[256,7]{0,1:T(8,128)}, u32[]{:S(2)}) copy-start(f32[256,7]{0,1:T(8,128)} %copy-done.62) | copy-start | bytes 21508
  607.2 84.7 %copy-start.72 = (s32[1792]{0:T(1024)S(1)}, s32[1792]{0:T(1024)}, u32[]{:S(2)}) copy-start(s32[1792]{0:T(1024)} %copy-done.71) | copy-start | bytes 21508
  607.2 84.8 %copy-start.8 = (bf16[256,1280]{1,0:T(8,128)(2,1)S(1)}, bf16[256,1280]{1,0:T(8,128)(2,1)}, u32[]{:S(2)}) copy-start(bf16[256,1280]{1,0:T(8,128)(2,1)} %copy-done.7) | copy-start | bytes 1966084
  686.1 107.5 %all-to-all-start.3 = ((bf16[8,2,224,1280]{3,2,1,0:T(8,128)(2,1)}), bf16[8,2,224,1280]{3,2,1,0:T(8,128)(2,1)}, u32[]{:S(2)}, u32[]{:S(2)}) async-start(bf16[8,2,224,1280]{3,2,1,0:T(8,128)(2,1)} %copy.212), calls=%async_computation.3 | async-start | bytes 18350080 | tf_op jit(solution)/shard_map/all_to_all | solution.py:306
  691.1 264.7 %reduce-scatter.8.cloned.1.call-start = ((), (), s32[]{:S(2)}) async-start(), calls=%async_computation.14 | async-start | bytes 3276800 | tf_op jit(solution)/shard_map/reduce_scatter | solution.py:387
  700.5 131.9 %copy-start.36 = (bf16[256,896]{1,0:T(8,128)(2,1)}, bf16[256,896]{1,0:T(8,128)(2,1)S(1)}, u32[]{:S(2)}) copy-start(bf16[256,896]{1,0:T(8,128)(2,1)S(1)} %get-tuple-element.666) | copy-start | bytes 1376260
  700.5 134.5 %copy-start.34 = (bf16[256,896]{1,0:T(8,128)(2,1)}, bf16[256,896]{1,0:T(8,128)(2,1)S(1)}, u32[]{:S(2)}) copy-start(bf16[256,896]{1,0:T(8,128)(2,1)S(1)} %get-tuple-element.665) | copy-start | bytes 1376260
  723.7 8.2 copy-start.17
  731.9 9.0 copy-start.65
  731.9 9.0 copy-start.51
  731.9 9.0 copy-start.75
  731.9 9.0 copy-start.81
  824.9 7.1 copy-start.53
  844.0 8.8 copy-start.1
  844.0 8.8 copy-start.4
  844.0 8.8 copy-start.55
  844.0 8.8 copy-start.57
  844.0 8.8 copy-start.79
  876.6 126.6 %reduce-scatter.10.cloned.1.call-start = ((), (), s32[]{:S(2)}) async-start(), calls=%async_computation.15 | async-start | bytes 3276800 | tf_op jit(solution)/shard_map/reduce_scatter | solution.py:390
  877.4 251.1 %all-reduce.8.cloned.1.call-start = ((), (), s32[]{:S(2)}) async-start(), calls=%async_computation.19 | async-start | bytes 163840
  887.7 404.3 %reduce-scatter.14.cloned.1.call-start = ((), (), s32[]{:S(2)}) async-start(), calls=%async_computation.17 | async-start | bytes 14192640 | tf_op jit(solution)/shard_map/reduce_scatter | solution.py:415
  898.5 624.4 %reduce-scatter.16.cloned.1.call-start = ((), (), s32[]{:S(2)}) async-start(), calls=%async_computation.18 | async-start | bytes 17203200 | tf_op jit(solution)/shard_map/reduce_scatter | solution.py:419
  948.2 856.7 %reduce-scatter.12.cloned.1.call-start = ((), (), s32[]{:S(2)}) async-start(), calls=%async_computation.16 | async-start | bytes 27033600 | tf_op jit(solution)/shard_map/reduce_scatter | solution.py:414
  1026.0 107.1 %copy-start.32 = (bf16[256,10,128]{0,2,1:T(8,128)(2,1)S(1)}, bf16[256,10,128]{0,2,1:T(8,128)(2,1)}, u32[]{:S(2)}) copy-start(bf16[256,10,128]{0,2,1:T(8,128)(2,1)} %copy-done.31) | copy-start | bytes 1966084
  (61 other events, 201.2 us)
Sparse Core Ops, SparseCore 0:
  11.5 100.8 all-gather.7
  132.7 55.2 all-gather.11
  190.1 53.1 all-gather.9
  245.3 234.0 all-gather.15
  567.8 105.8 all-gather.13
  876.7 72.2 reduce-scatter.7
  951.3 51.7 reduce-scatter.9
  1009.3 119.1 all-reduce.7
  1130.8 161.1 reduce-scatter.13
  1294.3 228.5 reduce-scatter.15
  1525.2 279.6 reduce-scatter.11
where the time goes:
time: 1910 us; the launch traced here: 1890 us
  waiting for transfers between devices  1130 us (59%)
  matrix products  231 us (12%)
  local copies, waits for them, and re-layouts  209 us (11%)
  blocking collectives  177 us (9%)
  other arithmetic  106 us (6%)
  starting transfers between devices  21.9 us (1%)
  between operations  20.9 us (1%)
    reduce_scatter x1, waiting for transfers between devices, body(): lax.psum_scatter(attn_grad, ('dp', 'expert'), scatter_dimension=1, tiled=...  278 us
    reduce_scatter x1, waiting for transfers between devices, body(): lax.psum_scatter(expert_grad.astype(jnp.bfloat16), 'dp', scatter_dimensio...  229 us
    reduce_scatter x1, waiting for transfers between devices, body(): lax.psum_scatter(shared_grad, ('dp', 'expert'), scatter_dimension=1, tile...  104 us
    unnamed x12, waiting for transfers between devices  103 us
    all_gather x1, waiting for transfers between devices, body(): lax.all_gather(dispatched_projection_matrices.astype(jnp.bfloat16), 'dp',...  86.4 us
    all_to_all x1, waiting for transfers between devices, body(): lax.all_to_all(result, 'expert', split_axis=0, concat_axis=0, tiled=True)  78.9 us
    dot_general x24, matrix products, contract(): lax.dot_general(left, right, (((left_dim,), (right_dim,)), ((), ())), pre...  66.9 us
    all_to_all x1, waiting for transfers between devices, body(): lax.all_to_all(outgoing, 'expert', split_axis=0, concat_axis=0, tiled=True)  57.9 us
  transfers between devices with their start and end apart: 15, of which 11 were waited for; matrix products, arithmetic and copies ran while one was open for 19% of the time, Pallas kernels for 0%

commit v1 on v0

v1 whole, which is shorter than its diff:
```python
import jax
import jax.numpy as jnp
from jax import lax
from jax.sharding import PartitionSpec as P

HEAD_DIM = 128
STEP = 10


NORM_EPS = 1e-06
THETA = 10000.0
CLIP_VALUE = 1.0
BETA_ONE = 0.9
BETA_TWO = 0.999
ADAM_EPS = 1e-08
DECAY = 0.1
RATE_MATRIX = 0.02
RATE_EXPERT = 0.1
RATE_GAIN = 0.3
MASKED = -1e30

F32 = jnp.float32
BF16 = jnp.bfloat16


def contract(left, right, left_dim, right_dim):
    return lax.dot_general(
        left, right, (((left_dim,), (right_dim,)), ((), ())), preferred_element_type=F32
    )


def rotary_tables(places, head_dim):
    half = head_dim // 2
    freq = THETA ** (-2.0 * jnp.arange(half, dtype=F32) / head_dim)
    angle = places.astype(F32)[:, None] * freq
    cosine = jnp.concatenate([jnp.cos(angle), jnp.cos(angle)], -1)[:, None, :]
    sine = jnp.concatenate([jnp.sin(angle), jnp.sin(angle)], -1)[:, None, :]
    return (cosine, sine)


def turn(values, cosine, sine):
    half = values.shape[-1] // 2
    turned = jnp.concatenate([-values[..., half:], values[..., :half]], -1)
    return values * cosine + turned * sine


def norm_forward(values, gain):
    inverse = lax.rsqrt(jnp.mean(values * values, axis=-1, keepdims=True) + NORM_EPS)
    scaled = values * inverse
    return ((scaled * gain).astype(BF16), scaled, inverse)


def norm_backward(grad, scaled, inverse, gain):
    local = grad * gain
    return inverse * (local - scaled * jnp.mean(local * scaled, axis=-1, keepdims=True))


def adam(master, first, second, grad, scale, rate):
    clipped = grad * scale
    first_new = BETA_ONE * first + (1.0 - BETA_ONE) * clipped
    second_new = BETA_TWO * second + (1.0 - BETA_TWO) * clipped * clipped
    first_hat = first_new / (1.0 - BETA_ONE**STEP)
    second_hat = second_new / (1.0 - BETA_TWO**STEP)
    master_new = master - rate * (first_hat / (jnp.sqrt(second_hat) + ADAM_EPS) + DECAY * master)
    return (master_new, first_new, second_new)


def after(value, *others):
    return lax.optimization_barrier((value,) + others)[0]


def swap(value, mask):
    size = lax.axis_size("expert")
    return lax.ppermute(value, "expert", [(i, i ^ mask) for i in range(size)])


def rotate(value, step):
    size = lax.axis_size("dp")
    return lax.ppermute(value, "dp", [(i, (i + step) % size) for i in range(size)])


def shift(value, step):
    size = lax.axis_size("dp")
    return lax.ppermute(
        value, "dp", [(i, i + step) for i in range(size) if 0 <= i + step < size]
    )


def put(buffer, block, index, axis):
    return lax.dynamic_update_slice_in_dim(buffer, jnp.expand_dims(block, axis), index, axis)


def pick(buffer, index, axis):
    return lax.dynamic_index_in_dim(buffer, index, axis, keepdims=False)


def gather_rotations(block):
    size, here = lax.axis_size("dp"), lax.axis_index("dp")
    received = [block] + [rotate(block, step) for step in range(1, size)]
    out = jnp.zeros((size,) + block.shape, block.dtype)
    for step, piece in enumerate(received):
        out = put(out, piece, (here - step) % size, 0)
    return out


def gather_swaps(block):
    size = lax.axis_size("expert")
    received = {0: block}
    for mask in range(2, size, 2):
        received[mask] = swap(block, mask)
    for mask in range(0, size, 2):
        received[mask + 1] = swap(received[mask], 1)
    return [received[mask] for mask in range(size)]


def gather_dense(block):
    size, here = lax.axis_size("expert"), lax.axis_index("expert")
    stacked = gather_rotations(block)
    received = gather_swaps(stacked)
    out = jnp.zeros((stacked.shape[0], size) + block.shape, block.dtype)
    for mask, piece in enumerate(received):
        out = put(out, piece, here ^ mask, 1)
    return out


def scatter_swaps(blocks):
    size = lax.axis_size("expert")
    other = swap(jnp.stack([blocks[m].astype(BF16) for m in range(1, size, 2)]), 1)
    summed = [blocks[m].astype(F32) + other[m // 2].astype(F32) for m in range(0, size, 2)]
    total = summed[0]
    for index in range(1, size // 2):
        total = total + swap(summed[index].astype(BF16), 2 * index).astype(F32)
    return total


def scatter_dense(grad):
    size, here = lax.axis_size("expert"), lax.axis_index("expert")
    deep, level = lax.axis_size("dp"), lax.axis_index("dp")
    core, chip = here % 2, here // 2
    low = grad.astype(BF16).reshape((deep, size // 2, 2) + grad.shape[2:])
    other = swap(pick(low, 1 - core, 2), 1)
    summed = (pick(low, core, 2).astype(F32) + other.astype(F32)).astype(BF16)
    total = pick(summed, chip, 1).astype(F32)
    for mask in range(1, size // 2):
        total = total + swap(pick(summed, chip ^ mask, 1), 2 * mask).astype(F32)
    column = total.astype(BF16)
    result = pick(total, level, 0)
    for step in range(1, deep):
        result = result + rotate(pick(column, (level + step) % deep, 0), step).astype(F32)
    return result


def roles(size, here):
    low = here < size // 2
    return (here, here ^ 1, jnp.where(low, 2, 1), jnp.where(low, 3, 0))


def send(value, pairs):
    return lax.ppermute(value, "dp", pairs)


ENDS_IN = [(1, 0), (2, 3)]
ENDS_OUT = [(0, 1), (3, 2)]
PAIRS = [(0, 1), (1, 0), (2, 3), (3, 2)]
MIDDLE = [(1, 2), (2, 1)]
LEAP = [(0, 2), (3, 1)]
LEAP_BACK = [(2, 0), (1, 3)]


def line_first(block):
    return (send(block, PAIRS), send(block, MIDDLE), send(block, LEAP))


def line_second(first):
    pair, near, far = first
    return (pair, near + send(near, ENDS_IN), far + send(far, ENDS_IN))


def line_join(block, pieces, axis):
    size, here = lax.axis_size("dp"), lax.axis_index("dp")
    shape = block.shape[:axis] + (size,) + block.shape[axis:]
    out = jnp.zeros(shape, block.dtype)
    for piece, index in zip((block,) + pieces, roles(size, here)):
        out = put(out, piece, index, axis)
    return out


def line_scatter(blocks):
    own, pair, near, far = blocks
    here = lax.axis_index("dp")
    inner = (here == 1) | (here == 2)
    from_pair = send(pair, PAIRS)
    near_in, far_in = send(near, ENDS_OUT), send(far, ENDS_OUT)
    near_sum = (near.astype(F32) + near_in.astype(F32)).astype(BF16)
    far_sum = (far.astype(F32) + far_in.astype(F32)).astype(BF16)
    near_out, far_out = send(near_sum, MIDDLE), send(far_sum, LEAP_BACK)
    return (
        own.astype(F32) + from_pair.astype(F32) + near_out.astype(F32) + far_out.astype(F32)
    )


def rotation_scatter(stacked):
    size, here = lax.axis_size("dp"), lax.axis_index("dp")
    total = pick(stacked, here, 0).astype(F32)
    for step in range(1, size):
        total = total + rotate(pick(stacked, (here + step) % size, 0), step).astype(F32)
    return total


def visible(starts, rows, place):
    index = jnp.arange(starts.shape[0], dtype=jnp.int32)
    own_start = lax.dynamic_slice_in_dim(starts, place, rows)
    own_index = place + jnp.arange(rows, dtype=jnp.int32)
    return (own_start[:, None] == starts[None, :]) & (index[None, :] <= own_index[:, None])


def expert_forward(tokens, weights):
    gate_part = contract(tokens, weights[0], 1, 0)
    up_part = contract(tokens, weights[1], 1, 0)
    hidden = (jax.nn.silu(gate_part) * up_part).astype(BF16)
    result = contract(hidden, weights[2], 1, 1).astype(BF16)
    return gate_part, up_part, hidden, result


def expert_backward(tokens, weights, gate_part, up_part, grad_pair):
    grad_hidden = contract(grad_pair, weights[2], 1, 0)
    sigma = jax.nn.sigmoid(gate_part)
    grad_gate = (grad_hidden * up_part * sigma * (1.0 + gate_part * (1.0 - sigma))).astype(BF16)
    grad_up = (grad_hidden * gate_part * sigma).astype(BF16)
    entry = (contract(grad_gate, weights[0], 1, 1) + contract(grad_up, weights[1], 1, 1)).astype(
        BF16
    )
    return grad_gate, grad_up, entry


def body(
    block_input_vectors,
    output_sensitivity,
    rotary_offsets,
    dispatched_specialist_ids,
    specialist_quotas,
    storage_holder,
    mixer_projection_matrices,
    mixer_mean_estimate,
    mixer_variance_estimate,
    common_projection_matrices,
    common_mean_estimate,
    common_variance_estimate,
    gating_projection_matrix,
    gating_mean_estimate,
    gating_variance_estimate,
    scaling_factors,
    scaling_mean_estimate,
    scaling_variance_estimate,
    dispatched_projection_matrices,
    dispatched_mean_estimate,
    dispatched_variance_estimate,
):
    token_rows = block_input_vectors.shape[1]
    width = block_input_vectors.shape[2]
    head_dim = HEAD_DIM
    heads = width // head_dim
    length = rotary_offsets.shape[1]
    specialist_total = specialist_quotas.shape[0]
    expert_local = dispatched_projection_matrices.shape[0]
    hidden_width = dispatched_projection_matrices.shape[3]
    part_rows = dispatched_projection_matrices.shape[2]
    dense_rows = mixer_projection_matrices.shape[1]
    groups = lax.axis_size("expert")
    deep = lax.axis_size("dp")
    here = lax.axis_index("expert")
    level = lax.axis_index("dp")
    scale_attn = head_dim ** (-0.5)
    straight = deep == 4

    attn_own = mixer_projection_matrices.astype(BF16)
    shared_own = common_projection_matrices.astype(BF16)
    router_own = gating_projection_matrix.astype(BF16)
    gain_own = scaling_factors.astype(BF16)
    expert_own = dispatched_projection_matrices.astype(BF16)

    small = jnp.concatenate([router_own.reshape(-1), gain_own.reshape(-1)])
    small_rows = -(-small.shape[0] // width)
    first_rows = 3 * dense_rows + small_rows
    fill = -first_rows % 8
    small = jnp.pad(small, (0, (small_rows + fill) * width - small.shape[0]))
    first_block = jnp.concatenate(
        [attn_own[:3].reshape(3 * dense_rows, width), small.reshape(small_rows + fill, width)], 0
    )
    first_all = gather_dense(first_block)
    projections = (
        first_all[:, :, : 3 * dense_rows]
        .reshape(deep, groups, 3, dense_rows, width)
        .transpose(2, 0, 1, 3, 4)
        .reshape(3, width, width)
    )
    small_all = first_all[:, :, 3 * dense_rows :].reshape(deep, groups, -1)
    router_low = small_all[:, :, : dense_rows * specialist_total].reshape(width, specialist_total)
    gain_low = (
        small_all[:, :, dense_rows * specialist_total : dense_rows * (specialist_total + 2)]
        .reshape(deep, groups, 2, dense_rows)
        .transpose(2, 0, 1, 3)
        .reshape(2, width)
    )
    gain_one = gain_low[0].astype(F32)
    gain_two = gain_low[1].astype(F32)

    inputs_low = block_input_vectors[0]
    sequence = jnp.zeros((deep, token_rows, width), BF16)
    sequence = put(sequence, inputs_low, level, 0)
    for step in range(1, deep):
        sequence = put(sequence, shift(inputs_low, step), (level - step) % deep, 0)
    sequence = sequence.reshape(length, width).astype(F32)

    out_all = gather_dense(attn_own[3])
    out_low = out_all.reshape(width, width)
    shared_all = gather_dense(shared_own.reshape(3 * dense_rows, hidden_width))
    shared_low = (
        shared_all.reshape(deep, groups, 3, dense_rows, hidden_width)
        .transpose(2, 0, 1, 3, 4)
        .reshape(3, width, hidden_width)
    )

    expert_low = []
    for number in range(expert_local):
        if straight:
            pieces = line_second(line_first(expert_own[number]))
            whole = line_join(expert_own[number], pieces, 1)
        else:
            whole = gather_rotations(expert_own[number]).transpose(1, 0, 2, 3)
        expert_low.append(whole.reshape(3, width, hidden_width))

    grad_low = output_sensitivity[0]
    grad_out = grad_low.astype(F32)
    grads_plane = jnp.concatenate(gather_swaps(grad_low), 0)

    normed_all, scaled_all, _ = norm_forward(sequence, gain_one)
    inputs = inputs_low.astype(F32)
    normed, scaled_one, inverse_one = norm_forward(inputs, gain_one)
    place = level * token_rows
    cosine_all, sine_all = rotary_tables(rotary_offsets[0], head_dim)
    cosine = lax.dynamic_slice_in_dim(cosine_all, place, token_rows)
    sine = lax.dynamic_slice_in_dim(sine_all, place, token_rows)
    query = turn(
        contract(normed, projections[0], 1, 0).reshape(token_rows, heads, head_dim), cosine, sine
    ).astype(BF16)
    keys = turn(
        contract(normed_all, projections[1], 1, 0).reshape(length, heads, head_dim),
        cosine_all,
        sine_all,
    ).astype(BF16)
    values = contract(normed_all, projections[2], 1, 0).astype(BF16)
    values = values.reshape(length, heads, head_dim)
    starts = jnp.arange(length, dtype=jnp.int32) - rotary_offsets[0]
    allowed = visible(starts, token_rows, place)[None]
    scores = jnp.einsum("qhd,khd->hqk", query, keys, preferred_element_type=F32) * scale_attn
    weights = jax.nn.softmax(jnp.where(allowed, scores, MASKED), axis=-1)
    weights_low = weights.astype(BF16)
    mixed = jnp.einsum("hqk,khd->qhd", weights_low, values, preferred_element_type=F32)
    mixed_low = mixed.reshape(token_rows, width).astype(BF16)
    middle = inputs + contract(mixed_low, out_low, 1, 0)
    second, scaled_two, inverse_two = norm_forward(middle, gain_two)

    probs = jax.nn.softmax(contract(second, router_low, 1, 0), axis=-1)
    experts = jnp.arange(specialist_total, dtype=jnp.int32)
    named = jnp.any(dispatched_specialist_ids[0][:, :, None] == experts, axis=1)
    order = jnp.arange(token_rows)
    earlier = contract(
        (order[:, None] > order[None, :]).astype(BF16), named.astype(BF16), 1, 0
    )
    kept = named & (earlier < specialist_quotas.astype(F32)[None, :])
    gate = jnp.where(kept, probs, 0.0)
    to_storage = (storage_holder[:, None] == experts[None, :]).astype(F32)
    gate_stored = jnp.sum(gate[:, :, None] * to_storage[None], axis=1)
    gates_sent = gate_stored.reshape(token_rows, groups, expert_local).transpose(1, 0, 2)
    gates_received = lax.all_to_all(gates_sent, "expert", 0, 0, tiled=True)
    relative = here ^ jnp.arange(groups)
    gates_plane = gates_received[relative].reshape(groups * token_rows, expert_local)

    tokens = jnp.concatenate(gather_swaps(second), 0)

    plane_rows = groups * token_rows
    routed_part = jnp.zeros((plane_rows, width), F32)
    entry_part = jnp.zeros((plane_rows, width), F32)
    grads_plane_wide = grads_plane.astype(F32)
    gate_grads = []
    expert_sums = []
    for number in range(expert_local):
        gate_column = gates_plane[:, number : number + 1]
        gate_part, up_part, hidden, result = expert_forward(tokens, expert_low[number])
        result_wide = result.astype(F32)
        routed_part = routed_part + gate_column * result_wide
        gate_grads.append(jnp.sum(grads_plane_wide * result_wide, axis=-1))
        grad_pair = (gate_column * grads_plane_wide).astype(BF16)
        grad_gate, grad_up, entry = expert_backward(
            tokens, expert_low[number], gate_part, up_part, grad_pair
        )
        entry_part = entry_part + entry.astype(F32)
        expert_grad = jnp.stack(
            [
                contract(tokens, grad_gate, 0, 0).astype(BF16),
                contract(tokens, grad_up, 0, 0).astype(BF16),
                contract(grad_pair, hidden, 0, 0).astype(BF16),
            ]
        ).reshape(3, deep, part_rows, hidden_width)
        if straight:
            expert_sums.append(
                line_scatter([pick(expert_grad, index, 1) for index in roles(deep, level)])
            )
        else:
            expert_sums.append(rotation_scatter(expert_grad.transpose(1, 0, 2, 3)))
    expert_sum = jnp.stack(expert_sums)

    entry_blocks = entry_part.reshape(groups, token_rows, width)
    grad_second = scatter_swaps([entry_blocks[m] for m in range(groups)])
    routed_blocks = routed_part.reshape(groups, token_rows, width)
    routed = scatter_swaps([routed_blocks[m] for m in range(groups)])
    gate_grad_sent = jnp.stack(gate_grads, -1).reshape(groups, token_rows, expert_local)[relative]
    gate_grad_back = lax.all_to_all(gate_grad_sent, "expert", 0, 0, tiled=True)
    gate_grad_stored = gate_grad_back.transpose(1, 0, 2).reshape(token_rows, specialist_total)
    grad_prob = jnp.sum(gate_grad_stored[:, None, :] * to_storage[None], axis=-1)
    grad_prob = jnp.where(kept, grad_prob, 0.0)

    gate_shared = contract(second, shared_low[0], 1, 0)
    up_shared = contract(second, shared_low[1], 1, 0)
    hidden_shared = (jax.nn.silu(gate_shared) * up_shared).astype(BF16)
    shared_out = contract(hidden_shared, shared_low[2], 1, 1)
    grad_gate_shared, grad_up_shared, _ = expert_backward(
        second, shared_low, gate_shared, up_shared, grad_low
    )
    shared_entry = contract(grad_gate_shared, shared_low[0], 1, 1) + contract(
        grad_up_shared, shared_low[1], 1, 1
    )
    block_out = (middle + shared_out + routed).astype(BF16)

    grad_logit = (probs * (grad_prob - jnp.sum(probs * grad_prob, axis=-1, keepdims=True))).astype(
        BF16
    )
    router_grad = contract(second, grad_logit, 0, 0)
    grad_second = grad_second + contract(grad_logit, router_low, 1, 1) + shared_entry
    shared_grad = jnp.stack(
        [
            contract(second, grad_gate_shared, 0, 0),
            contract(second, grad_up_shared, 0, 0),
            contract(grad_low, hidden_shared, 0, 0),
        ]
    )
    gain_two_grad = jnp.sum(grad_second * scaled_two, axis=0)
    grad_middle = norm_backward(grad_second, scaled_two, inverse_two, gain_two) + grad_out
    grad_attn_out = grad_middle.astype(BF16)
    out_grad = contract(mixed_low, grad_attn_out, 0, 0)
    grad_mixed = contract(grad_attn_out, out_low, 1, 1).astype(BF16)
    grad_mixed = grad_mixed.reshape(token_rows, heads, head_dim)
    correction = jnp.sum(grad_mixed.astype(F32) * mixed, axis=-1).T
    grad_weights = jnp.einsum("qhd,khd->hqk", grad_mixed, values, preferred_element_type=F32)
    grad_scores = jnp.where(
        allowed, weights * (grad_weights - correction[..., None]), 0.0
    ).astype(BF16)
    grad_query = (
        jnp.einsum("hqk,khd->qhd", grad_scores, keys, preferred_element_type=F32) * scale_attn
    )
    grad_keys = (
        jnp.einsum("hqk,qhd->khd", grad_scores, query, preferred_element_type=F32) * scale_attn
    )
    grad_values = jnp.einsum("hqk,qhd->khd", weights_low, grad_mixed, preferred_element_type=F32)
    grad_query_low = turn(grad_query, cosine, -sine).reshape(token_rows, width).astype(BF16)
    grad_key_low = turn(grad_keys, cosine_all, -sine_all).reshape(length, width).astype(BF16)
    grad_value_low = grad_values.reshape(length, width).astype(BF16)
    projection_grad = jnp.stack(
        [
            contract(normed, grad_query_low, 0, 0),
            contract(normed_all, grad_key_low, 0, 0),
            contract(normed_all, grad_value_low, 0, 0),
        ]
    )
    grad_normed_all = contract(grad_key_low, projections[1], 1, 1) + contract(
        grad_value_low, projections[2], 1, 1
    )
    grad_normed_own = contract(grad_query_low, projections[0], 1, 1)
    gain_one_grad = jnp.sum(grad_normed_all * scaled_all, axis=0) + jnp.sum(
        grad_normed_own * scaled_one, axis=0
    )
    normed_low = grad_normed_all.astype(BF16).reshape(deep, token_rows, width)
    grad_normed = grad_normed_own + pick(
        grad_normed_all.reshape(deep, token_rows, width), level, 0
    )
    for step in range(1, deep):
        grad_normed = grad_normed + shift(pick(normed_low, (level - step) % deep, 0), -step).astype(
            F32
        )
    grad_inputs = norm_backward(grad_normed, scaled_one, inverse_one, gain_one) + grad_middle

    def by_owner(grad):
        return grad.reshape(grad.shape[0], deep, groups, dense_rows, grad.shape[-1]).transpose(
            1, 2, 0, 3, 4
        )

    small_grad = jnp.concatenate(
        [
            router_grad.reshape(deep, groups, dense_rows * specialist_total),
            jnp.stack([gain_one_grad, gain_two_grad])
            .reshape(2, deep, groups, dense_rows)
            .transpose(1, 2, 0, 3)
            .reshape(deep, groups, 2 * dense_rows),
        ],
        -1,
    )
    small_grad = jnp.pad(
        small_grad, ((0, 0), (0, 0), (0, (small_rows + fill) * width - small_grad.shape[-1]))
    ).reshape(deep, groups, small_rows + fill, width)
    projection_sums = scatter_dense(
        jnp.concatenate(
            [
                by_owner(projection_grad).reshape(deep, groups, 3 * dense_rows, width),
                small_grad,
            ],
            2,
        )
    )
    out_sum = scatter_dense(out_grad.reshape(deep, groups, dense_rows, width))
    shared_sum = scatter_dense(
        by_owner(shared_grad).reshape(deep, groups, 3 * dense_rows, hidden_width)
    ).reshape(3, dense_rows, hidden_width)
    attn_sum = jnp.concatenate(
        [projection_sums[: 3 * dense_rows].reshape(3, dense_rows, width), out_sum[None]], 0
    )
    small_sum = projection_sums[3 * dense_rows :].reshape(-1)
    router_sum = small_sum[: dense_rows * specialist_total].reshape(dense_rows, specialist_total)
    gain_sum = small_sum[
        dense_rows * specialist_total : dense_rows * (specialist_total + 2)
    ].reshape(2, dense_rows)

    local_squares = (
        jnp.sum(attn_sum * attn_sum)
        + jnp.sum(shared_sum * shared_sum)
        + jnp.sum(router_sum * router_sum)
        + jnp.sum(gain_sum * gain_sum)
        + jnp.sum(expert_sum * expert_sum)
    )
    everyone = deep * groups
    spread = jnp.broadcast_to(local_squares, (everyone, 8, 128))
    squares = lax.all_to_all(spread, ("dp", "expert"), 0, 0, tiled=True)
    grad_norm = jnp.sqrt(jnp.sum(squares[:, 0, 0]))
    scale = jnp.minimum(1.0, CLIP_VALUE / (grad_norm + 1e-06))
    attn_new, attn_moment, attn_square = adam(
        mixer_projection_matrices,
        mixer_mean_estimate,
        mixer_variance_estimate,
        attn_sum,
        scale,
        RATE_MATRIX,
    )
    shared_new, shared_moment, shared_square = adam(
        common_projection_matrices,
        common_mean_estimate,
        common_variance_estimate,
        shared_sum,
        scale,
        RATE_MATRIX,
    )
    router_new, router_moment, router_square = adam(
        gating_projection_matrix,
        gating_mean_estimate,
        gating_variance_estimate,
        router_sum,
        scale,
        RATE_MATRIX,
    )
    gain_new, gain_moment, gain_square = adam(
        scaling_factors,
        scaling_mean_estimate,
        scaling_variance_estimate,
        gain_sum,
        scale,
        RATE_GAIN,
    )
    expert_new, expert_moment, expert_square = adam(
        dispatched_projection_matrices,
        dispatched_mean_estimate,
        dispatched_variance_estimate,
        expert_sum,
        scale,
        RATE_EXPERT,
    )
    return (
        block_out[None],
        grad_inputs[None],
        grad_norm,
        attn_new,
        attn_moment,
        attn_square,
        attn_new.astype(BF16),
        shared_new,
        shared_moment,
        shared_square,
        shared_new.astype(BF16),
        router_new,
        router_moment,
        router_square,
        router_new.astype(BF16),
        gain_new,
        gain_moment,
        gain_square,
        expert_new,
        expert_moment,
        expert_square,
        expert_new.astype(BF16),
    )


def solution(mesh):
    placed = (
        P("expert", "dp", None),
        P("expert", "dp", None),
        P("expert", None),
        P("expert", "dp", None),
        P(),
        P(),
        P(None, ("dp", "expert"), None),
        P(None, ("dp", "expert"), None),
        P(None, ("dp", "expert"), None),
        P(None, ("dp", "expert"), None),
        P(None, ("dp", "expert"), None),
        P(None, ("dp", "expert"), None),
        P(("dp", "expert"), None),
        P(("dp", "expert"), None),
        P(("dp", "expert"), None),
        P(None, ("dp", "expert")),
        P(None, ("dp", "expert")),
        P(None, ("dp", "expert")),
        P("expert", None, "dp", None),
        P("expert", None, "dp", None),
        P("expert", None, "dp", None),
    )
    return jax.shard_map(
        body,
        mesh=mesh,
        in_specs=placed,
        out_specs=(
            P("expert", "dp", None),
            P("expert", "dp", None),
            P(),
            P(None, ("dp", "expert"), None),
            P(None, ("dp", "expert"), None),
            P(None, ("dp", "expert"), None),
            P(None, ("dp", "expert"), None),
            P(None, ("dp", "expert"), None),
            P(None, ("dp", "expert"), None),
            P(None, ("dp", "expert"), None),
            P(None, ("dp", "expert"), None),
            P(("dp", "expert"), None),
            P(("dp", "expert"), None),
            P(("dp", "expert"), None),
            P(("dp", "expert"), None),
            P(None, ("dp", "expert")),
            P(None, ("dp", "expert")),
            P(None, ("dp", "expert")),
            P("expert", None, "dp", None),
            P("expert", None, "dp", None),
            P("expert", None, "dp", None),
            P("expert", None, "dp", None),
        ),
        check_vma=False,
    )
```

time: 1910 us -> 1360 us (0.71)
  waiting for transfers between devices: 1130 us -> 592 us
  blocking collectives: 177 us -> 0 us
  starting transfers between devices: 21.9 us -> 148 us
  other arithmetic: 106 us -> 157 us
  matrix products: 231 us -> 259 us
  local copies, waits for them, and re-layouts: 209 us -> 181 us
    reduce_scatter x5 -> x0, waiting for transfers between devices: 645 us -> none  [the longest x1 278 us: body(): lax.psum_scatter(attn_grad, ('dp', 'expert'), scatter_dimension=1, tiled=...]
    ppermute x0 -> x99, waiting for transfers between devices: none -> 585 us  [the longest x20 309 us: send(): return lax.ppermute(value, 'dp', pairs)]
    all_gather x5 -> x0, waiting for transfers between devices: 190 us -> none  [the longest x1 86.4 us: body(): lax.all_gather(dispatched_projection_matrices.astype(jnp.bfloat16), 'dp',...]
    all_to_all x4 -> x3, waiting for transfers between devices: 189 us -> 6.96 us  [the longest x1 4.94 us: body(): squares = lax.all_to_all(spread, ('dp', 'expert'), 0, 0, tiled=True)]
    dot_general x24 -> x43, matrix products: 66.9 us -> 234 us  [contract(): lax.dot_general(left, right, (((left_dim,), (right_dim,)), ((), ())), pre...]
    dot_general x16 -> x5, matrix products: 164 us -> 17.3 us  [the longest x1 6.14 us: body(): jnp.einsum('qhd,khd->hqk', grad_mixed, values, preferred_element_type=F32)]
    ppermute x0 -> x99, starting transfers between devices: none -> 128 us  [the longest x20 46 us: send(): return lax.ppermute(value, 'dp', pairs)]
    unnamed x12 -> x0, waiting for transfers between devices: 103 us -> none
  transfers between devices with their start and end apart: 15 -> 102, of which waited for: 11 -> 35; matrix products, arithmetic and copies ran while one was open for 19% -> 40% of each run, Pallas kernels for 0% -> 0%
where the time goes in v1:
time: 1360 us; the launch traced here: 1350 us
  waiting for transfers between devices  592 us (44%)
  matrix products  259 us (19%)
  local copies, waits for them, and re-layouts  181 us (13%)
  other arithmetic  157 us (12%)
  starting transfers between devices  148 us (11%)
    ppermute x20, waiting for transfers between devices, send(): return lax.ppermute(value, 'dp', pairs)  309 us
    dot_general x43, matrix products, contract(): lax.dot_general(left, right, (((left_dim,), (right_dim,)), ((), ())), pre...  234 us
    ppermute x55, waiting for transfers between devices, swap(): return lax.ppermute(value, 'expert', [(i, i ^ mask) for i in range(size)])  195 us
    ppermute x18, waiting for transfers between devices, rotate(): lax.ppermute(value, 'dp', [(i, (i + step) % size) for i in range(size)])  53 us
    ppermute x20, starting transfers between devices, send(): return lax.ppermute(value, 'dp', pairs)  46 us
    ppermute x55, starting transfers between devices, swap(): return lax.ppermute(value, 'expert', [(i, i ^ mask) for i in range(size)])  44.1 us
    unnamed x352, local copies, waits for them, and re-layouts  42.5 us
    dynamic_update_slice x42, local copies, waits for them, and re-layouts, put(): lax.dynamic_update_slice_in_dim(buffer, jnp.expand_dims(block, axis), ind...  34.6 us
  transfers between devices with their start and end apart: 102, of which 35 were waited for; matrix products, arithmetic and copies ran while one was open for 40% of the time, Pallas kernels for 0%

profile of v1, /device:TPU:0, one launch (start us, length us, event | category | flops | bytes accessed | tf_op | source)
XLA Modules:
  0.0 1345.5 jit_solution(6276781555680643040)
XLA Ops:
  56.1 7.5 collective-permute-done.24
  94.4 10.5 collective-permute-done.17
  117.6 36.2 %collective-permute-done.19 = bf16[4,40,1280]{2,1,0:T(8,128)(2,1)S(1)} collective-permute-done((bf16[4,40,1280]{2,1,0:T(8,128)(2,1)}, bf16[4,40,1280]{2,1,0:T(8,128)(2,1)S(1)}, u32[]{:S(2)}, u32[]{:S(2)}) %collective-permute-start.19) | collective-permute-done | bytes 409632 | tf_op jit(solution)/shard_map/ppermute | solution.py:74
  158.6 8.7 collective-permute-start.45
  167.9 7.8 collective-permute-done.27
  188.7 19.0 %collective-permute-done.7 = bf16[4,128,1280]{2,1,0:T(8,128)(2,1)S(1)} collective-permute-done((bf16[4,128,1280]{2,1,0:T(8,128)(2,1)}, bf16[4,128,1280]{2,1,0:T(8,128)(2,1)S(1)}, u32[]{:S(2)}, u32[]{:S(2)}) %collective-permute-start.7) | collective-permute-done | bytes 1310752 | tf_op jit(solution)/shard_map/ppermute | solution.py:74
  212.0 14.8 %collective-permute-done.31 = bf16[4,120,896]{2,1,0:T(8,128)(2,1)S(1)} collective-permute-done((bf16[4,120,896]{2,1,0:T(8,128)(2,1)}, bf16[4,120,896]{2,1,0:T(8,128)(2,1)S(1)}, u32[]{:S(2)}, u32[]{:S(2)}) %collective-permute-start.31) | collective-permute-done | bytes 860192 | tf_op jit(solution)/shard_map/ppermute | solution.py:74
  228.0 15.9 %collective-permute-done.40 = bf16[3,320,896]{2,1,0:T(8,128)(2,1)S(1)} collective-permute-done((bf16[3,320,896]{2,1,0:T(8,128)(2,1)S(1)}, bf16[3,320,896]{2,1,0:T(8,128)(2,1)S(1)}, u32[]{:S(2)}, u32[]{:S(2)}) %collective-permute-start.40) | collective-permute-done | bytes 1720352 | tf_op jit(solution)/shard_map/ppermute | solution.py:159
  248.2 34.7 %collective-permute-done.9 = bf16[4,128,1280]{2,1,0:T(8,128)(2,1)S(1)} collective-permute-done((bf16[4,128,1280]{2,1,0:T(8,128)(2,1)}, bf16[4,128,1280]{2,1,0:T(8,128)(2,1)S(1)}, u32[]{:S(2)}, u32[]{:S(2)}) %collective-permute-start.9) | collective-permute-done | bytes 1310752 | tf_op jit(solution)/shard_map/ppermute | solution.py:74
  284.8 8.0 collective-permute-start.43
  302.6 26.9 %collective-permute-done.43 = bf16[3,320,896]{2,1,0:T(8,128)(2,1)} collective-permute-done((bf16[3,320,896]{2,1,0:T(8,128)(2,1)S(1)}, bf16[3,320,896]{2,1,0:T(8,128)(2,1)}, u32[]{:S(2)}, u32[]{:S(2)}) %collective-permute-start.43) | collective-permute-done | bytes 1720352 | tf_op jit(solution)/shard_map/ppermute | solution.py:159
  330.8 34.6 %collective-permute-done.48 = bf16[3,320,896]{2,1,0:T(8,128)(2,1)} collective-permute-done((bf16[3,320,896]{2,1,0:T(8,128)(2,1)S(1)}, bf16[3,320,896]{2,1,0:T(8,128)(2,1)}, u32[]{:S(2)}, u32[]{:S(2)}) %collective-permute-start.48) | collective-permute-done | bytes 1720352 | tf_op jit(solution)/shard_map/ppermute | solution.py:159
  371.4 8.1 slice.312
  429.9 7.5 fusion.148
  495.5 19.9 %collective-permute-done.44 = bf16[3,320,896]{2,1,0:T(8,128)(2,1)} collective-permute-done((bf16[3,320,896]{2,1,0:T(8,128)(2,1)}, bf16[3,320,896]{2,1,0:T(8,128)(2,1)}, u32[]{:S(2)}, u32[]{:S(2)}) %collective-permute-start.44) | collective-permute-done | bytes 1720352 | tf_op jit(solution)/shard_map/ppermute | solution.py:159
  516.8 34.1 %collective-permute-done.49 = bf16[3,320,896]{2,1,0:T(8,128)(2,1)} collective-permute-done((bf16[3,320,896]{2,1,0:T(8,128)(2,1)}, bf16[3,320,896]{2,1,0:T(8,128)(2,1)}, u32[]{:S(2)}, u32[]{:S(2)}) %collective-permute-start.49) | collective-permute-done | bytes 1720352 | tf_op jit(solution)/shard_map/ppermute | solution.py:159
  574.5 10.6 fusion.155
  585.2 7.6 fusion.156
  592.8 10.0 multiply_convert_fusion.5
  602.8 11.3 multiply_convert_fusion.4
  620.0 12.1 fusion.4
  652.8 9.0 convolution_convert_fusion.10
  661.9 13.4 multiply_convert_fusion.2
  675.3 8.1 convolution_convert_fusion.12
  683.5 8.1 fusion.157
  691.6 12.8 multiply_convert_fusion
  704.4 9.1 convolution_convert_fusion.9
  713.5 8.1 fusion.158
  745.8 10.0 add_convert_fusion
  755.8 14.3 %fusion.151 = (bf16[2048,1280]{1,0:T(8,128)(2,1)}, f32[2048,1280]{1,0:T(8,128)}) fusion(bf16[2048,1280]{1,0:T(8,128)(2,1)} %add_convert_fusion, f32[2048,1280]{1,0:T(8,128)} %fusion.157, bf16[2048,896]{1,0:T(8,128)(2,1)} %get-tuple-element.153, bf16[1280,896]{1,0:T(8,128)(2,1)S(1)} %bitcast.672), kind=kOutput, calls=%fused_computation.423 | convolution fusion | flops 4713349120 | bytes 37421056 | tf_op jit(solution)/shard_map/dot_general | solution.py:27
  807.8 13.9 %collective-permute-done.63 = bf16[256,1280]{1,0:T(8,128)(2,1)S(1)} collective-permute-done((bf16[256,1280]{1,0:T(8,128)(2,1)S(1)}, bf16[256,1280]{1,0:T(8,128)(2,1)S(1)}, u32[]{:S(2)}, u32[]{:S(2)}) %collective-permute-start.63) | collective-permute-done | bytes 655392 | tf_op jit(solution)/shard_map/ppermute | solution.py:74
  853.2 7.9 fusion.161
  861.1 8.0 fusion.19
  889.6 8.2 copy.352
  899.3 29.3 %collective-permute-done.66 = bf16[256,1280]{1,0:T(8,128)(2,1)} collective-permute-done((bf16[256,1280]{1,0:T(8,128)(2,1)}, bf16[256,1280]{1,0:T(8,128)(2,1)}, u32[]{:S(2)}, u32[]{:S(2)}) %collective-permute-start.66) | collective-permute-done | bytes 655392 | tf_op jit(solution)/shard_map/ppermute | solution.py:84
  940.4 26.4 %collective-permute-done.84 = bf16[4,120,896]{2,1,0:T(8,128)(2,1)} collective-permute-done((bf16[4,120,896]{2,1,0:T(8,128)(2,1)}, bf16[4,120,896]{2,1,0:T(8,128)(2,1)}, u32[]{:S(2)}, u32[]{:S(2)}) %collective-permute-start.84) | collective-permute-done | bytes 860192 | tf_op jit(solution)/shard_map/ppermute | solution.py:74
  982.3 31.7 %collective-permute-done.95 = bf16[3,320,896]{2,1,0:T(8,128)(2,1)S(1)} collective-permute-done((bf16[3,320,896]{2,1,0:T(8,128)(2,1)}, bf16[3,320,896]{2,1,0:T(8,128)(2,1)S(1)}, u32[]{:S(2)}, u32[]{:S(2)}) %collective-permute-start.95) | collective-permute-done | bytes 1720352 | tf_op jit(solution)/shard_map/ppermute | solution.py:159
  1014.6 35.7 %collective-permute-done.97 = bf16[3,320,896]{2,1,0:T(8,128)(2,1)S(1)} collective-permute-done((bf16[3,320,896]{2,1,0:T(8,128)(2,1)}, bf16[3,320,896]{2,1,0:T(8,128)(2,1)S(1)}, u32[]{:S(2)}, u32[]{:S(2)}) %collective-permute-start.97) | collective-permute-done | bytes 1720352 | tf_op jit(solution)/shard_map/ppermute | solution.py:159
  1054.8 10.1 collective-permute-done.87
  1083.2 59.3 %collective-permute-done.89 = bf16[3,320,896]{2,1,0:T(8,128)(2,1)S(1)} collective-permute-done((bf16[3,320,896]{2,1,0:T(8,128)(2,1)S(1)}, bf16[3,320,896]{2,1,0:T(8,128)(2,1)S(1)}, u32[]{:S(2)}, u32[]{:S(2)}) %collective-permute-start.89) | collective-permute-done | bytes 1720352 | tf_op jit(solution)/shard_map/ppermute | solution.py:159
  1145.7 8.1 collective-permute-done.93
  1175.0 12.2 collective-permute-done.94
  1189.5 30.3 %collective-permute-done.98 = bf16[3,320,896]{2,1,0:T(8,128)(2,1)} collective-permute-done((bf16[3,320,896]{2,1,0:T(8,128)(2,1)}, bf16[3,320,896]{2,1,0:T(8,128)(2,1)}, u32[]{:S(2)}, u32[]{:S(2)}) %collective-permute-start.98) | collective-permute-done | bytes 1720352 | tf_op jit(solution)/shard_map/ppermute | solution.py:159
  1228.9 22.0 %collective-permute-done.77 = bf16[4,40,1280]{2,1,0:T(8,128)(2,1)S(1)} collective-permute-done((bf16[4,40,1280]{2,1,0:T(8,128)(2,1)S(1)}, bf16[4,40,1280]{2,1,0:T(8,128)(2,1)S(1)}, u32[]{:S(2)}, u32[]{:S(2)}) %collective-permute-start.77) | collective-permute-done | bytes 409632 | tf_op jit(solution)/shard_map/ppermute | solution.py:74
  1263.3 10.2 collective-permute-done.80
  1274.3 11.1 collective-permute-done.73
  1296.6 10.8 all-to-all-start.2
  1318.0 19.5 %fusion.121 = (bf16[2,3,320,896]{3,2,1,0:T(8,128)(2,1)}, f32[2,3,320,896]{3,2,1,0:T(8,128)}, f32[2,3,320,896]{3,2,1,0:T(8,128)}, f32[2,3,320,896]{3,2,1,0:T(8,128)}) fusion(f32[2,3,320,896]{3,2,1,0:T(8,128)} %param.39, f32[]{:T(128)S(6)} %min.3, f32[1,3,320,896]{3,2,1,0:T(8,128)} %copy-done.1, f32[1,3,320,896]{3,2,1,0:T(8,128)S(1)} %fusion.32, ...), kind=kLoop, calls=%fused_computation.406 | loop fusion | flops 30965760 | bytes 51609604 | tf_op jit(solution)/shard_map/convert_element_type | solution.py:607
  (775 shorter events, 543.3 us)
Async XLA Ops:
  4.4 72.0 %collective-permute-start.3 = (bf16[128,1280]{1,0:T(8,128)(2,1)}, bf16[128,1280]{1,0:T(8,128)(2,1)}, u32[]{:S(2)}, u32[]{:S(2)}) collective-permute-start(bf16[128,1280]{1,0:T(8,128)(2,1)} %pad_maximum_fusion.8), channel_id=1, source_target_pairs={{0,8},{8,16},{16,24},{24,0},{1,9},{9,17},{17,25},{25,1},{2,10},{10... | collective-permute-start | bytes 983048 | tf_op jit(solution)/shard_map/ppermute | solution.py:79
  7.5 72.8 %collective-permute-start.4 = (bf16[128,1280]{1,0:T(8,128)(2,1)}, bf16[128,1280]{1,0:T(8,128)(2,1)}, u32[]{:S(2)}, u32[]{:S(2)}) collective-permute-start(bf16[128,1280]{1,0:T(8,128)(2,1)} %pad_maximum_fusion.8), channel_id=1, source_target_pairs={{0,16},{8,24},{16,0},{24,8},{1,17},{9,25},{17,1},{25,9},{2,18},{10... | collective-permute-start | bytes 983048 | tf_op jit(solution)/shard_map/ppermute | solution.py:79
  10.1 73.4 %collective-permute-start.5 = (bf16[128,1280]{1,0:T(8,128)(2,1)}, bf16[128,1280]{1,0:T(8,128)(2,1)}, u32[]{:S(2)}, u32[]{:S(2)}) collective-permute-start(bf16[128,1280]{1,0:T(8,128)(2,1)} %pad_maximum_fusion.8), channel_id=1, source_target_pairs={{0,24},{8,0},{16,8},{24,16},{1,25},{9,1},{17,9},{25,17},{2,26},{10... | collective-permute-start | bytes 983048 | tf_op jit(solution)/shard_map/ppermute | solution.py:79
  105.0 62.5 %collective-permute-start.57 = (bf16[256,1280]{1,0:T(8,128)(2,1)S(1)}, bf16[256,1280]{1,0:T(8,128)(2,1)S(1)}, u32[]{:S(2)}, u32[]{:S(2)}) collective-permute-start(bf16[256,1280]{1,0:T(8,128)(2,1)S(1)} %bitcast.641), channel_id=1, source_target_pairs={{0,4},{1,5},{2,6},{3,7},{4,0},{5,1},{6,2},{7,3},{8,12},{9,13},{10,... | collective-permute-start | bytes 1966088 | tf_op jit(solution)/shard_map/ppermute | solution.py:74
  107.7 68.1 %collective-permute-start.59 = (bf16[256,1280]{1,0:T(8,128)(2,1)S(1)}, bf16[256,1280]{1,0:T(8,128)(2,1)S(1)}, u32[]{:S(2)}, u32[]{:S(2)}) collective-permute-start(bf16[256,1280]{1,0:T(8,128)(2,1)S(1)} %bitcast.642), channel_id=1, source_target_pairs={{0,6},{1,7},{2,4},{3,5},{4,2},{5,3},{6,0},{7,1},{8,14},{9,15},{10,... | collective-permute-start | bytes 1966088 | tf_op jit(solution)/shard_map/ppermute | solution.py:74
  110.1 43.7 %collective-permute-start.19 = (bf16[4,40,1280]{2,1,0:T(8,128)(2,1)}, bf16[4,40,1280]{2,1,0:T(8,128)(2,1)S(1)}, u32[]{:S(2)}, u32[]{:S(2)}) collective-permute-start(bf16[4,40,1280]{2,1,0:T(8,128)(2,1)} %bitcast_dynamic-update-slice_fusion.43), channel_id=1, source_target_pairs={{0,4},{1,5},{2,6},{3,7},{4,0},{5,1},{6,2},{7,3},{8,12},{9,13},{10,... | collective-permute-start | bytes 1228808 | tf_op jit(solution)/shard_map/ppermute | solution.py:74
  158.6 51.8 %collective-permute-start.45 = (bf16[3,320,896]{2,1,0:T(8,128)(2,1)S(1)}, bf16[3,320,896]{2,1,0:T(8,128)(2,1)S(1)}, u32[]{:S(2)}, u32[]{:S(2)}) collective-permute-start(bf16[3,320,896]{2,1,0:T(8,128)(2,1)S(1)} %copy-done.92), channel_id=1, source_target_pairs={{0,8},{8,0},{16,24},{24,16},{1,9},{9,1},{17,25},{25,17},{2,10},{10... | collective-permute-start | bytes 5160968 | tf_op jit(solution)/shard_map/ppermute | solution.py:159
  179.2 64.7 %collective-permute-start.40 = (bf16[3,320,896]{2,1,0:T(8,128)(2,1)S(1)}, bf16[3,320,896]{2,1,0:T(8,128)(2,1)S(1)}, u32[]{:S(2)}, u32[]{:S(2)}) collective-permute-start(bf16[3,320,896]{2,1,0:T(8,128)(2,1)S(1)} %copy-done.93), channel_id=1, source_target_pairs={{0,8},{8,0},{16,24},{24,16},{1,9},{9,1},{17,25},{25,17},{2,10},{10... | collective-permute-start | bytes 5160968 | tf_op jit(solution)/shard_map/ppermute | solution.py:159
  208.9 74.0 %collective-permute-start.9 = (bf16[4,128,1280]{2,1,0:T(8,128)(2,1)}, bf16[4,128,1280]{2,1,0:T(8,128)(2,1)S(1)}, u32[]{:S(2)}, u32[]{:S(2)}) collective-permute-start(bf16[4,128,1280]{2,1,0:T(8,128)(2,1)} %bitcast_dynamic-update-slice_fusion.35), channel_id=1, source_target_pairs={{0,4},{1,5},{2,6},{3,7},{4,0},{5,1},{6,2},{7,3},{8,12},{9,13},{10,... | collective-permute-start | bytes 3932168 | tf_op jit(solution)/shard_map/ppermute | solution.py:74
  226.8 58.0 %collective-permute-start.11 = (bf16[4,128,1280]{2,1,0:T(8,128)(2,1)}, bf16[4,128,1280]{2,1,0:T(8,128)(2,1)S(1)}, u32[]{:S(2)}, u32[]{:S(2)}) collective-permute-start(bf16[4,128,1280]{2,1,0:T(8,128)(2,1)} %bitcast_dynamic-update-slice_fusion.35), channel_id=1, source_target_pairs={{0,6},{1,7},{2,4},{3,5},{4,2},{5,3},{6,0},{7,1},{8,14},{9,15},{10,... | collective-permute-start | bytes 3932168 | tf_op jit(solution)/shard_map/ppermute | solution.py:74
  243.9 48.9 %collective-permute-start.32 = (bf16[4,120,896]{2,1,0:T(8,128)(2,1)S(1)}, bf16[4,120,896]{2,1,0:T(8,128)(2,1)S(1)}, u32[]{:S(2)}, u32[]{:S(2)}) collective-permute-start(bf16[4,120,896]{2,1,0:T(8,128)(2,1)S(1)} %collective-permute-done.31), channel_id=1, source_target_pairs={{0,1},{1,0},{2,3},{3,2},{4,5},{5,4},{6,7},{7,6},{8,9},{9,8},{10,11... | collective-permute-start | bytes 2580488 | tf_op jit(solution)/shard_map/ppermute | solution.py:74
  245.3 50.1 %collective-permute-start.8 = (bf16[4,128,1280]{2,1,0:T(8,128)(2,1)S(1)}, bf16[4,128,1280]{2,1,0:T(8,128)(2,1)S(1)}, u32[]{:S(2)}, u32[]{:S(2)}) collective-permute-start(bf16[4,128,1280]{2,1,0:T(8,128)(2,1)S(1)} %collective-permute-done.7), channel_id=1, source_target_pairs={{0,1},{1,0},{2,3},{3,2},{4,5},{5,4},{6,7},{7,6},{8,9},{9,8},{10,11... | collective-permute-start | bytes 3932168 | tf_op jit(solution)/shard_map/ppermute | solution.py:74
  246.0 53.8 %collective-permute-start.46 = (bf16[3,320,896]{2,1,0:T(8,128)(2,1)S(1)}, bf16[3,320,896]{2,1,0:T(8,128)(2,1)}, u32[]{:S(2)}, u32[]{:S(2)}) collective-permute-start(bf16[3,320,896]{2,1,0:T(8,128)(2,1)S(1)} %copy-done.92), channel_id=1, source_target_pairs={{8,16},{16,8},{9,17},{17,9},{10,18},{18,10},{11,19},{19,11},{12,20... | collective-permute-start | bytes 5160968 | tf_op jit(solution)/shard_map/ppermute | solution.py:159
  284.8 44.7 %collective-permute-start.43 = (bf16[3,320,896]{2,1,0:T(8,128)(2,1)S(1)}, bf16[3,320,896]{2,1,0:T(8,128)(2,1)}, u32[]{:S(2)}, u32[]{:S(2)}) collective-permute-start(bf16[3,320,896]{2,1,0:T(8,128)(2,1)S(1)} %copy-done.93), channel_id=1, source_target_pairs={{0,16},{24,8},{1,17},{25,9},{2,18},{26,10},{3,19},{27,11},{4,20},{... | collective-permute-start | bytes 5160968 | tf_op jit(solution)/shard_map/ppermute | solution.py:159
  292.8 72.6 %collective-permute-start.48 = (bf16[3,320,896]{2,1,0:T(8,128)(2,1)S(1)}, bf16[3,320,896]{2,1,0:T(8,128)(2,1)}, u32[]{:S(2)}, u32[]{:S(2)}) collective-permute-start(bf16[3,320,896]{2,1,0:T(8,128)(2,1)S(1)} %copy-done.92), channel_id=1, source_target_pairs={{0,16},{24,8},{1,17},{25,9},{2,18},{26,10},{3,19},{27,11},{4,20},{... | collective-permute-start | bytes 5160968 | tf_op jit(solution)/shard_map/ppermute | solution.py:159
  295.4 71.2 %collective-permute-start.10 = (bf16[4,128,1280]{2,1,0:T(8,128)(2,1)S(1)}, bf16[4,128,1280]{2,1,0:T(8,128)(2,1)S(1)}, u32[]{:S(2)}, u32[]{:S(2)}) collective-permute-start(bf16[4,128,1280]{2,1,0:T(8,128)(2,1)S(1)} %collective-permute-done.9), channel_id=1, source_target_pairs={{0,1},{1,0},{2,3},{3,2},{4,5},{5,4},{6,7},{7,6},{8,9},{9,8},{10,11... | collective-permute-start | bytes 3932168 | tf_op jit(solution)/shard_map/ppermute | solution.py:74
  299.8 70.4 %collective-permute-start.12 = (bf16[4,128,1280]{2,1,0:T(8,128)(2,1)S(1)}, bf16[4,128,1280]{2,1,0:T(8,128)(2,1)S(1)}, u32[]{:S(2)}, u32[]{:S(2)}) collective-permute-start(bf16[4,128,1280]{2,1,0:T(8,128)(2,1)S(1)} %collective-permute-done.11), channel_id=1, source_target_pairs={{0,1},{1,0},{2,3},{3,2},{4,5},{5,4},{6,7},{7,6},{8,9},{9,8},{10,11... | collective-permute-start | bytes 3932168 | tf_op jit(solution)/shard_map/ppermute | solution.py:74
  301.3 185.9 %collective-permute-start.47 = (bf16[3,320,896]{2,1,0:T(8,128)(2,1)}, bf16[3,320,896]{2,1,0:T(8,128)(2,1)}, u32[]{:S(2)}, u32[]{:S(2)}) collective-permute-start(bf16[3,320,896]{2,1,0:T(8,128)(2,1)} %collective-permute-done.46), channel_id=1, source_target_pairs={{8,0},{16,24},{9,1},{17,25},{10,2},{18,26},{11,3},{19,27},{12,4},{... | collective-permute-start | bytes 5160968 | tf_op jit(solution)/shard_map/ppermute | solution.py:159
  329.5 161.7 %collective-permute-start.42 = (bf16[3,320,896]{2,1,0:T(8,128)(2,1)}, bf16[3,320,896]{2,1,0:T(8,128)(2,1)}, u32[]{:S(2)}, u32[]{:S(2)}) collective-permute-start(bf16[3,320,896]{2,1,0:T(8,128)(2,1)} %collective-permute-done.41), channel_id=1, source_target_pairs={{8,0},{16,24},{9,1},{17,25},{10,2},{18,26},{11,3},{19,27},{12,4},{... | collective-permute-start | bytes 5160968 | tf_op jit(solution)/shard_map/ppermute | solution.py:159
  365.3 150.1 %collective-permute-start.44 = (bf16[3,320,896]{2,1,0:T(8,128)(2,1)}, bf16[3,320,896]{2,1,0:T(8,128)(2,1)}, u32[]{:S(2)}, u32[]{:S(2)}) collective-permute-start(bf16[3,320,896]{2,1,0:T(8,128)(2,1)} %collective-permute-done.43), channel_id=1, source_target_pairs={{8,0},{16,24},{9,1},{17,25},{10,2},{18,26},{11,3},{19,27},{12,4},{... | collective-permute-start | bytes 5160968 | tf_op jit(solution)/shard_map/ppermute | solution.py:159
  366.6 184.3 %collective-permute-start.49 = (bf16[3,320,896]{2,1,0:T(8,128)(2,1)}, bf16[3,320,896]{2,1,0:T(8,128)(2,1)}, u32[]{:S(2)}, u32[]{:S(2)}) collective-permute-start(bf16[3,320,896]{2,1,0:T(8,128)(2,1)} %collective-permute-done.48), channel_id=1, source_target_pairs={{8,0},{16,24},{9,1},{17,25},{10,2},{18,26},{11,3},{19,27},{12,4},{... | collective-permute-start | bytes 5160968 | tf_op jit(solution)/shard_map/ppermute | solution.py:159
  449.9 114.0 %collective-permute-start.33 = (bf16[256,1280]{1,0:T(8,128)(2,1)S(1)}, bf16[256,1280]{1,0:T(8,128)(2,1)}, u32[]{:S(2)}, u32[]{:S(2)}) collective-permute-start(bf16[256,1280]{1,0:T(8,128)(2,1)S(1)} %get-tuple-element.152), channel_id=1, source_target_pairs={{0,1},{1,0},{2,3},{3,2},{4,5},{5,4},{6,7},{7,6},{8,9},{9,8},{10,11... | collective-permute-start | bytes 1966088 | tf_op jit(solution)/shard_map/ppermute | solution.py:74
  487.2 75.0 %collective-permute-start.34 = (bf16[256,1280]{1,0:T(8,128)(2,1)S(1)}, bf16[256,1280]{1,0:T(8,128)(2,1)S(1)}, u32[]{:S(2)}, u32[]{:S(2)}) collective-permute-start(bf16[256,1280]{1,0:T(8,128)(2,1)S(1)} %get-tuple-element.152), channel_id=1, source_target_pairs={{0,2},{1,3},{2,0},{3,1},{4,6},{5,7},{6,4},{7,5},{8,10},{9,11},{10,... | collective-permute-start | bytes 1966088 | tf_op jit(solution)/shard_map/ppermute | solution.py:74
  491.2 72.1 %collective-permute-start.36 = (bf16[256,1280]{1,0:T(8,128)(2,1)S(1)}, bf16[256,1280]{1,0:T(8,128)(2,1)S(1)}, u32[]{:S(2)}, u32[]{:S(2)}) collective-permute-start(bf16[256,1280]{1,0:T(8,128)(2,1)S(1)} %get-tuple-element.152), channel_id=1, source_target_pairs={{0,4},{1,5},{2,6},{3,7},{4,0},{5,1},{6,2},{7,3},{8,12},{9,13},{10,... | collective-permute-start | bytes 1966088 | tf_op jit(solution)/shard_map/ppermute | solution.py:74
  515.4 48.1 %collective-permute-start.38 = (bf16[256,1280]{1,0:T(8,128)(2,1)S(1)}, bf16[256,1280]{1,0:T(8,128)(2,1)}, u32[]{:S(2)}, u32[]{:S(2)}) collective-permute-start(bf16[256,1280]{1,0:T(8,128)(2,1)S(1)} %get-tuple-element.152), channel_id=1, source_target_pairs={{0,6},{1,7},{2,4},{3,5},{4,2},{5,3},{6,0},{7,1},{8,14},{9,15},{10,... | collective-permute-start | bytes 1966088 | tf_op jit(solution)/shard_map/ppermute | solution.py:74
  550.9 245.3 %collective-permute-start.82 = (bf16[4,4,120,896]{3,2,1,0:T(8,128)(2,1)}, bf16[4,4,120,896]{3,2,1,0:T(8,128)(2,1)}, u32[]{:S(2)}, u32[]{:S(2)}) collective-permute-start(bf16[4,4,120,896]{3,2,1,0:T(8,128)(2,1)} %dynamic-slice_bitcast_fusion), channel_id=1, source_target_pairs={{0,1},{1,0},{2,3},{3,2},{4,5},{5,4},{6,7},{7,6},{8,9},{9,8},{10,11... | collective-permute-start | bytes 10321928 | tf_op jit(solution)/shard_map/ppermute | solution.py:74
  733.8 203.8 %collective-permute-start.90 = (bf16[3,320,896]{2,1,0:T(8,128)(2,1)}, bf16[3,320,896]{2,1,0:T(8,128)(2,1)}, u32[]{:S(2)}, u32[]{:S(2)}) collective-permute-start(bf16[3,320,896]{2,1,0:T(8,128)(2,1)} %get-tuple-element.168), channel_id=1, source_target_pairs={{0,8},{24,16},{1,9},{25,17},{2,10},{26,18},{3,11},{27,19},{4,12},{... | collective-permute-start | bytes 5160968 | tf_op jit(solution)/shard_map/ppermute | solution.py:159
  796.2 182.1 %collective-permute-start.50 = (bf16[4,256,1280]{2,1,0:T(8,128)(2,1)}, bf16[4,256,1280]{2,1,0:T(8,128)(2,1)}, u32[]{:S(2)}, u32[]{:S(2)}) collective-permute-start(bf16[4,256,1280]{2,1,0:T(8,128)(2,1)} %pad_maximum_fusion.3), channel_id=1, source_target_pairs={{0,1},{1,0},{2,3},{3,2},{4,5},{5,4},{6,7},{7,6},{8,9},{9,8},{10,11... | collective-permute-start | bytes 7864328 | tf_op jit(solution)/shard_map/ppermute | solution.py:74
  871.8 56.8 %collective-permute-start.66 = (bf16[256,1280]{1,0:T(8,128)(2,1)}, bf16[256,1280]{1,0:T(8,128)(2,1)}, u32[]{:S(2)}, u32[]{:S(2)}) collective-permute-start(bf16[256,1280]{1,0:T(8,128)(2,1)} %get-tuple-element.205), channel_id=1, source_target_pairs={{16,0},{24,8},{17,1},{25,9},{18,2},{26,10},{19,3},{27,11},{20,4},{... | collective-permute-start | bytes 1966088 | tf_op jit(solution)/shard_map/ppermute | solution.py:84
  873.1 56.9 %collective-permute-start.67 = (bf16[256,1280]{1,0:T(8,128)(2,1)}, bf16[256,1280]{1,0:T(8,128)(2,1)}, u32[]{:S(2)}, u32[]{:S(2)}) collective-permute-start(bf16[256,1280]{1,0:T(8,128)(2,1)} %get-tuple-element.204), channel_id=1, source_target_pairs={{24,0},{25,1},{26,2},{27,3},{28,4},{29,5},{30,6},{31,7}} | collective-permute-start | bytes 1966088 | tf_op jit(solution)/shard_map/ppermute | solution.py:84
  930.0 43.7 %collective-permute-start.85 = (bf16[4,120,896]{2,1,0:T(8,128)(2,1)}, bf16[4,120,896]{2,1,0:T(8,128)(2,1)}, u32[]{:S(2)}, u32[]{:S(2)}) collective-permute-start(bf16[4,120,896]{2,1,0:T(8,128)(2,1)} %get-tuple-element.199), channel_id=1, source_target_pairs={{0,6},{1,7},{2,4},{3,5},{4,2},{5,3},{6,0},{7,1},{8,14},{9,15},{10,... | collective-permute-start | bytes 2580488 | tf_op jit(solution)/shard_map/ppermute | solution.py:74
  939.0 75.1 %collective-permute-start.95 = (bf16[3,320,896]{2,1,0:T(8,128)(2,1)}, bf16[3,320,896]{2,1,0:T(8,128)(2,1)S(1)}, u32[]{:S(2)}, u32[]{:S(2)}) collective-permute-start(bf16[3,320,896]{2,1,0:T(8,128)(2,1)} %get-tuple-element.171), channel_id=1, source_target_pairs={{0,8},{24,16},{1,9},{25,17},{2,10},{26,18},{3,11},{27,19},{4,12},{... | collective-permute-start | bytes 5160968 | tf_op jit(solution)/shard_map/ppermute | solution.py:159
  966.8 83.5 %collective-permute-start.97 = (bf16[3,320,896]{2,1,0:T(8,128)(2,1)}, bf16[3,320,896]{2,1,0:T(8,128)(2,1)S(1)}, u32[]{:S(2)}, u32[]{:S(2)}) collective-permute-start(bf16[3,320,896]{2,1,0:T(8,128)(2,1)} %get-tuple-element.170), channel_id=1, source_target_pairs={{0,8},{24,16},{1,9},{25,17},{2,10},{26,18},{3,11},{27,19},{4,12},{... | collective-permute-start | bytes 5160968 | tf_op jit(solution)/shard_map/ppermute | solution.py:159
  973.6 191.4 %collective-permute-start.68 = (bf16[4,4,128,1280]{3,2,1,0:T(8,128)(2,1)}, bf16[4,4,128,1280]{3,2,1,0:T(8,128)(2,1)}, u32[]{:S(2)}, u32[]{:S(2)}) collective-permute-start(bf16[4,4,128,1280]{3,2,1,0:T(8,128)(2,1)} %fusion.11), channel_id=1, source_target_pairs={{0,1},{1,0},{2,3},{3,2},{4,5},{5,4},{6,7},{7,6},{8,9},{9,8},{10,11... | collective-permute-start | bytes 15728648 | tf_op jit(solution)/shard_map/ppermute | solution.py:74
  978.4 75.9 %collective-permute-start.86 = (bf16[120,896]{1,0:T(8,128)(2,1)S(1)}, bf16[120,896]{1,0:T(8,128)(2,1)S(1)}, u32[]{:S(2)}, u32[]{:S(2)}) collective-permute-start(bf16[120,896]{1,0:T(8,128)(2,1)S(1)} %get-tuple-element.219), channel_id=1, source_target_pairs={{0,8},{8,16},{16,24},{24,0},{1,9},{9,17},{17,25},{25,1},{2,10},{10... | collective-permute-start | bytes 645128 | tf_op jit(solution)/shard_map/ppermute | solution.py:79
  980.9 92.2 %collective-permute-start.51 = (bf16[256,1280]{1,0:T(8,128)(2,1)S(1)}, bf16[256,1280]{1,0:T(8,128)(2,1)S(1)}, u32[]{:S(2)}, u32[]{:S(2)}) collective-permute-start(bf16[256,1280]{1,0:T(8,128)(2,1)S(1)} %get-tuple-element.160), channel_id=1, source_target_pairs={{0,2},{1,3},{2,0},{3,1},{4,6},{5,7},{6,4},{7,5},{8,10},{9,11},{10,... | collective-permute-start | bytes 1966088 | tf_op jit(solution)/shard_map/ppermute | solution.py:74
  1014.0 59.8 %collective-permute-start.52 = (bf16[256,1280]{1,0:T(8,128)(2,1)S(1)}, bf16[256,1280]{1,0:T(8,128)(2,1)S(1)}, u32[]{:S(2)}, u32[]{:S(2)}) collective-permute-start(bf16[256,1280]{1,0:T(8,128)(2,1)S(1)} %get-tuple-element.161), channel_id=1, source_target_pairs={{0,4},{1,5},{2,6},{3,7},{4,0},{5,1},{6,2},{7,3},{8,12},{9,13},{10,... | collective-permute-start | bytes 1966088 | tf_op jit(solution)/shard_map/ppermute | solution.py:74
  1073.0 69.5 %collective-permute-start.89 = (bf16[3,320,896]{2,1,0:T(8,128)(2,1)S(1)}, bf16[3,320,896]{2,1,0:T(8,128)(2,1)S(1)}, u32[]{:S(2)}, u32[]{:S(2)}) collective-permute-start(bf16[3,320,896]{2,1,0:T(8,128)(2,1)S(1)} %copy-done.88), channel_id=1, source_target_pairs={{0,8},{8,0},{16,24},{24,16},{1,9},{9,1},{17,25},{25,17},{2,10},{10... | collective-permute-start | bytes 5160968 | tf_op jit(solution)/shard_map/ppermute | solution.py:159
  1073.0 70.7 %collective-permute-start.91 = (bf16[3,320,896]{2,1,0:T(8,128)(2,1)S(1)}, bf16[3,320,896]{2,1,0:T(8,128)(2,1)S(1)}, u32[]{:S(2)}, u32[]{:S(2)}) collective-permute-start(bf16[3,320,896]{2,1,0:T(8,128)(2,1)S(1)} %add_convert_fusion.5), channel_id=1, source_target_pairs={{8,16},{16,8},{9,17},{17,9},{10,18},{18,10},{11,19},{19,11},{12,20... | collective-permute-start | bytes 5160968 | tf_op jit(solution)/shard_map/ppermute | solution.py:159
  1073.8 79.9 %collective-permute-start.93 = (bf16[3,320,896]{2,1,0:T(8,128)(2,1)S(1)}, bf16[3,320,896]{2,1,0:T(8,128)(2,1)S(1)}, u32[]{:S(2)}, u32[]{:S(2)}) collective-permute-start(bf16[3,320,896]{2,1,0:T(8,128)(2,1)S(1)} %add_convert_fusion.4), channel_id=1, source_target_pairs={{16,0},{8,24},{17,1},{9,25},{18,2},{10,26},{19,3},{11,27},{20,4},{... | collective-permute-start | bytes 5160968 | tf_op jit(solution)/shard_map/ppermute | solution.py:159
  1076.6 83.5 %collective-permute-start.75 = (bf16[4,4,40,1280]{3,2,1,0:T(8,128)(2,1)}, bf16[4,4,40,1280]{3,2,1,0:T(8,128)(2,1)}, u32[]{:S(2)}, u32[]{:S(2)}) collective-permute-start(bf16[4,4,40,1280]{3,2,1,0:T(8,128)(2,1)} %dynamic-slice_bitcast_fusion.7), channel_id=1, source_target_pairs={{0,1},{1,0},{2,3},{3,2},{4,5},{5,4},{6,7},{7,6},{8,9},{9,8},{10,11... | collective-permute-start | bytes 4915208 | tf_op jit(solution)/shard_map/ppermute | solution.py:74
  1143.7 43.4 %collective-permute-start.94 = (bf16[3,320,896]{2,1,0:T(8,128)(2,1)}, bf16[3,320,896]{2,1,0:T(8,128)(2,1)}, u32[]{:S(2)}, u32[]{:S(2)}) collective-permute-start(bf16[3,320,896]{2,1,0:T(8,128)(2,1)} %get-tuple-element.169), channel_id=1, source_target_pairs={{0,8},{8,0},{16,24},{24,16},{1,9},{9,1},{17,25},{25,17},{2,10},{10... | collective-permute-start | bytes 5160968 | tf_op jit(solution)/shard_map/ppermute | solution.py:159
  1143.8 44.5 %collective-permute-start.96 = (bf16[3,320,896]{2,1,0:T(8,128)(2,1)}, bf16[3,320,896]{2,1,0:T(8,128)(2,1)}, u32[]{:S(2)}, u32[]{:S(2)}) collective-permute-start(bf16[3,320,896]{2,1,0:T(8,128)(2,1)} %add_convert_fusion.3), channel_id=1, source_target_pairs={{8,16},{16,8},{9,17},{17,9},{10,18},{18,10},{11,19},{19,11},{12,20... | collective-permute-start | bytes 5160968 | tf_op jit(solution)/shard_map/ppermute | solution.py:159
  1155.0 64.7 %collective-permute-start.98 = (bf16[3,320,896]{2,1,0:T(8,128)(2,1)}, bf16[3,320,896]{2,1,0:T(8,128)(2,1)}, u32[]{:S(2)}, u32[]{:S(2)}) collective-permute-start(bf16[3,320,896]{2,1,0:T(8,128)(2,1)} %add_convert_fusion.2), channel_id=1, source_target_pairs={{16,0},{8,24},{17,1},{9,25},{18,2},{10,26},{19,3},{11,27},{20,4},{... | collective-permute-start | bytes 5160968 | tf_op jit(solution)/shard_map/ppermute | solution.py:159
  1164.2 60.4 %collective-permute-start.76 = (bf16[4,40,1280]{2,1,0:T(8,128)(2,1)}, bf16[4,40,1280]{2,1,0:T(8,128)(2,1)S(1)}, u32[]{:S(2)}, u32[]{:S(2)}) collective-permute-start(bf16[4,40,1280]{2,1,0:T(8,128)(2,1)} %get-tuple-element.209), channel_id=1, source_target_pairs={{0,2},{1,3},{2,0},{3,1},{4,6},{5,7},{6,4},{7,5},{8,10},{9,11},{10,... | collective-permute-start | bytes 1228808 | tf_op jit(solution)/shard_map/ppermute | solution.py:74
  1173.7 83.0 %collective-permute-start.69 = (bf16[4,128,1280]{2,1,0:T(8,128)(2,1)S(1)}, bf16[4,128,1280]{2,1,0:T(8,128)(2,1)S(1)}, u32[]{:S(2)}, u32[]{:S(2)}) collective-permute-start(bf16[4,128,1280]{2,1,0:T(8,128)(2,1)S(1)} %get-tuple-element.181), channel_id=1, source_target_pairs={{0,2},{1,3},{2,0},{3,1},{4,6},{5,7},{6,4},{7,5},{8,10},{9,11},{10,... | collective-permute-start | bytes 3932168 | tf_op jit(solution)/shard_map/ppermute | solution.py:74
  1187.1 70.0 %collective-permute-start.70 = (bf16[4,128,1280]{2,1,0:T(8,128)(2,1)S(1)}, bf16[4,128,1280]{2,1,0:T(8,128)(2,1)S(1)}, u32[]{:S(2)}, u32[]{:S(2)}) collective-permute-start(bf16[4,128,1280]{2,1,0:T(8,128)(2,1)S(1)} %get-tuple-element.183), channel_id=1, source_target_pairs={{0,4},{1,5},{2,6},{3,7},{4,0},{5,1},{6,2},{7,3},{8,12},{9,13},{10,... | collective-permute-start | bytes 3932168 | tf_op jit(solution)/shard_map/ppermute | solution.py:74
  1188.2 68.9 %collective-permute-start.71 = (bf16[4,128,1280]{2,1,0:T(8,128)(2,1)S(1)}, bf16[4,128,1280]{2,1,0:T(8,128)(2,1)S(1)}, u32[]{:S(2)}, u32[]{:S(2)}) collective-permute-start(bf16[4,128,1280]{2,1,0:T(8,128)(2,1)S(1)} %get-tuple-element.182), channel_id=1, source_target_pairs={{0,6},{1,7},{2,4},{3,5},{4,2},{5,3},{6,0},{7,1},{8,14},{9,15},{10,... | collective-permute-start | bytes 3932168 | tf_op jit(solution)/shard_map/ppermute | solution.py:74
  (222 other events, 4045.0 us)

commit v2 on v1

v2 whole, which is shorter than its diff:
```python
import functools

import jax
import jax.numpy as jnp
from jax import lax
from jax.experimental import pallas as pl
from jax.experimental.pallas import tpu as pltpu
from jax.sharding import PartitionSpec as P

HEAD_DIM = 128
STEP = 10


NORM_EPS = 1e-06
THETA = 10000.0
CLIP_VALUE = 1.0
BETA_ONE = 0.9
BETA_TWO = 0.999
ADAM_EPS = 1e-08
DECAY = 0.1
RATE_MATRIX = 0.02
RATE_EXPERT = 0.1
RATE_GAIN = 0.3
MASKED = -1e30

F32 = jnp.float32
BF16 = jnp.bfloat16


def contract(left, right, left_dim, right_dim):
    return lax.dot_general(
        left, right, (((left_dim,), (right_dim,)), ((), ())), preferred_element_type=F32
    )


def rotary_tables(places, head_dim):
    half = head_dim // 2
    freq = THETA ** (-2.0 * jnp.arange(half, dtype=F32) / head_dim)
    angle = places.astype(F32)[:, None] * freq
    cosine, sine = jnp.cos(angle), jnp.sin(angle)
    return (jnp.concatenate([cosine, cosine], -1), jnp.concatenate([-sine, sine], -1))


def norm_forward(values, gain):
    inverse = lax.rsqrt(jnp.mean(values * values, axis=-1, keepdims=True) + NORM_EPS)
    scaled = values * inverse
    return ((scaled * gain).astype(BF16), scaled, inverse)


def norm_backward(grad, scaled, inverse, gain):
    local = grad * gain
    return inverse * (local - scaled * jnp.mean(local * scaled, axis=-1, keepdims=True))


def adam(master, first, second, grad, scale, rate):
    clipped = grad * scale
    first_new = BETA_ONE * first + (1.0 - BETA_ONE) * clipped
    second_new = BETA_TWO * second + (1.0 - BETA_TWO) * clipped * clipped
    first_hat = first_new / (1.0 - BETA_ONE**STEP)
    second_hat = second_new / (1.0 - BETA_TWO**STEP)
    master_new = master - rate * (first_hat / (jnp.sqrt(second_hat) + ADAM_EPS) + DECAY * master)
    return (master_new, first_new, second_new)


def after(value, *others):
    return lax.optimization_barrier((value,) + others)[0]


def swap(value, mask):
    size = lax.axis_size("expert")
    return lax.ppermute(value, "expert", [(i, i ^ mask) for i in range(size)])


def rotate(value, step):
    size = lax.axis_size("dp")
    return lax.ppermute(value, "dp", [(i, (i + step) % size) for i in range(size)])


def shift(value, step):
    size = lax.axis_size("dp")
    return lax.ppermute(
        value, "dp", [(i, i + step) for i in range(size) if 0 <= i + step < size]
    )


def put(buffer, block, index, axis):
    return lax.dynamic_update_slice_in_dim(buffer, jnp.expand_dims(block, axis), index, axis)


def pick(buffer, index, axis):
    return lax.dynamic_index_in_dim(buffer, index, axis, keepdims=False)


def fan(block, *others):
    size = lax.axis_size("expert")
    block = after(block, *others) if others else block
    return [block] + [swap(block, mask) for mask in range(2, size, 2)]


def gather_swaps(block, *others):
    even = jnp.stack(fan(block, *others))
    return even, swap(even, 1)


def join_cores(even, other):
    return [even[k].astype(F32) + other[k].astype(F32) for k in range(even.shape[0])]


def join_chips(summed):
    total = summed[0]
    for index in range(1, len(summed)):
        total = total + swap(summed[index].astype(BF16), 2 * index).astype(F32)
    return total


def scatter_dense(grad):
    size, here = lax.axis_size("expert"), lax.axis_index("expert")
    deep, level = lax.axis_size("dp"), lax.axis_index("dp")
    core, chip = here % 2, here // 2
    low = grad.astype(BF16).reshape((deep, size // 2, 2) + grad.shape[2:])
    other = swap(pick(low, 1 - core, 2), 1)
    summed = (pick(low, core, 2).astype(F32) + other.astype(F32)).astype(BF16)
    total = pick(summed, chip, 1).astype(F32)
    for mask in range(1, size // 2):
        total = total + swap(pick(summed, chip ^ mask, 1), 2 * mask).astype(F32)
    column = total.astype(BF16)
    result = pick(total, level, 0)
    for step in range(1, deep):
        result = result + rotate(pick(column, (level + step) % deep, 0), step).astype(F32)
    return result


VMEM_LIMIT = 60 * 1024 * 1024


def product(left, right, left_dim, right_dim):
    return lax.dot_general(
        left, right, (((left_dim,), (right_dim,)), ((), ())), preferred_element_type=F32
    )


def kernel_params(steps):
    return pltpu.CompilerParams(
        dimension_semantics=("arbitrary",) * steps, vmem_limit_bytes=VMEM_LIMIT
    )


def whole(array):
    shape = array.shape
    return pl.BlockSpec(shape, lambda *_: (0,) * len(shape), pipeline_mode=pl.Buffered(1))


def assemble_kernel(place_ref, even, odd, out):
    core = place_ref[0] % 2
    out[:, :, pl.ds(core, 1)] = jnp.swapaxes(even[0], 0, 1)[:, :, None]
    out[:, :, pl.ds(1 - core, 1)] = jnp.swapaxes(odd[0], 0, 1)[:, :, None]


def assemble(even, odd):
    chips, deep, parts, rows, width = even.shape
    here = lax.axis_index("expert")
    chip = pl.BlockSpec(
        (1, deep, parts, rows, width), lambda c, p: (c ^ (p[0] // 2), 0, 0, 0, 0)
    )
    joined = pl.pallas_call(
        assemble_kernel,
        grid_spec=pltpu.PrefetchScalarGridSpec(
            num_scalar_prefetch=1,
            grid=(chips,),
            in_specs=[chip, chip],
            out_specs=pl.BlockSpec(
                (parts, deep, 2, rows, width), lambda c, p: (0, 0, c, 0, 0)
            ),
        ),
        out_shape=jax.ShapeDtypeStruct((parts, deep, 2 * chips, rows, width), even.dtype),
        compiler_params=kernel_params(1),
        cost_estimate=pl.CostEstimate(
            flops=0, bytes_accessed=8 * even.size, transcendentals=0
        ),
        name="assemble",
    )(here[None], even, odd)
    return joined.reshape(parts, deep * 2 * chips * rows, width)


def turn_head(values, cosine, sine):
    return values * cosine + pltpu.roll(values, HEAD_DIM // 2, 1) * sine


def head_weights(query, keys, allowed):
    scores = product(query, keys, 1, 1) * HEAD_DIM ** (-0.5)
    scores = jnp.where(allowed, scores, MASKED)
    raised = jnp.exp(scores - jnp.max(scores, axis=-1, keepdims=True))
    return raised / jnp.sum(raised, axis=-1, keepdims=True)


def visible_keys(place, own_starts, starts):
    shape = (own_starts.shape[0], starts.shape[1])
    query_index = place + lax.broadcasted_iota(jnp.int32, shape, 0)
    key_index = lax.broadcasted_iota(jnp.int32, shape, 1)
    return (own_starts == starts) & (key_index <= query_index)


def attention_kernel(
    place_ref, normed, wq, wk, wv, cosine, sine, starts, own_starts, q_out, k_out, v_out, o_out, low_out
):
    rows = q_out.shape[0]
    place = pl.multiple_of(place_ref[0], rows)
    own = normed[pl.ds(place, rows), :]
    everything = normed[...]
    allowed = visible_keys(place, own_starts[...], starts[...])
    query = product(own, wq[0], 1, 0)
    keys = product(everything, wk[0], 1, 0)
    values = product(everything, wv[0], 1, 0).astype(BF16)
    v_out[...] = values
    own_cosine, own_sine = cosine[pl.ds(place, rows), :], sine[pl.ds(place, rows), :]
    for head in range(q_out.shape[1] // HEAD_DIM):
        lanes = slice(head * HEAD_DIM, (head + 1) * HEAD_DIM)
        turned_query = turn_head(query[:, lanes], own_cosine, own_sine).astype(BF16)
        turned_keys = turn_head(keys[:, lanes], cosine[...], sine[...]).astype(BF16)
        weights = head_weights(turned_query, turned_keys, allowed).astype(BF16)
        mixed = product(weights, values[:, lanes], 1, 0)
        q_out[:, lanes] = turned_query
        k_out[:, lanes] = turned_keys
        o_out[:, lanes] = mixed
        low_out[:, lanes] = mixed.astype(BF16)


def attention(place, normed, projections, cosine, sine, starts, rows):
    length, width = normed.shape
    span = 2 * HEAD_DIM
    own_starts = lax.dynamic_slice_in_dim(starts, place, rows)[:, None]
    starts = starts[None, :]
    column = lambda index: pl.BlockSpec((1, width, span), lambda p, _: (index, 0, p))
    blocks = lambda count: pl.BlockSpec((count, span), lambda p, _: (0, p))
    return pl.pallas_call(
        attention_kernel,
        grid_spec=pltpu.PrefetchScalarGridSpec(
            num_scalar_prefetch=1,
            grid=(width // span,),
            in_specs=[
                whole(normed),
                column(0),
                column(1),
                column(2),
                whole(cosine),
                whole(sine),
                whole(starts),
                whole(own_starts),
            ],
            out_specs=[blocks(rows), blocks(length), blocks(length), blocks(rows), blocks(rows)],
        ),
        out_shape=[
            jax.ShapeDtypeStruct((rows, width), BF16),
            jax.ShapeDtypeStruct((length, width), BF16),
            jax.ShapeDtypeStruct((length, width), BF16),
            jax.ShapeDtypeStruct((rows, width), F32),
            jax.ShapeDtypeStruct((rows, width), BF16),
        ],
        compiler_params=kernel_params(1),
        cost_estimate=pl.CostEstimate(
            flops=2 * width * width * (rows + 2 * length) + 4 * rows * length * width,
            bytes_accessed=6 * width * width + 10 * length * width,
            transcendentals=rows * length * width // HEAD_DIM,
        ),
        name="attention_forward",
    )(place[None], normed, projections, projections, projections, cosine, sine, starts, own_starts)


def attention_grad_kernel(
    place_ref, turned_normed, own_turned, wq, wk, wv, wo, q, k, v, o, arriving,
    cosine, sine, starts, own_starts, grads, normed_grad, own_grad, dq_s, dk_s, dv_s,
):
    rows = q.shape[0]
    place = pl.multiple_of(place_ref[0], rows)
    allowed = visible_keys(place, own_starts[...], starts[...])
    own_cosine, own_sine = cosine[pl.ds(place, rows), :], sine[pl.ds(place, rows), :]
    mixed_grad = product(arriving[...], wo[...], 1, 1).astype(BF16)
    for head in range(q.shape[1] // HEAD_DIM):
        lanes = slice(head * HEAD_DIM, (head + 1) * HEAD_DIM)
        query, keys, values = q[:, lanes], k[:, lanes], v[:, lanes]
        incoming = mixed_grad[:, lanes]
        weights = head_weights(query, keys, allowed)
        correction = jnp.sum(incoming.astype(F32) * o[:, lanes], axis=-1, keepdims=True)
        weights_grad = product(incoming, values, 1, 1)
        scores_grad = (weights * (weights_grad - correction)).astype(BF16)
        factor = HEAD_DIM ** (-0.5)
        query_grad = product(scores_grad, keys, 1, 0) * factor
        keys_grad = product(scores_grad, query, 0, 0) * factor
        values_grad = product(weights.astype(BF16), incoming, 0, 0)
        dq_s[:, lanes] = turn_head(query_grad, own_cosine, -own_sine).astype(BF16)
        dk_s[:, lanes] = turn_head(keys_grad, cosine[...], -sine[...]).astype(BF16)
        dv_s[:, lanes] = values_grad.astype(BF16)
    dq, dk, dv = dq_s[...], dk_s[...], dv_s[...]
    grads[0] = product(own_turned[...], dq, 1, 0).astype(BF16)
    grads[1] = product(turned_normed[...], dk, 1, 0).astype(BF16)
    grads[2] = product(turned_normed[...], dv, 1, 0).astype(BF16)
    part = product(dk, wk[0], 1, 1) + product(dv, wv[0], 1, 1)
    own_part = product(dq, wq[0], 1, 1)

    @pl.when(pl.program_id(0) == 0)
    def _():
        normed_grad[...] = part
        own_grad[...] = own_part

    @pl.when(pl.program_id(0) > 0)
    def _():
        normed_grad[...] += part
        own_grad[...] += own_part


def attention_grad(place, normed, own_normed, projections, wo, q, k, v, o, arriving, cosine, sine, starts):
    length, width = normed.shape
    rows = q.shape[0]
    span = 2 * HEAD_DIM
    own_starts = lax.dynamic_slice_in_dim(starts, place, rows)[:, None]
    starts = starts[None, :]
    turned, own_turned = normed.T, own_normed.T
    column = lambda index: pl.BlockSpec((1, width, span), lambda p, _: (index, 0, p))
    blocks = lambda count: pl.BlockSpec((count, span), lambda p, _: (0, p))
    return pl.pallas_call(
        attention_grad_kernel,
        grid_spec=pltpu.PrefetchScalarGridSpec(
            num_scalar_prefetch=1,
            grid=(width // span,),
            in_specs=[
                whole(turned),
                whole(own_turned),
                column(0),
                column(1),
                column(2),
                pl.BlockSpec((span, width), lambda p, _: (p, 0)),
                blocks(rows),
                blocks(length),
                blocks(length),
                blocks(rows),
                whole(arriving),
                whole(cosine),
                whole(sine),
                whole(starts),
                whole(own_starts),
            ],
            out_specs=[
                pl.BlockSpec((3, width, span), lambda p, _: (0, 0, p)),
                pl.BlockSpec((length, width), lambda p, _: (0, 0)),
                pl.BlockSpec((rows, width), lambda p, _: (0, 0)),
            ],
            scratch_shapes=[
                pltpu.VMEM((rows, span), BF16),
                pltpu.VMEM((length, span), BF16),
                pltpu.VMEM((length, span), BF16),
            ],
        ),
        out_shape=[
            jax.ShapeDtypeStruct((3, width, width), BF16),
            jax.ShapeDtypeStruct((length, width), F32),
            jax.ShapeDtypeStruct((rows, width), F32),
        ],
        compiler_params=kernel_params(1),
        cost_estimate=pl.CostEstimate(
            flops=4 * width * width * (rows + 2 * length) + 10 * rows * length * width,
            bytes_accessed=14 * width * width + 14 * length * width,
            transcendentals=rows * length * width // HEAD_DIM,
        ),
        name="attention_backward",
    )(
        place[None], turned, own_turned, projections, projections, projections, wo,
        q, k, v, o, arriving, cosine, sine, starts, own_starts,
    )


def expert_kernel(has_before, split, part_rows, *refs):
    odd_n, even_n, odd_c, even_c, gates, weights = refs[:6]
    refs = refs[6:]
    if has_before:
        routed_in, entry_in = refs[:2]
        refs = refs[2:]
    if split:
        routed_odd, routed_even, entry_odd, entry_even = refs[:4]
        refs = refs[4:]
    else:
        routed_out, entry_out = refs[:2]
        refs = refs[2:]
    gate_grad, hidden_out, pair_out, both, down, arrived = refs
    step = pl.program_id(0)
    half = pl.num_programs(0) // 2
    hidden_width = weights.shape[3]

    @pl.when(step == 0)
    def _():
        copies = []
        for level in range(weights.shape[0]):
            rows = pl.ds(level * part_rows, part_rows)
            for index in range(3):
                if index < 2:
                    target = both.at[rows, pl.ds(index * hidden_width, hidden_width)]
                else:
                    target = down.at[rows]
                copies.append(
                    pltpu.make_async_copy(
                        weights.at[level, index, pl.ds(0, part_rows)],
                        target,
                        arrived.at[level, index],
                    )
                )
        for copy in copies:
            copy.start()
        for copy in copies:
            copy.wait()

    first = step < half
    tokens = jnp.where(first, odd_n[0], even_n[0])
    incoming = jnp.where(first, odd_c[0], even_c[0]).astype(F32)
    gate = gates[...]
    parts = product(tokens, both[...], 1, 0)
    gate_part, up_part = parts[:, :hidden_width], parts[:, hidden_width:]
    sigma = 1.0 / (1.0 + jnp.exp(-gate_part))
    smooth = gate_part * sigma
    hidden = (smooth * up_part).astype(BF16)
    hidden_out[...] = hidden
    result = product(hidden, down[...], 1, 1).astype(BF16).astype(F32)
    gate_grad[...] = jnp.sum(incoming * result, axis=-1, keepdims=True)
    routed = gate * result
    grad_pair = (gate * incoming).astype(BF16)
    grad_hidden = product(grad_pair, down[...], 1, 0)
    grad_gate = (grad_hidden * up_part * sigma * (1.0 + gate_part * (1.0 - sigma))).astype(BF16)
    grad_up = (grad_hidden * smooth).astype(BF16)
    grad_parts = jnp.concatenate([grad_gate, grad_up], axis=1)
    pair_out[...] = grad_parts
    entry = product(grad_parts, both[...], 1, 1).astype(BF16).astype(F32)
    if has_before:
        routed = routed + routed_in[...]
        entry = entry + entry_in[...]
    if split:

        @pl.when(first)
        def _():
            routed_odd[0] = routed.astype(BF16)
            entry_odd[0] = entry.astype(BF16)

        @pl.when(jnp.logical_not(first))
        def _():
            routed_even[0] = routed.astype(BF16)
            entry_even[0] = entry.astype(BF16)
    else:
        routed_out[...] = routed
        entry_out[...] = entry


def expert_pass(tokens, grads, gates, weights, part_rows, before, split):
    even_n, odd_n = tokens
    even_c, odd_c = grads
    count, rows, width = even_n.shape
    hidden_width = weights.shape[3]
    tiles = 2 * count
    total = tiles * rows
    odd = pl.BlockSpec((1, rows, width), lambda t: (jnp.minimum(t, count - 1), 0, 0))
    even = pl.BlockSpec((1, rows, width), lambda t: (jnp.maximum(t - count, 0), 0, 0))
    tile = lambda size: pl.BlockSpec((rows, size), lambda t: (t, 0))
    in_specs = [odd, even, odd, even, tile(1), pl.BlockSpec(memory_space=pl.ANY)]
    operands = [odd_n, even_n, odd_c, even_c, gates, weights]
    if before is not None:
        in_specs += [tile(width), tile(width)]
        operands += list(before)
    if split:
        out_specs = [odd, even, odd, even]
        out_shape = [jax.ShapeDtypeStruct((count, rows, width), BF16)] * 4
    else:
        out_specs = [tile(width), tile(width)]
        out_shape = [jax.ShapeDtypeStruct((total, width), F32)] * 2
    out_specs += [tile(1), tile(hidden_width), tile(2 * hidden_width)]
    out_shape += [
        jax.ShapeDtypeStruct((total, 1), F32),
        jax.ShapeDtypeStruct((total, hidden_width), BF16),
        jax.ShapeDtypeStruct((total, 2 * hidden_width), BF16),
    ]
    return pl.pallas_call(
        functools.partial(expert_kernel, before is not None, split, part_rows),
        grid=(tiles,),
        in_specs=in_specs,
        out_specs=out_specs,
        out_shape=out_shape,
        scratch_shapes=[
            pltpu.VMEM((width, 2 * hidden_width), BF16),
            pltpu.VMEM((width, hidden_width), BF16),
            pltpu.SemaphoreType.DMA((weights.shape[0], 3)),
        ],
        compiler_params=kernel_params(1),
        cost_estimate=pl.CostEstimate(
            flops=12 * total * width * hidden_width,
            bytes_accessed=total * (8 * width + 6 * hidden_width) + 6 * width * hidden_width,
            transcendentals=total * hidden_width,
        ),
        name="expert_pass",
    )(*operands)


def expert_grad_kernel(odd_n, even_n, odd_c, even_c, gates, hidden, pair, out):
    count, rows, span = odd_n.shape
    half = count * rows
    hidden_width = hidden.shape[1]
    tokens = jnp.concatenate(
        [odd_n[...].reshape(half, span), even_n[...].reshape(half, span)], axis=0
    )
    incoming = jnp.concatenate(
        [odd_c[...].reshape(half, span), even_c[...].reshape(half, span)], axis=0
    )
    grad_pair = (gates[...] * incoming.astype(F32)).astype(BF16)
    both = product(tokens, pair[...], 0, 0)
    out[0] = both[:, :hidden_width].astype(BF16)
    out[1] = both[:, hidden_width:].astype(BF16)
    out[2] = product(grad_pair, hidden[...], 0, 0).astype(BF16)


def expert_grad(tokens, grads, gates, hidden, pair):
    even_n, odd_n = tokens
    even_c, odd_c = grads
    count, rows, width = even_n.shape
    hidden_width = hidden.shape[1]
    span = 256
    stack = pl.BlockSpec((count, rows, span), lambda t: (0, 0, t))
    return pl.pallas_call(
        expert_grad_kernel,
        grid=(width // span,),
        in_specs=[stack, stack, stack, stack, whole(gates), whole(hidden), whole(pair)],
        out_specs=pl.BlockSpec((3, span, hidden_width), lambda t: (0, t, 0)),
        out_shape=jax.ShapeDtypeStruct((3, width, hidden_width), BF16),
        compiler_params=kernel_params(1),
        cost_estimate=pl.CostEstimate(
            flops=12 * count * rows * width * hidden_width,
            bytes_accessed=8 * count * rows * (width + 2 * hidden_width) + 6 * width * hidden_width,
            transcendentals=0,
        ),
        name="expert_weight_grad",
    )(odd_n, even_n, odd_c, even_c, gates, hidden, pair)


def body(
    block_input_vectors,
    output_sensitivity,
    rotary_offsets,
    dispatched_specialist_ids,
    specialist_quotas,
    storage_holder,
    mixer_projection_matrices,
    mixer_mean_estimate,
    mixer_variance_estimate,
    common_projection_matrices,
    common_mean_estimate,
    common_variance_estimate,
    gating_projection_matrix,
    gating_mean_estimate,
    gating_variance_estimate,
    scaling_factors,
    scaling_mean_estimate,
    scaling_variance_estimate,
    dispatched_projection_matrices,
    dispatched_mean_estimate,
    dispatched_variance_estimate,
):
    token_rows = block_input_vectors.shape[1]
    width = block_input_vectors.shape[2]
    head_dim = HEAD_DIM
    heads = width // head_dim
    length = rotary_offsets.shape[1]
    specialist_total = specialist_quotas.shape[0]
    expert_local = dispatched_projection_matrices.shape[0]
    hidden_width = dispatched_projection_matrices.shape[3]
    part_rows = dispatched_projection_matrices.shape[2]
    dense_rows = mixer_projection_matrices.shape[1]
    groups = lax.axis_size("expert")
    deep = lax.axis_size("dp")
    here = lax.axis_index("expert")
    level = lax.axis_index("dp")
    scale_attn = head_dim ** (-0.5)
    straight = deep == 4

    attn_own = mixer_projection_matrices.astype(BF16)
    shared_own = common_projection_matrices.astype(BF16)
    router_own = gating_projection_matrix.astype(BF16)
    gain_own = scaling_factors.astype(BF16)
    expert_own = dispatched_projection_matrices.astype(BF16)

    everyone = deep * groups
    small = jnp.concatenate([router_own.reshape(-1), gain_own.reshape(-1)])
    small_size = small.shape[0]
    small_rows = -(-small_size // 1024) * 8
    small = jnp.pad(small, (0, small_rows * 128 - small_size)).reshape(small_rows, 128)
    small_all = lax.all_to_all(
        jnp.broadcast_to(small, (everyone, small_rows, 128)),
        ("dp", "expert"),
        0,
        0,
        tiled=True,
    ).reshape(everyone, small_rows * 128)
    router_size = dense_rows * specialist_total
    router_low = small_all[:, :router_size].reshape(width, specialist_total)
    gain_low = (
        small_all[:, router_size : router_size + 2 * dense_rows]
        .reshape(everyone, 2, dense_rows)
        .transpose(1, 0, 2)
        .reshape(2, width)
    )
    inputs_low = block_input_vectors[0]
    grad_low = output_sensitivity[0]
    grad_out = grad_low.astype(F32)
    attn_column = lax.all_gather(attn_own, "dp")
    projection_fan = fan(attn_column[:, :3])
    sequence = lax.all_gather(after(inputs_low, attn_column), "dp", axis=0, tiled=True)
    sequence, *projection_fan = lax.optimization_barrier((sequence, *projection_fan))
    expert_parts = [
        lax.all_gather(
            after(jnp.concatenate([expert_own[0], shared_own], 1), sequence), "dp"
        )
    ]
    projection_even = jnp.stack(projection_fan)
    projection_odd = swap(projection_even, 1)
    out_even, out_odd = gather_swaps(attn_column[:, 3:], sequence)
    for number in range(1, expert_local):
        expert_parts.append(
            lax.all_gather(after(expert_own[number], projection_odd), "dp")
        )
    projections = assemble(projection_even, projection_odd)
    out_low = assemble(out_even, out_odd)[0]
    grads_plane = gather_swaps(grad_low, out_even)
    shared_low = assemble(*gather_swaps(expert_parts[0][:, :, part_rows:]))
    gain_one = gain_low[0].astype(F32)
    gain_two = gain_low[1].astype(F32)

    sequence = sequence.astype(F32)

    normed_all, scaled_all, _ = norm_forward(sequence, gain_one)
    inputs = inputs_low.astype(F32)
    normed, scaled_one, inverse_one = norm_forward(inputs, gain_one)
    place = level * token_rows
    cosine_all, sine_all = rotary_tables(rotary_offsets[0], head_dim)
    starts = jnp.arange(length, dtype=jnp.int32) - rotary_offsets[0]
    query, keys, values, mixed, mixed_low = attention(
        place, normed_all, projections, cosine_all, sine_all, starts, token_rows
    )
    middle = inputs + contract(mixed_low, out_low, 1, 0)
    second, scaled_two, inverse_two = norm_forward(middle, gain_two)

    probs = jax.nn.softmax(contract(second, router_low, 1, 0), axis=-1)
    experts = jnp.arange(specialist_total, dtype=jnp.int32)
    named = jnp.any(dispatched_specialist_ids[0][:, :, None] == experts, axis=1)
    order = jnp.arange(token_rows)
    earlier = contract(
        (order[:, None] > order[None, :]).astype(BF16), named.astype(BF16), 1, 0
    )
    kept = named & (earlier < specialist_quotas.astype(F32)[None, :])
    gate = jnp.where(kept, probs, 0.0)
    to_storage = (storage_holder[:, None] == experts[None, :]).astype(F32)
    gate_stored = jnp.sum(gate[:, :, None] * to_storage[None], axis=1)
    gates_sent = gate_stored.reshape(token_rows, groups, expert_local).transpose(1, 0, 2)
    gates_received = lax.all_to_all(gates_sent, "expert", 0, 0, tiled=True)
    half = jnp.arange(groups // 2) * 2
    relative = here ^ jnp.concatenate([half + 1, half])
    gates_plane = gates_received[relative].reshape(groups * token_rows, expert_local)

    tokens = gather_swaps(second)

    gate_grads = []
    expert_sums = []
    before = None
    for number in range(expert_local):
        last = number == expert_local - 1
        gate_column = gates_plane[:, number : number + 1]
        parts = expert_pass(
            tokens, grads_plane, gate_column, expert_parts[number], part_rows, before, last
        )
        before, (gate_grad, hidden, pair) = parts[:-3], parts[-3:]
        gate_grads.append(gate_grad)
        if last:
            routed_odd, routed_even, entry_odd, entry_even = before
            entry_other = swap(entry_odd, 1)
            routed_other = swap(after(routed_odd, entry_other), 1)
            hidden = after(hidden, entry_other)
        expert_sums.append(
            lax.psum_scatter(
                expert_grad(tokens, grads_plane, gate_column, hidden, pair),
                "dp",
                scatter_dimension=1,
                tiled=True,
            ).astype(F32)
        )
    expert_sum = jnp.stack(expert_sums)

    grad_second = join_chips(join_cores(entry_even, entry_other))
    routed_even, routed_other = lax.optimization_barrier((routed_even, routed_other, grad_second))[:2]
    routed = join_chips(join_cores(routed_even, routed_other))
    mask = here ^ jnp.arange(groups)
    back = mask // 2 + jnp.where(mask % 2 == 1, 0, groups // 2)
    gate_grad_sent = jnp.concatenate(gate_grads, -1).reshape(groups, token_rows, expert_local)[back]
    gate_grad_back = lax.all_to_all(gate_grad_sent, "expert", 0, 0, tiled=True)
    gate_grad_stored = gate_grad_back.transpose(1, 0, 2).reshape(token_rows, specialist_total)
    grad_prob = jnp.sum(gate_grad_stored[:, None, :] * to_storage[None], axis=-1)
    grad_prob = jnp.where(kept, grad_prob, 0.0)

    gate_shared = contract(second, shared_low[0], 1, 0)
    up_shared = contract(second, shared_low[1], 1, 0)
    hidden_shared = (jax.nn.silu(gate_shared) * up_shared).astype(BF16)
    shared_out = contract(hidden_shared, shared_low[2], 1, 1)
    grad_hidden_shared = contract(grad_low, shared_low[2], 1, 0)
    sigma = jax.nn.sigmoid(gate_shared)
    grad_gate_shared = (
        grad_hidden_shared * up_shared * sigma * (1.0 + gate_shared * (1.0 - sigma))
    ).astype(BF16)
    grad_up_shared = (grad_hidden_shared * gate_shared * sigma).astype(BF16)
    shared_entry = contract(grad_gate_shared, shared_low[0], 1, 1) + contract(
        grad_up_shared, shared_low[1], 1, 1
    )
    block_out = (middle + shared_out + routed).astype(BF16)

    grad_logit = (probs * (grad_prob - jnp.sum(probs * grad_prob, axis=-1, keepdims=True))).astype(
        BF16
    )
    router_grad = contract(second, grad_logit, 0, 0)
    grad_second = grad_second + contract(grad_logit, router_low, 1, 1) + shared_entry
    shared_grad = jnp.stack(
        [
            contract(second, grad_gate_shared, 0, 0),
            contract(second, grad_up_shared, 0, 0),
            contract(grad_low, hidden_shared, 0, 0),
        ]
    )
    gain_two_grad = jnp.sum(grad_second * scaled_two, axis=0)
    grad_middle = norm_backward(grad_second, scaled_two, inverse_two, gain_two) + grad_out
    grad_attn_out = grad_middle.astype(BF16)
    out_grad = contract(mixed_low, grad_attn_out, 0, 0)
    projection_grad, grad_normed_all, grad_normed_own = attention_grad(
        place,
        normed_all,
        normed,
        projections,
        out_low,
        query,
        keys,
        values,
        mixed,
        after(grad_attn_out, routed_other),
        cosine_all,
        sine_all,
        starts,
    )
    gain_one_grad = jnp.sum(grad_normed_all * scaled_all, axis=0) + jnp.sum(
        grad_normed_own * scaled_one, axis=0
    )
    normed_low = grad_normed_all.astype(BF16).reshape(deep, token_rows, width)
    grad_normed = grad_normed_own + pick(
        grad_normed_all.reshape(deep, token_rows, width), level, 0
    )
    for step in range(1, deep):
        grad_normed = grad_normed + shift(pick(normed_low, (level - step) % deep, 0), -step).astype(
            F32
        )
    grad_inputs = norm_backward(grad_normed, scaled_one, inverse_one, gain_one) + grad_middle

    fill_rows = -(-(dense_rows * (specialist_total + 2)) // (8 * width)) * 8
    def by_owner(grad):
        return grad.reshape(grad.shape[0], deep, groups, dense_rows, grad.shape[-1]).transpose(
            1, 2, 0, 3, 4
        )

    small_grad = jnp.concatenate(
        [
            router_grad.reshape(deep, groups, dense_rows * specialist_total),
            jnp.stack([gain_one_grad, gain_two_grad])
            .reshape(2, deep, groups, dense_rows)
            .transpose(1, 2, 0, 3)
            .reshape(deep, groups, 2 * dense_rows),
        ],
        -1,
    )
    small_grad = jnp.pad(
        small_grad, ((0, 0), (0, 0), (0, fill_rows * width - small_grad.shape[-1]))
    ).reshape(deep, groups, fill_rows, width)
    projection_sums = scatter_dense(
        jnp.concatenate(
            [
                by_owner(projection_grad).reshape(deep, groups, 3 * dense_rows, width),
                small_grad,
            ],
            2,
        )
    )
    out_sum = scatter_dense(out_grad.reshape(deep, groups, dense_rows, width))
    shared_sum = scatter_dense(
        by_owner(shared_grad).reshape(deep, groups, 3 * dense_rows, hidden_width)
    ).reshape(3, dense_rows, hidden_width)
    attn_sum = jnp.concatenate(
        [projection_sums[: 3 * dense_rows].reshape(3, dense_rows, width), out_sum[None]], 0
    )
    small_sum = projection_sums[3 * dense_rows :].reshape(-1)
    router_sum = small_sum[: dense_rows * specialist_total].reshape(dense_rows, specialist_total)
    gain_sum = small_sum[
        dense_rows * specialist_total : dense_rows * (specialist_total + 2)
    ].reshape(2, dense_rows)

    local_squares = (
        jnp.sum(attn_sum * attn_sum)
        + jnp.sum(shared_sum * shared_sum)
        + jnp.sum(router_sum * router_sum)
        + jnp.sum(gain_sum * gain_sum)
        + jnp.sum(expert_sum * expert_sum)
    )
    spread = jnp.broadcast_to(local_squares, (everyone, 8, 128))
    squares = lax.all_to_all(spread, ("dp", "expert"), 0, 0, tiled=True)
    grad_norm = jnp.sqrt(jnp.sum(squares[:, 0, 0]))
    scale = jnp.minimum(1.0, CLIP_VALUE / (grad_norm + 1e-06))
    attn_new, attn_moment, attn_square = adam(
        mixer_projection_matrices,
        mixer_mean_estimate,
        mixer_variance_estimate,
        attn_sum,
        scale,
        RATE_MATRIX,
    )
    shared_new, shared_moment, shared_square = adam(
        common_projection_matrices,
        common_mean_estimate,
        common_variance_estimate,
        shared_sum,
        scale,
        RATE_MATRIX,
    )
    router_new, router_moment, router_square = adam(
        gating_projection_matrix,
        gating_mean_estimate,
        gating_variance_estimate,
        router_sum,
        scale,
        RATE_MATRIX,
    )
    gain_new, gain_moment, gain_square = adam(
        scaling_factors,
        scaling_mean_estimate,
        scaling_variance_estimate,
        gain_sum,
        scale,
        RATE_GAIN,
    )
    expert_new, expert_moment, expert_square = adam(
        dispatched_projection_matrices,
        dispatched_mean_estimate,
        dispatched_variance_estimate,
        expert_sum,
        scale,
        RATE_EXPERT,
    )
    return (
        block_out[None],
        grad_inputs[None],
        grad_norm,
        attn_new,
        attn_moment,
        attn_square,
        attn_new.astype(BF16),
        shared_new,
        shared_moment,
        shared_square,
        shared_new.astype(BF16),
        router_new,
        router_moment,
        router_square,
        router_new.astype(BF16),
        gain_new,
        gain_moment,
        gain_square,
        expert_new,
        expert_moment,
        expert_square,
        expert_new.astype(BF16),
    )


def solution(mesh):
    placed = (
        P("expert", "dp", None),
        P("expert", "dp", None),
        P("expert", None),
        P("expert", "dp", None),
        P(),
        P(),
        P(None, ("dp", "expert"), None),
        P(None, ("dp", "expert"), None),
        P(None, ("dp", "expert"), None),
        P(None, ("dp", "expert"), None),
        P(None, ("dp", "expert"), None),
        P(None, ("dp", "expert"), None),
        P(("dp", "expert"), None),
        P(("dp", "expert"), None),
        P(("dp", "expert"), None),
        P(None, ("dp", "expert")),
        P(None, ("dp", "expert")),
        P(None, ("dp", "expert")),
        P("expert", None, "dp", None),
        P("expert", None, "dp", None),
        P("expert", None, "dp", None),
    )
    return jax.shard_map(
        body,
        mesh=mesh,
        in_specs=placed,
        out_specs=(
            P("expert", "dp", None),
            P("expert", "dp", None),
            P(),
            P(None, ("dp", "expert"), None),
            P(None, ("dp", "expert"), None),
            P(None, ("dp", "expert"), None),
            P(None, ("dp", "expert"), None),
            P(None, ("dp", "expert"), None),
            P(None, ("dp", "expert"), None),
            P(None, ("dp", "expert"), None),
            P(None, ("dp", "expert"), None),
            P(("dp", "expert"), None),
            P(("dp", "expert"), None),
            P(("dp", "expert"), None),
            P(("dp", "expert"), None),
            P(None, ("dp", "expert")),
            P(None, ("dp", "expert")),
            P(None, ("dp", "expert")),
            P("expert", None, "dp", None),
            P("expert", None, "dp", None),
            P("expert", None, "dp", None),
            P("expert", None, "dp", None),
        ),
        check_vma=False,
    )
```

time: 1360 us -> 915 us (0.67)
  matrix products: 259 us -> 23.3 us
  Pallas kernels: 0 us -> 214 us
  waiting for transfers between devices: 592 us -> 392 us
  local copies, waits for them, and re-layouts: 181 us -> 67.4 us
  starting transfers between devices: 148 us -> 69.7 us
  other arithmetic: 157 us -> 123 us
    ppermute x20 -> x0, waiting for transfers between devices: 309 us -> none  [send(): return lax.ppermute(value, 'dp', pairs)]
    pallas_call x0 -> x9, Pallas kernels: none -> 214 us  [the longest x2 92.1 us: expert_pass(): pl.pallas_call(functools.partial(expert_kernel, before is not None, split...]
    dot_general x43 -> x15, matrix products: 234 us -> 23.3 us  [contract(): lax.dot_general(left, right, (((left_dim,), (right_dim,)), ((), ())), pre...]
    ppermute x6 -> x3, waiting for transfers between devices: 29.3 us -> 93.1 us  [shift(): lax.ppermute(value, 'dp', [(i, i + step) for i in range(size) if 0 <= i +...]
    all_gather x0 -> x4, waiting for transfers between devices: none -> 60.5 us  [the longest x1 41.8 us: body(): attn_column = lax.all_gather(attn_own, 'dp')]
    ppermute x20 -> x0, starting transfers between devices: 46 us -> none  [send(): return lax.ppermute(value, 'dp', pairs)]
    ppermute x18 -> x9, waiting for transfers between devices: 53 us -> 15.6 us  [rotate(): lax.ppermute(value, 'dp', [(i, (i + step) % size) for i in range(size)])]
    dynamic_update_slice x42 -> x0, local copies, waits for them, and re-layouts: 34.6 us -> none  [put(): lax.dynamic_update_slice_in_dim(buffer, jnp.expand_dims(block, axis), ind...]
  transfers between devices with their start and end apart: 102 -> 62, of which waited for: 35 -> 27; matrix products, arithmetic and copies ran while one was open for 40% -> 19% of each run, Pallas kernels for 0% -> 24%
where the time goes in v2:
time: 915 us; the launch traced here: 911 us
  waiting for transfers between devices  392 us (43%)
  Pallas kernels  214 us (23%)
  other arithmetic  123 us (13%)
  starting transfers between devices  69.7 us (8%)
  local copies, waits for them, and re-layouts  67.4 us (7%)
  matrix products  23.3 us (3%)
  between operations  20.8 us (2%)
    ppermute x40, waiting for transfers between devices, swap(): return lax.ppermute(value, 'expert', [(i, i ^ mask) for i in range(size)])  215 us
    ppermute x3, waiting for transfers between devices, shift(): lax.ppermute(value, 'dp', [(i, i + step) for i in range(size) if 0 <= i +...  93.1 us
    pallas_call x2, Pallas kernels, expert_pass(): pl.pallas_call(functools.partial(expert_kernel, before is not None, split...  92.1 us
    pallas_call x2, Pallas kernels, expert_grad(): pl.pallas_call(expert_grad_kernel, grid=(width // span,), in_specs=[stack...  45.4 us
    all_gather x1, waiting for transfers between devices, body(): attn_column = lax.all_gather(attn_own, 'dp')  41.8 us
    pallas_call x1, Pallas kernels, attention_grad(): pl.pallas_call(attention_grad_kernel, grid_spec=pltpu.PrefetchScalarGridS...  38.9 us
    ppermute x40, starting transfers between devices, swap(): return lax.ppermute(value, 'expert', [(i, i ^ mask) for i in range(size)])  37.2 us
    dot_general x15, matrix products, contract(): lax.dot_general(left, right, (((left_dim,), (right_dim,)), ((), ())), pre...  23.3 us
  transfers between devices with their start and end apart: 62, of which 27 were waited for; matrix products, arithmetic and copies ran while one was open for 19% of the time, Pallas kernels for 24%

profile of v2, /device:TPU:0, one launch (start us, length us, event | category | flops | bytes accessed | tf_op | source)
XLA Modules:
  0.0 910.7 jit_solution(5825308947686214164)
XLA Ops:
  9.3 41.8 %all-gather.10.cloned.1.call-done = bf16[16,40,1280]{2,1,0:T(8,128)(2,1)} async-done(((bf16[4,40,1280]{2,1,0:T(8,128)(2,1)}), bf16[16,40,1280]{2,1,0:T(8,128)(2,1)}) %all-gather.10.cloned.1.call-update) | async-done | bytes 1638416 | tf_op jit(solution)/shard_map/all_gather | solution.py:606
  56.1 3.7 convert_element_type.395
  62.7 19.8 %collective-permute-done = bf16[4,3,40,1280]{3,2,1,0:T(8,128)(2,1)S(1)} collective-permute-done((bf16[4,3,40,1280]{3,2,1,0:T(8,128)(2,1)S(1)}, bf16[4,3,40,1280]{3,2,1,0:T(8,128)(2,1)S(1)}, u32[]{:S(2)}, u32[]{:S(2)}) %collective-permute-start) | collective-permute-done | bytes 1228832 | tf_op jit(solution)/shard_map/ppermute | solution.py:71
  82.5 26.4 %collective-permute-done.1 = bf16[4,3,40,1280]{3,2,1,0:T(8,128)(2,1)} collective-permute-done((bf16[4,3,40,1280]{3,2,1,0:T(8,128)(2,1)S(1)}, bf16[4,3,40,1280]{3,2,1,0:T(8,128)(2,1)}, u32[]{:S(2)}, u32[]{:S(2)}) %collective-permute-start.1) | collective-permute-done | bytes 1228832 | tf_op jit(solution)/shard_map/ppermute | solution.py:71
  109.0 4.5 pad_maximum_fusion.even
  125.3 6.3 collective-permute-done.4
  131.6 9.5 %collective-permute-done.5 = bf16[4,1,40,1280]{3,2,0,1:T(8,128)(2,1)S(1)} collective-permute-done((bf16[4,1,40,1280]{3,2,0,1:T(8,128)(2,1)S(1)}, bf16[4,1,40,1280]{3,2,0,1:T(8,128)(2,1)S(1)}, u32[]{:S(2)}, u32[]{:S(2)}) %collective-permute-start.5) | collective-permute-done | bytes 409632 | tf_op jit(solution)/shard_map/ppermute | solution.py:71
  147.2 4.0 fusion.8.normed
  154.7 4.2 assemble.4
  158.9 7.8 assemble.3
  166.7 19.6 %attention_forward.1 = (bf16[256,1280]{1,0:T(8,128)(2,1)}, bf16[1024,1280]{1,0:T(8,128)(2,1)}, bf16[1024,1280]{1,0:T(8,128)(2,1)}, f32[256,1280]{1,0:T(8,128)}, bf16[256,1280]{1,0:T(8,128)(2,1)}) custom-call(s32[1]{0:T(128)} %bitcast.1.place_ref, bf16[1024,1280]{1,0:T(8,128)(2,1)} %fusion.8.normed, bf16[3,1280,1280]{2,1,0:T(8,128)(2,1)} %bitcast.285, ...), custom_call_target="tpu_custom_call" | custom-call | flops 8891924480 | bytes 22937600 | tf_op jit(solution)/shard_map/attention_forward/pallas_call | solution.py:235
  196.8 10.7 %collective-permute-done.12 = bf16[256,1280]{1,0:T(8,128)(2,1)S(1)} collective-permute-done((bf16[256,1280]{1,0:T(8,128)(2,1)S(1)}, bf16[256,1280]{1,0:T(8,128)(2,1)S(1)}, u32[]{:S(2)}, u32[]{:S(2)}) %collective-permute-start.12) | collective-permute-done | bytes 655392 | tf_op jit(solution)/shard_map/ppermute | solution.py:71
  207.5 12.0 %collective-permute-done.13 = bf16[256,1280]{1,0:T(8,128)(2,1)S(1)} collective-permute-done((bf16[256,1280]{1,0:T(8,128)(2,1)S(1)}, bf16[256,1280]{1,0:T(8,128)(2,1)S(1)}, u32[]{:S(2)}, u32[]{:S(2)}) %collective-permute-start.13) | collective-permute-done | bytes 655392 | tf_op jit(solution)/shard_map/ppermute | solution.py:71
  230.0 4.4 all-to-all-done.1
  239.7 7.9 all-gather.12.cloned.1.call-done
  247.7 44.3 %expert_pass.2 = (f32[2048,1280]{1,0:T(8,128)}, f32[2048,1280]{1,0:T(8,128)}, f32[2048,1]{1,0:T(8,128)}, bf16[2048,896]{1,0:T(8,128)(2,1)}, bf16[2048,1792]{1,0:T(8,128)(2,1)}) custom-call(bf16[4,256,1280]{2,1,0:T(8,128)(2,1)} %collective-permute-done.15.refs_0_.odd_n, bf16[4,256,1280]{2,1,0:T(8,128)(2,1)} %pad_maximum_fusion.3.refs_1_.even_n, ...), custom_call_target="tpu_custom_call" | custom-call | flops 28185722880 | bytes 38862848 | tf_op jit(solution)/shard_map/expert_pass/pallas_call | solution.py:476
  292.0 22.5 %expert_weight_grad.2 = bf16[3,1280,896]{2,1,0:T(8,128)(2,1)} custom-call(bf16[4,256,1280]{2,1,0:T(8,128)(2,1)} %collective-permute-done.15.refs_0_.odd_n, bf16[4,256,1280]{2,1,0:T(8,128)(2,1)} %pad_maximum_fusion.3.refs_1_.even_n, bf16[4,256,1280]{2,1,0:T(8,128)(2,1)} %collective-permute-done.19.refs_2_.odd_c, ...), custom_call_target="tpu_custom_call" | custom-call | flops 14092861440 | bytes 32047104 | tf_op jit(solution)/shard_map/expert_weight_grad/pallas_call | solution.py:521
  325.6 13.8 %collective-permute-done.8 = bf16[4,3,40,896]{3,2,1,0:T(8,128)(2,1)} collective-permute-done((bf16[4,3,40,896]{3,2,1,0:T(8,128)(2,1)}, bf16[4,3,40,896]{3,2,1,0:T(8,128)(2,1)}, u32[]{:S(2)}, u32[]{:S(2)}) %collective-permute-start.8) | collective-permute-done | bytes 860192 | tf_op jit(solution)/shard_map/ppermute | solution.py:71
  339.4 18.7 %collective-permute-done.9 = bf16[4,3,40,896]{3,2,1,0:T(8,128)(2,1)} collective-permute-done((bf16[4,3,40,896]{3,2,1,0:T(8,128)(2,1)}, bf16[4,3,40,896]{3,2,1,0:T(8,128)(2,1)}, u32[]{:S(2)}, u32[]{:S(2)}) %collective-permute-start.9) | collective-permute-done | bytes 860192 | tf_op jit(solution)/shard_map/ppermute | solution.py:71
  361.5 10.7 %all-gather.14.cloned.1.call-done = bf16[12,320,896]{2,1,0:T(8,128)(2,1)} async-done(((bf16[3,320,896]{2,1,0:T(8,128)(2,1)}), bf16[12,320,896]{2,1,0:T(8,128)(2,1)}) %all-gather.14.cloned.1.call-update) | async-done | bytes 6881296 | tf_op jit(solution)/shard_map/all_gather | solution.py:620
  372.3 47.8 %expert_pass.3 = (bf16[4,256,1280]{2,1,0:T(8,128)(2,1)}, bf16[4,256,1280]{2,1,0:T(8,128)(2,1)}, bf16[4,256,1280]{2,1,0:T(8,128)(2,1)}, bf16[4,256,1280]{2,1,0:T(...) custom-call(bf16[4,256,1280]{2,1,0:T(8,128)(2,1)} %collective-permute-done.15.refs_0_.odd_n, ...), custom_call_target="tpu_custom_call" | custom-call | flops 28185722880 | bytes 38862848 | tf_op jit(solution)/shard_map/expert_pass/pallas_call | solution.py:476
  426.5 3.9 fusion.136
  430.4 4.7 copy.201.turned_normed
  436.5 6.2 assemble.5
  442.7 3.7 fusion.104
  454.2 4.3 copy.207
  473.3 22.9 %expert_weight_grad.3 = bf16[3,1280,896]{2,1,0:T(8,128)(2,1)} custom-call(bf16[4,256,1280]{2,1,0:T(8,128)(2,1)} %collective-permute-done.15.refs_0_.odd_n, bf16[4,256,1280]{2,1,0:T(8,128)(2,1)} %pad_maximum_fusion.3.refs_1_.even_n, bf16[4,256,1280]{2,1,0:T(8,128)(2,1)} %collective-permute-done.19.refs_2_.odd_c, ...), custom_call_target="tpu_custom_call" | custom-call | flops 14092861440 | bytes 32047104 | tf_op jit(solution)/shard_map/expert_weight_grad/pallas_call | solution.py:521
  496.3 6.2 collective-permute-done.23
  507.6 38.9 %attention_backward.1 = (bf16[3,1280,1280]{2,1,0:T(8,128)(2,1)}, f32[1024,1280]{1,0:T(8,128)}, f32[256,1280]{1,0:T(8,128)}) custom-call(s32[1]{0:T(128)} %bitcast.1.place_ref, bf16[1280,1024]{1,0:T(8,128)(2,1)} %copy.201.turned_normed, bf16[1280,256]{1,0:T(8,128)(2,1)} %copy.202.own_turned, bf16[3,1280,1280]{2,1,0:T(8,128)(2,1)} %bitcast.288, ...), custom_call_target="tpu_custom_call" | custom-call | flops 18454937600 | bytes 41287680 | tf_op jit(solution)/shard_map/attention_backward/pallas_call | solution.py:320
  546.6 5.3 fusion.9
  568.4 8.4 copy.204
  576.9 19.2 %collective-permute-done.28 = bf16[256,1280]{1,0:T(8,128)(2,1)} collective-permute-done((bf16[256,1280]{1,0:T(8,128)(2,1)}, bf16[256,1280]{1,0:T(8,128)(2,1)}, u32[]{:S(2)}, u32[]{:S(2)}) %collective-permute-start.28) | collective-permute-done | bytes 655392 | tf_op jit(solution)/shard_map/ppermute | solution.py:81
  596.1 73.9 %collective-permute-done.29 = bf16[256,1280]{1,0:T(8,128)(2,1)} collective-permute-done((bf16[256,1280]{1,0:T(8,128)(2,1)}, bf16[256,1280]{1,0:T(8,128)(2,1)}, u32[]{:S(2)}, u32[]{:S(2)}) %collective-permute-start.29) | collective-permute-done | bytes 655392 | tf_op jit(solution)/shard_map/ppermute | solution.py:81
  674.0 5.5 fusion.12
  684.1 3.9 fusion.5
  698.2 14.7 %collective-permute-done.46 = bf16[4,120,896]{2,1,0:T(8,128)(2,1)} collective-permute-done((bf16[4,120,896]{2,1,0:T(8,128)(2,1)}, bf16[4,120,896]{2,1,0:T(8,128)(2,1)}, u32[]{:S(2)}, u32[]{:S(2)}) %collective-permute-start.46) | collective-permute-done | bytes 860192 | tf_op jit(solution)/shard_map/ppermute | solution.py:71
  714.3 17.4 %collective-permute-done.47 = bf16[4,120,896]{2,1,0:T(8,128)(2,1)} collective-permute-done((bf16[4,120,896]{2,1,0:T(8,128)(2,1)}, bf16[4,120,896]{2,1,0:T(8,128)(2,1)}, u32[]{:S(2)}, u32[]{:S(2)}) %collective-permute-start.47) | collective-permute-done | bytes 860192 | tf_op jit(solution)/shard_map/ppermute | solution.py:71
  736.2 3.8 collective-permute-done.39
  740.0 9.1 %collective-permute-done.40 = bf16[4,40,1280]{2,1,0:T(8,128)(2,1)S(1)} collective-permute-done((bf16[4,40,1280]{2,1,0:T(8,128)(2,1)S(1)}, bf16[4,40,1280]{2,1,0:T(8,128)(2,1)S(1)}, u32[]{:S(2)}, u32[]{:S(2)}) %collective-permute-start.40) | collective-permute-done | bytes 409632 | tf_op jit(solution)/shard_map/ppermute | solution.py:71
  753.0 6.3 fusion
  777.8 15.8 %collective-permute-done.32 = bf16[4,128,1280]{2,1,0:T(8,128)(2,1)S(1)} collective-permute-done((bf16[4,128,1280]{2,1,0:T(8,128)(2,1)S(1)}, bf16[4,128,1280]{2,1,0:T(8,128)(2,1)S(1)}, u32[]{:S(2)}, u32[]{:S(2)}) %collective-permute-start.32) | collective-permute-done | bytes 1310752 | tf_op jit(solution)/shard_map/ppermute | solution.py:71
  793.6 27.5 %collective-permute-done.33 = bf16[4,128,1280]{2,1,0:T(8,128)(2,1)S(1)} collective-permute-done((bf16[4,128,1280]{2,1,0:T(8,128)(2,1)S(1)}, bf16[4,128,1280]{2,1,0:T(8,128)(2,1)S(1)}, u32[]{:S(2)}, u32[]{:S(2)}) %collective-permute-start.33) | collective-permute-done | bytes 1310752 | tf_op jit(solution)/shard_map/ppermute | solution.py:71
  830.4 7.0 collective-permute-done.35
  839.4 6.7 collective-permute-done.36
  851.4 4.4 fusion.3
  857.0 9.2 %all-to-all-start.3 = ((f32[32,8,128]{2,1,0:T(8,128)}), f32[32,8,128]{2,1,0:T(8,128)}, u32[]{:S(2)}, u32[]{:S(2)}) async-start(f32[32,8,128]{2,1,0:T(8,128)} %broadcast_in_dim.36), calls=%async_computation.5 | async-start | bytes 262144 | tf_op jit(solution)/shard_map/all_to_all | solution.py:807
  866.3 4.5 fusion.22
  876.9 18.8 %fusion.87 = (bf16[2,3,320,896]{3,2,1,0:T(8,128)(2,1)}, f32[2,3,320,896]{3,2,1,0:T(8,128)}, f32[2,3,320,896]{3,2,1,0:T(8,128)}, f32[2,3,320,896]{3,2,1,0:T(8,128)}) fusion(f32[2,3,320,896]{3,2,1,0:T(8,128)} %param.39, f32[]{:T(128)S(6)} %min.3, bf16[1,3,320,896]{3,2,1,0:T(8,128)(2,1)} %bitcast.320, bf16[1,3,320,896]{3,2,1,0:T(8,128)(2,1)S(1)} %bitcast.318, ...), kind=kLoop, calls=%fused_computation.238 | loop fusion | flops 32686080 | bytes 48168964 | tf_op jit(solution)/shard_map/convert_element_type | solution.py:872
  (365 shorter events, 197.4 us)
Async XLA Ops:
  7.2 43.9 %all-gather.10.cloned.1.call-start = ((), (), s32[]{:S(2)}) async-start(), calls=%async_computation.9 | async-start | bytes 2048000 | tf_op jit(solution)/shard_map/all_gather | solution.py:606
  9.2 99.7 %all-gather.8.cloned.1.call-start = ((), (), s32[]{:S(2)}) async-start(), calls=%async_computation.6 | async-start | bytes 3276800 | tf_op jit(solution)/shard_map/all_gather | solution.py:608
  51.1 196.6 %all-gather.12.cloned.1.call-start = ((), (), s32[]{:S(2)}) async-start(), calls=%async_computation.10 | async-start | bytes 9676800 | tf_op jit(solution)/shard_map/all_gather | solution.py:611
  52.5 30.0 %collective-permute-start = (bf16[4,3,40,1280]{3,2,1,0:T(8,128)(2,1)S(1)}, bf16[4,3,40,1280]{3,2,1,0:T(8,128)(2,1)S(1)}, u32[]{:S(2)}, u32[]{:S(2)}) collective-permute-start(bf16[4,3,40,1280]{3,2,1,0:T(8,128)(2,1)S(1)} %slice.160), channel_id=1, source_target_pairs={{0,2},{1,3},{2,0},{3,1},{4,6},{5,7},{6,4},{7,5},{8,10},{9,11},{10,... | collective-permute-start | bytes 3686408 | tf_op jit(solution)/shard_map/ppermute | solution.py:71
  54.1 54.9 %collective-permute-start.1 = (bf16[4,3,40,1280]{3,2,1,0:T(8,128)(2,1)S(1)}, bf16[4,3,40,1280]{3,2,1,0:T(8,128)(2,1)}, u32[]{:S(2)}, u32[]{:S(2)}) collective-permute-start(bf16[4,3,40,1280]{3,2,1,0:T(8,128)(2,1)S(1)} %slice.160), channel_id=1, source_target_pairs={{0,4},{1,5},{2,6},{3,7},{4,0},{5,1},{6,2},{7,3},{8,12},{9,13},{10,... | collective-permute-start | bytes 3686408 | tf_op jit(solution)/shard_map/ppermute | solution.py:71
  55.5 53.4 %collective-permute-start.2 = (bf16[4,3,40,1280]{3,2,1,0:T(8,128)(2,1)S(1)}, bf16[4,3,40,1280]{3,2,1,0:T(8,128)(2,1)}, u32[]{:S(2)}, u32[]{:S(2)}) collective-permute-start(bf16[4,3,40,1280]{3,2,1,0:T(8,128)(2,1)S(1)} %slice.160), channel_id=1, source_target_pairs={{0,6},{1,7},{2,4},{3,5},{4,2},{5,3},{6,0},{7,1},{8,14},{9,15},{10,... | collective-permute-start | bytes 3686408 | tf_op jit(solution)/shard_map/ppermute | solution.py:71
  113.5 33.7 %collective-permute-start.3 = (bf16[4,4,3,40,1280]{4,3,2,1,0:T(8,128)(2,1)}, bf16[4,4,3,40,1280]{4,3,2,1,0:T(8,128)(2,1)}, u32[]{:S(2)}, u32[]{:S(2)}) collective-permute-start(bf16[4,4,3,40,1280]{4,3,2,1,0:T(8,128)(2,1)} %pad_maximum_fusion.even), channel_id=1, source_target_pairs={{0,1},{1,0},{2,3},{3,2},{4,5},{5,4},{6,7},{7,6},{8,9},{9,8},{10,11... | collective-permute-start | bytes 14745608 | tf_op jit(solution)/shard_map/ppermute | solution.py:71
  114.4 30.0 %all-to-all-start = ((bf16[32,8,128]{2,1,0:T(8,128)(2,1)}), bf16[32,8,128]{2,1,0:T(8,128)(2,1)S(1)}, u32[]{:S(2)}, u32[]{:S(2)}) async-start(bf16[32,8,128]{2,1,0:T(8,128)(2,1)} %broadcast_in_dim.26), calls=%async_computation | async-start | bytes 131072 | tf_op jit(solution)/shard_map/all_to_all | solution.py:588
  117.3 255.0 %all-gather.14.cloned.1.call-start = ((), (), s32[]{:S(2)}) async-start(), calls=%async_computation.11 | async-start | bytes 8601600 | tf_op jit(solution)/shard_map/all_gather | solution.py:620
  120.8 20.3 %collective-permute-start.5 = (bf16[4,1,40,1280]{3,2,0,1:T(8,128)(2,1)S(1)}, bf16[4,1,40,1280]{3,2,0,1:T(8,128)(2,1)S(1)}, u32[]{:S(2)}, u32[]{:S(2)}) collective-permute-start(bf16[4,1,40,1280]{3,2,0,1:T(8,128)(2,1)S(1)} %slice_bitcast_fusion.2), channel_id=1, source_target_pairs={{0,4},{1,5},{2,6},{3,7},{4,0},{5,1},{6,2},{7,3},{8,12},{9,13},{10,... | collective-permute-start | bytes 1228808 | tf_op jit(solution)/shard_map/ppermute | solution.py:71
  122.2 18.8 %collective-permute-start.6 = (bf16[4,1,40,1280]{3,2,0,1:T(8,128)(2,1)S(1)}, bf16[4,1,40,1280]{3,2,0,1:T(8,128)(2,1)S(1)}, u32[]{:S(2)}, u32[]{:S(2)}) collective-permute-start(bf16[4,1,40,1280]{3,2,0,1:T(8,128)(2,1)S(1)} %slice_bitcast_fusion.2), channel_id=1, source_target_pairs={{0,6},{1,7},{2,4},{3,5},{4,2},{5,3},{6,0},{7,1},{8,14},{9,15},{10,... | collective-permute-start | bytes 1228808 | tf_op jit(solution)/shard_map/ppermute | solution.py:71
  151.2 40.7 %collective-permute-start.16 = (bf16[256,1280]{1,0:T(8,128)(2,1)S(1)}, bf16[256,1280]{1,0:T(8,128)(2,1)}, u32[]{:S(2)}, u32[]{:S(2)}) collective-permute-start(bf16[256,1280]{1,0:T(8,128)(2,1)S(1)} %bitcast.301), channel_id=1, source_target_pairs={{0,2},{1,3},{2,0},{3,1},{4,6},{5,7},{6,4},{7,5},{8,10},{9,11},{10,... | collective-permute-start | bytes 1966088 | tf_op jit(solution)/shard_map/ppermute | solution.py:71
  152.4 41.0 %collective-permute-start.17 = (bf16[256,1280]{1,0:T(8,128)(2,1)S(1)}, bf16[256,1280]{1,0:T(8,128)(2,1)}, u32[]{:S(2)}, u32[]{:S(2)}) collective-permute-start(bf16[256,1280]{1,0:T(8,128)(2,1)S(1)} %bitcast.302), channel_id=1, source_target_pairs={{0,4},{1,5},{2,6},{3,7},{4,0},{5,1},{6,2},{7,3},{8,12},{9,13},{10,... | collective-permute-start | bytes 1966088 | tf_op jit(solution)/shard_map/ppermute | solution.py:71
  153.2 40.2 %collective-permute-start.18 = (bf16[256,1280]{1,0:T(8,128)(2,1)S(1)}, bf16[256,1280]{1,0:T(8,128)(2,1)}, u32[]{:S(2)}, u32[]{:S(2)}) collective-permute-start(bf16[256,1280]{1,0:T(8,128)(2,1)S(1)} %bitcast.303), channel_id=1, source_target_pairs={{0,6},{1,7},{2,4},{3,5},{4,2},{5,3},{6,0},{7,1},{8,14},{9,15},{10,... | collective-permute-start | bytes 1966088 | tf_op jit(solution)/shard_map/ppermute | solution.py:71
  191.0 28.4 %collective-permute-start.13 = (bf16[256,1280]{1,0:T(8,128)(2,1)S(1)}, bf16[256,1280]{1,0:T(8,128)(2,1)S(1)}, u32[]{:S(2)}, u32[]{:S(2)}) collective-permute-start(bf16[256,1280]{1,0:T(8,128)(2,1)S(1)} %multiply_convert_fusion), channel_id=1, source_target_pairs={{0,4},{1,5},{2,6},{3,7},{4,0},{5,1},{6,2},{7,3},{8,12},{9,13},{10,... | collective-permute-start | bytes 1966088 | tf_op jit(solution)/shard_map/ppermute | solution.py:71
  191.8 29.2 %collective-permute-start.14 = (bf16[256,1280]{1,0:T(8,128)(2,1)S(1)}, bf16[256,1280]{1,0:T(8,128)(2,1)S(1)}, u32[]{:S(2)}, u32[]{:S(2)}) collective-permute-start(bf16[256,1280]{1,0:T(8,128)(2,1)S(1)} %multiply_convert_fusion), channel_id=1, source_target_pairs={{0,6},{1,7},{2,4},{3,5},{4,2},{5,3},{6,0},{7,1},{8,14},{9,15},{10,... | collective-permute-start | bytes 1966088 | tf_op jit(solution)/shard_map/ppermute | solution.py:71
  196.6 43.1 %collective-permute-start.19 = (bf16[4,256,1280]{2,1,0:T(8,128)(2,1)}, bf16[4,256,1280]{2,1,0:T(8,128)(2,1)}, u32[]{:S(2)}, u32[]{:S(2)}) collective-permute-start(bf16[4,256,1280]{2,1,0:T(8,128)(2,1)} %pad_maximum_fusion.4.refs_3_.even_c), channel_id=1, source_target_pairs={{0,1},{1,0},{2,3},{3,2},{4,5},{5,4},{6,7},{7,6},{8,9},{9,8},{10,11... | collective-permute-start | bytes 7864328 | tf_op jit(solution)/shard_map/ppermute | solution.py:71
  229.8 621.5 %reduce-scatter.3.cloned.1.call-start = ((), (), s32[]{:S(2)}) async-start(), calls=%async_computation.7 | async-start | bytes 8601600 | tf_op jit(solution)/shard_map/reduce_scatter | solution.py:679
  317.1 22.3 %collective-permute-start.8 = (bf16[4,3,40,896]{3,2,1,0:T(8,128)(2,1)}, bf16[4,3,40,896]{3,2,1,0:T(8,128)(2,1)}, u32[]{:S(2)}, u32[]{:S(2)}) collective-permute-start(bf16[4,3,40,896]{3,2,1,0:T(8,128)(2,1)} %get-tuple-element.235), channel_id=1, source_target_pairs={{0,2},{1,3},{2,0},{3,1},{4,6},{5,7},{6,4},{7,5},{8,10},{9,11},{10,... | collective-permute-start | bytes 2580488 | tf_op jit(solution)/shard_map/ppermute | solution.py:71
  318.6 39.6 %collective-permute-start.9 = (bf16[4,3,40,896]{3,2,1,0:T(8,128)(2,1)}, bf16[4,3,40,896]{3,2,1,0:T(8,128)(2,1)}, u32[]{:S(2)}, u32[]{:S(2)}) collective-permute-start(bf16[4,3,40,896]{3,2,1,0:T(8,128)(2,1)} %get-tuple-element.235), channel_id=1, source_target_pairs={{0,4},{1,5},{2,6},{3,7},{4,0},{5,1},{6,2},{7,3},{8,12},{9,13},{10,... | collective-permute-start | bytes 2580488 | tf_op jit(solution)/shard_map/ppermute | solution.py:71
  320.1 38.1 %collective-permute-start.10 = (bf16[4,3,40,896]{3,2,1,0:T(8,128)(2,1)}, bf16[4,3,40,896]{3,2,1,0:T(8,128)(2,1)}, u32[]{:S(2)}, u32[]{:S(2)}) collective-permute-start(bf16[4,3,40,896]{3,2,1,0:T(8,128)(2,1)} %get-tuple-element.235), channel_id=1, source_target_pairs={{0,6},{1,7},{2,4},{3,5},{4,2},{5,3},{6,0},{7,1},{8,14},{9,15},{10,... | collective-permute-start | bytes 2580488 | tf_op jit(solution)/shard_map/ppermute | solution.py:71
  361.5 74.9 %collective-permute-start.11 = (bf16[4,4,3,40,896]{4,3,2,1,0:T(8,128)(2,1)}, bf16[4,4,3,40,896]{4,3,2,1,0:T(8,128)(2,1)}, u32[]{:S(2)}, u32[]{:S(2)}) collective-permute-start(bf16[4,4,3,40,896]{4,3,2,1,0:T(8,128)(2,1)} %pad_maximum_fusion.1.even), channel_id=1, source_target_pairs={{0,1},{1,0},{2,3},{3,2},{4,5},{5,4},{6,7},{7,6},{8,9},{9,8},{10,11... | collective-permute-start | bytes 10321928 | tf_op jit(solution)/shard_map/ppermute | solution.py:71
  426.5 424.9 %reduce-scatter.5.cloned.1.call-start = ((), (), s32[]{:S(2)}) async-start(), calls=%async_computation.8 | async-start | bytes 8601600 | tf_op jit(solution)/shard_map/reduce_scatter | solution.py:679
  435.1 30.6 %collective-permute-start.20 = (bf16[4,256,1280]{2,1,0:T(8,128)(2,1)}, bf16[4,256,1280]{2,1,0:T(8,128)(2,1)}, u32[]{:S(2)}, u32[]{:S(2)}) collective-permute-start(bf16[4,256,1280]{2,1,0:T(8,128)(2,1)} %get-tuple-element.72), channel_id=1, source_target_pairs={{0,1},{1,0},{2,3},{3,2},{4,5},{5,4},{6,7},{7,6},{8,9},{9,8},{10,11... | collective-permute-start | bytes 7864328 | tf_op jit(solution)/shard_map/ppermute | solution.py:71
  469.8 26.5 %collective-permute-start.22 = (bf16[256,1280]{1,0:T(8,128)(2,1)}, bf16[256,1280]{1,0:T(8,128)(2,1)}, u32[]{:S(2)}, u32[]{:S(2)}) collective-permute-start(bf16[256,1280]{1,0:T(8,128)(2,1)} %get-tuple-element.247), channel_id=1, source_target_pairs={{0,2},{1,3},{2,0},{3,1},{4,6},{5,7},{6,4},{7,5},{8,10},{9,11},{10,... | collective-permute-start | bytes 1966088 | tf_op jit(solution)/shard_map/ppermute | solution.py:71
  471.4 31.0 %collective-permute-start.23 = (bf16[256,1280]{1,0:T(8,128)(2,1)}, bf16[256,1280]{1,0:T(8,128)(2,1)}, u32[]{:S(2)}, u32[]{:S(2)}) collective-permute-start(bf16[256,1280]{1,0:T(8,128)(2,1)} %get-tuple-element.249), channel_id=1, source_target_pairs={{0,4},{1,5},{2,6},{3,7},{4,0},{5,1},{6,2},{7,3},{8,12},{9,13},{10,... | collective-permute-start | bytes 1966088 | tf_op jit(solution)/shard_map/ppermute | solution.py:71
  472.9 29.5 %collective-permute-start.24 = (bf16[256,1280]{1,0:T(8,128)(2,1)}, bf16[256,1280]{1,0:T(8,128)(2,1)}, u32[]{:S(2)}, u32[]{:S(2)}) collective-permute-start(bf16[256,1280]{1,0:T(8,128)(2,1)} %get-tuple-element.248), channel_id=1, source_target_pairs={{0,6},{1,7},{2,4},{3,5},{4,2},{5,3},{6,0},{7,1},{8,14},{9,15},{10,... | collective-permute-start | bytes 1966088 | tf_op jit(solution)/shard_map/ppermute | solution.py:71
  473.3 34.3 %collective-permute-start.21 = (bf16[4,256,1280]{2,1,0:T(8,128)(2,1)}, bf16[4,256,1280]{2,1,0:T(8,128)(2,1)}, u32[]{:S(2)}, u32[]{:S(2)}) collective-permute-start(bf16[4,256,1280]{2,1,0:T(8,128)(2,1)} %get-tuple-element.73), channel_id=1, source_target_pairs={{0,1},{1,0},{2,3},{3,2},{4,5},{5,4},{6,7},{7,6},{8,9},{9,8},{10,11... | collective-permute-start | bytes 7864328 | tf_op jit(solution)/shard_map/ppermute | solution.py:71
  553.2 42.9 %collective-permute-start.28 = (bf16[256,1280]{1,0:T(8,128)(2,1)}, bf16[256,1280]{1,0:T(8,128)(2,1)}, u32[]{:S(2)}, u32[]{:S(2)}) collective-permute-start(bf16[256,1280]{1,0:T(8,128)(2,1)} %get-tuple-element.255), channel_id=1, source_target_pairs={{8,0},{16,8},{24,16},{9,1},{17,9},{25,17},{10,2},{18,10},{26,18},{... | collective-permute-start | bytes 1966088 | tf_op jit(solution)/shard_map/ppermute | solution.py:81
  554.7 115.3 %collective-permute-start.29 = (bf16[256,1280]{1,0:T(8,128)(2,1)}, bf16[256,1280]{1,0:T(8,128)(2,1)}, u32[]{:S(2)}, u32[]{:S(2)}) collective-permute-start(bf16[256,1280]{1,0:T(8,128)(2,1)} %get-tuple-element.257), channel_id=1, source_target_pairs={{16,0},{24,8},{17,1},{25,9},{18,2},{26,10},{19,3},{27,11},{20,4},{... | collective-permute-start | bytes 1966088 | tf_op jit(solution)/shard_map/ppermute | solution.py:81
  556.0 114.0 %collective-permute-start.30 = (bf16[256,1280]{1,0:T(8,128)(2,1)}, bf16[256,1280]{1,0:T(8,128)(2,1)}, u32[]{:S(2)}, u32[]{:S(2)}) collective-permute-start(bf16[256,1280]{1,0:T(8,128)(2,1)} %get-tuple-element.256), channel_id=1, source_target_pairs={{24,0},{25,1},{26,2},{27,3},{28,4},{29,5},{30,6},{31,7}} | collective-permute-start | bytes 1966088 | tf_op jit(solution)/shard_map/ppermute | solution.py:81
  568.3 115.8 %collective-permute-start.45 = (bf16[4,4,120,896]{3,2,1,0:T(8,128)(2,1)}, bf16[4,4,120,896]{3,2,1,0:T(8,128)(2,1)}, u32[]{:S(2)}, u32[]{:S(2)}) collective-permute-start(bf16[4,4,120,896]{3,2,1,0:T(8,128)(2,1)} %dynamic-slice_bitcast_fusion), channel_id=1, source_target_pairs={{0,1},{1,0},{2,3},{3,2},{4,5},{5,4},{6,7},{7,6},{8,9},{9,8},{10,11... | collective-permute-start | bytes 10321928 | tf_op jit(solution)/shard_map/ppermute | solution.py:71
  679.5 73.5 %collective-permute-start.31 = (bf16[4,4,128,1280]{3,2,1,0:T(8,128)(2,1)}, bf16[4,4,128,1280]{3,2,1,0:T(8,128)(2,1)}, u32[]{:S(2)}, u32[]{:S(2)}) collective-permute-start(bf16[4,4,128,1280]{3,2,1,0:T(8,128)(2,1)} %fusion.12), channel_id=1, source_target_pairs={{0,1},{1,0},{2,3},{3,2},{4,5},{5,4},{6,7},{7,6},{8,9},{9,8},{10,11... | collective-permute-start | bytes 15728648 | tf_op jit(solution)/shard_map/ppermute | solution.py:71
  690.5 22.3 %collective-permute-start.46 = (bf16[4,120,896]{2,1,0:T(8,128)(2,1)}, bf16[4,120,896]{2,1,0:T(8,128)(2,1)}, u32[]{:S(2)}, u32[]{:S(2)}) collective-permute-start(bf16[4,120,896]{2,1,0:T(8,128)(2,1)} %get-tuple-element.250), channel_id=1, source_target_pairs={{0,2},{1,3},{2,0},{3,1},{4,6},{5,7},{6,4},{7,5},{8,10},{9,11},{10,... | collective-permute-start | bytes 2580488 | tf_op jit(solution)/shard_map/ppermute | solution.py:71
  692.0 39.6 %collective-permute-start.47 = (bf16[4,120,896]{2,1,0:T(8,128)(2,1)}, bf16[4,120,896]{2,1,0:T(8,128)(2,1)}, u32[]{:S(2)}, u32[]{:S(2)}) collective-permute-start(bf16[4,120,896]{2,1,0:T(8,128)(2,1)} %get-tuple-element.252), channel_id=1, source_target_pairs={{0,4},{1,5},{2,6},{3,7},{4,0},{5,1},{6,2},{7,3},{8,12},{9,13},{10,... | collective-permute-start | bytes 2580488 | tf_op jit(solution)/shard_map/ppermute | solution.py:71
  693.5 39.3 %collective-permute-start.48 = (bf16[4,120,896]{2,1,0:T(8,128)(2,1)}, bf16[4,120,896]{2,1,0:T(8,128)(2,1)}, u32[]{:S(2)}, u32[]{:S(2)}) collective-permute-start(bf16[4,120,896]{2,1,0:T(8,128)(2,1)} %get-tuple-element.251), channel_id=1, source_target_pairs={{0,6},{1,7},{2,4},{3,5},{4,2},{5,3},{6,0},{7,1},{8,14},{9,15},{10,... | collective-permute-start | bytes 2580488 | tf_op jit(solution)/shard_map/ppermute | solution.py:71
  696.6 43.4 %collective-permute-start.39 = (bf16[4,40,1280]{2,1,0:T(8,128)(2,1)S(1)}, bf16[4,40,1280]{2,1,0:T(8,128)(2,1)S(1)}, u32[]{:S(2)}, u32[]{:S(2)}) collective-permute-start(bf16[4,40,1280]{2,1,0:T(8,128)(2,1)S(1)} %get-tuple-element.261), channel_id=1, source_target_pairs={{0,2},{1,3},{2,0},{3,1},{4,6},{5,7},{6,4},{7,5},{8,10},{9,11},{10,... | collective-permute-start | bytes 1228808 | tf_op jit(solution)/shard_map/ppermute | solution.py:71
  712.8 36.3 %collective-permute-start.40 = (bf16[4,40,1280]{2,1,0:T(8,128)(2,1)S(1)}, bf16[4,40,1280]{2,1,0:T(8,128)(2,1)S(1)}, u32[]{:S(2)}, u32[]{:S(2)}) collective-permute-start(bf16[4,40,1280]{2,1,0:T(8,128)(2,1)S(1)} %get-tuple-element.263), channel_id=1, source_target_pairs={{0,4},{1,5},{2,6},{3,7},{4,0},{5,1},{6,2},{7,3},{8,12},{9,13},{10,... | collective-permute-start | bytes 1228808 | tf_op jit(solution)/shard_map/ppermute | solution.py:71
  736.2 25.8 %collective-permute-start.49 = (bf16[120,896]{1,0:T(8,128)(2,1)}, bf16[120,896]{1,0:T(8,128)(2,1)}, u32[]{:S(2)}, u32[]{:S(2)}) collective-permute-start(bf16[120,896]{1,0:T(8,128)(2,1)} %get-tuple-element.269), channel_id=1, source_target_pairs={{0,8},{8,16},{16,24},{24,0},{1,9},{9,17},{17,25},{25,1},{2,10},{10... | collective-permute-start | bytes 645128 | tf_op jit(solution)/shard_map/ppermute | solution.py:76
  740.0 24.0 %collective-permute-start.50 = (bf16[120,896]{1,0:T(8,128)(2,1)}, bf16[120,896]{1,0:T(8,128)(2,1)}, u32[]{:S(2)}, u32[]{:S(2)}) collective-permute-start(bf16[120,896]{1,0:T(8,128)(2,1)} %get-tuple-element.271), channel_id=1, source_target_pairs={{0,16},{8,24},{16,0},{24,8},{1,17},{9,25},{17,1},{25,9},{2,18},{10... | collective-permute-start | bytes 645128 | tf_op jit(solution)/shard_map/ppermute | solution.py:76
  761.8 31.8 %collective-permute-start.32 = (bf16[4,128,1280]{2,1,0:T(8,128)(2,1)S(1)}, bf16[4,128,1280]{2,1,0:T(8,128)(2,1)S(1)}, u32[]{:S(2)}, u32[]{:S(2)}) collective-permute-start(bf16[4,128,1280]{2,1,0:T(8,128)(2,1)S(1)} %get-tuple-element.239), channel_id=1, source_target_pairs={{0,2},{1,3},{2,0},{3,1},{4,6},{5,7},{6,4},{7,5},{8,10},{9,11},{10,... | collective-permute-start | bytes 3932168 | tf_op jit(solution)/shard_map/ppermute | solution.py:71
  761.9 59.2 %collective-permute-start.33 = (bf16[4,128,1280]{2,1,0:T(8,128)(2,1)S(1)}, bf16[4,128,1280]{2,1,0:T(8,128)(2,1)S(1)}, u32[]{:S(2)}, u32[]{:S(2)}) collective-permute-start(bf16[4,128,1280]{2,1,0:T(8,128)(2,1)S(1)} %get-tuple-element.241), channel_id=1, source_target_pairs={{0,4},{1,5},{2,6},{3,7},{4,0},{5,1},{6,2},{7,3},{8,12},{9,13},{10,... | collective-permute-start | bytes 3932168 | tf_op jit(solution)/shard_map/ppermute | solution.py:71
  763.9 58.7 %collective-permute-start.34 = (bf16[4,128,1280]{2,1,0:T(8,128)(2,1)S(1)}, bf16[4,128,1280]{2,1,0:T(8,128)(2,1)S(1)}, u32[]{:S(2)}, u32[]{:S(2)}) collective-permute-start(bf16[4,128,1280]{2,1,0:T(8,128)(2,1)S(1)} %get-tuple-element.240), channel_id=1, source_target_pairs={{0,6},{1,7},{2,4},{3,5},{4,2},{5,3},{6,0},{7,1},{8,14},{9,15},{10,... | collective-permute-start | bytes 3932168 | tf_op jit(solution)/shard_map/ppermute | solution.py:71
  774.8 91.5 %collective-permute-start.25 = (bf16[256,1280]{1,0:T(8,128)(2,1)}, bf16[256,1280]{1,0:T(8,128)(2,1)}, u32[]{:S(2)}, u32[]{:S(2)}) collective-permute-start(bf16[256,1280]{1,0:T(8,128)(2,1)} %get-tuple-element.244), channel_id=1, source_target_pairs={{0,2},{1,3},{2,0},{3,1},{4,6},{5,7},{6,4},{7,5},{8,10},{9,11},{10,... | collective-permute-start | bytes 1966088 | tf_op jit(solution)/shard_map/ppermute | solution.py:71
  775.2 91.1 %collective-permute-start.26 = (bf16[256,1280]{1,0:T(8,128)(2,1)}, bf16[256,1280]{1,0:T(8,128)(2,1)}, u32[]{:S(2)}, u32[]{:S(2)}) collective-permute-start(bf16[256,1280]{1,0:T(8,128)(2,1)} %get-tuple-element.246), channel_id=1, source_target_pairs={{0,4},{1,5},{2,6},{3,7},{4,0},{5,1},{6,2},{7,3},{8,12},{9,13},{10,... | collective-permute-start | bytes 1966088 | tf_op jit(solution)/shard_map/ppermute | solution.py:71
  824.9 21.2 %collective-permute-start.36 = (bf16[128,1280]{1,0:T(8,128)(2,1)S(1)}, bf16[128,1280]{1,0:T(8,128)(2,1)S(1)}, u32[]{:S(2)}, u32[]{:S(2)}) collective-permute-start(bf16[128,1280]{1,0:T(8,128)(2,1)S(1)} %get-tuple-element.266), channel_id=1, source_target_pairs={{0,16},{8,24},{16,0},{24,8},{1,17},{9,25},{17,1},{25,9},{2,18},{10... | collective-permute-start | bytes 983048 | tf_op jit(solution)/shard_map/ppermute | solution.py:76
  827.5 18.6 %collective-permute-start.37 = (bf16[128,1280]{1,0:T(8,128)(2,1)S(1)}, bf16[128,1280]{1,0:T(8,128)(2,1)S(1)}, u32[]{:S(2)}, u32[]{:S(2)}) collective-permute-start(bf16[128,1280]{1,0:T(8,128)(2,1)S(1)} %get-tuple-element.265), channel_id=1, source_target_pairs={{0,24},{8,0},{16,8},{24,16},{1,25},{9,1},{17,9},{25,17},{2,26},{10... | collective-permute-start | bytes 983048 | tf_op jit(solution)/shard_map/ppermute | solution.py:76
  837.4 28.9 %collective-permute-start.27 = (bf16[256,1280]{1,0:T(8,128)(2,1)}, bf16[256,1280]{1,0:T(8,128)(2,1)}, u32[]{:S(2)}, u32[]{:S(2)}) collective-permute-start(bf16[256,1280]{1,0:T(8,128)(2,1)} %get-tuple-element.245), channel_id=1, source_target_pairs={{0,6},{1,7},{2,4},{3,5},{4,2},{5,3},{6,0},{7,1},{8,14},{9,15},{10,... | collective-permute-start | bytes 1966088 | tf_op jit(solution)/shard_map/ppermute | solution.py:71
  (77 other events, 1158.2 us)
Sparse Core Ops, SparseCore 0:
  10.2 40.8 all-gather.9
  52.6 53.6 all-gather.7
  109.1 138.5 all-gather.11
  249.1 123.1 all-gather.13
  375.0 118.5 reduce-scatter.2
  496.4 160.7 reduce-scatter.4

commit v3 on v2

--- a/solution.py
+++ b/solution.py
@@ -66,6 +66,23 @@
     return lax.optimization_barrier((value,) + others)[0]
 
 
+def hold_kernel(*_):
+    pass
+
+
+def hold(values, *others):
+    anywhere = pl.BlockSpec(memory_space=pl.ANY)
+    return pl.pallas_call(
+        hold_kernel,
+        in_specs=[anywhere] * (len(values) + len(others)),
+        out_specs=[anywhere] * len(values),
+        out_shape=[jax.ShapeDtypeStruct(value.shape, value.dtype) for value in values],
+        input_output_aliases={index: index for index in range(len(values))},
+        cost_estimate=LIGHT,
+        name="hold",
+    )(*values, *others)
+
+
 def swap(value, mask):
     size = lax.axis_size("expert")
     return lax.ppermute(value, "expert", [(i, i ^ mask) for i in range(size)])
@@ -106,31 +123,53 @@
     return [even[k].astype(F32) + other[k].astype(F32) for k in range(even.shape[0])]
 
 
+def spread_chips(summed):
+    return [swap(summed[index].astype(BF16), 2 * index) for index in range(1, len(summed))]
+
+
+def add_up(total, parts):
+    for part in parts:
+        total = total + part.astype(F32)
+    return total
+
+
 def join_chips(summed):
-    total = summed[0]
-    for index in range(1, len(summed)):
-        total = total + swap(summed[index].astype(BF16), 2 * index).astype(F32)
-    return total
-
-
-def scatter_dense(grad):
-    size, here = lax.axis_size("expert"), lax.axis_index("expert")
+    return add_up(summed[0], spread_chips(summed))
+
+
+def core_split(grad, rows):
+    core = lax.axis_index("expert") % 2
+    split = grad.reshape(grad.shape[0], -1, 2, rows, grad.shape[-1])
+    return pick(split, core, 2), pick(split, 1 - core, 2)
+
+
+def chip_sums(mine, received):
+    chip = lax.axis_index("expert") // 2
+    chips = lax.axis_size("expert") // 2
+    shape = (mine.shape[0], -1, chips) + mine.shape[2:]
+    mine, received = mine.reshape(shape), received.reshape(shape)
+    return [
+        pick(mine, chip ^ mask, 2).astype(F32) + pick(received, chip ^ mask, 2).astype(F32)
+        for mask in range(chips)
+    ]
+
+
+def column_sum(total, axis):
     deep, level = lax.axis_size("dp"), lax.axis_index("dp")
-    core, chip = here % 2, here // 2
-    low = grad.astype(BF16).reshape((deep, size // 2, 2) + grad.shape[2:])
-    other = swap(pick(low, 1 - core, 2), 1)
-    summed = (pick(low, core, 2).astype(F32) + other.astype(F32)).astype(BF16)
-    total = pick(summed, chip, 1).astype(F32)
-    for mask in range(1, size // 2):
-        total = total + swap(pick(summed, chip ^ mask, 1), 2 * mask).astype(F32)
-    column = total.astype(BF16)
-    result = pick(total, level, 0)
+    low = total.astype(BF16)
+    result = pick(total, level, axis)
+    arrived = low
     for step in range(1, deep):
-        result = result + rotate(pick(column, (level + step) % deep, 0), step).astype(F32)
+        block = pick(low, (level + step) % deep, axis)
+        if step == 2:
+            block = hold([block], arrived)[0]
+        arrived = rotate(block, step)
+        result = result + arrived.astype(F32)
     return result
 
 
 VMEM_LIMIT = 60 * 1024 * 1024
+LIGHT = pl.CostEstimate(flops=1, bytes_accessed=1, transcendentals=0)
 
 
 def product(left, right, left_dim, right_dim):
@@ -174,9 +213,7 @@
         ),
         out_shape=jax.ShapeDtypeStruct((parts, deep, 2 * chips, rows, width), even.dtype),
         compiler_params=kernel_params(1),
-        cost_estimate=pl.CostEstimate(
-            flops=0, bytes_accessed=8 * even.size, transcendentals=0
-        ),
+        cost_estimate=LIGHT,
         name="assemble",
     )(here[None], even, odd)
     return joined.reshape(parts, deep * 2 * chips * rows, width)
@@ -257,19 +294,34 @@
             jax.ShapeDtypeStruct((rows, width), BF16),
         ],
         compiler_params=kernel_params(1),
-        cost_estimate=pl.CostEstimate(
-            flops=2 * width * width * (rows + 2 * length) + 4 * rows * length * width,
-            bytes_accessed=6 * width * width + 10 * length * width,
-            transcendentals=rows * length * width // HEAD_DIM,
-        ),
+        cost_estimate=LIGHT,
         name="attention_forward",
     )(place[None], normed, projections, projections, projections, cosine, sine, starts, own_starts)
 
 
+def split_shapes(parts, rows_all, width, rows):
+    if rows % 8 == 0:
+        return [(parts, rows_all // (2 * rows), rows, width)] * 2
+    return [(parts, rows_all, width)]
+
+
+def store_split(grad, core, part, targets):
+    if len(targets) == 1:
+        targets[0][part] = grad.astype(BF16)
+        return
+    mine, other = targets
+    count, rows = mine.shape[1], mine.shape[2]
+    cut = grad.reshape(count, 2, rows, grad.shape[1])
+    even, odd = cut[:, 0], cut[:, 1]
+    mine[part] = jnp.where(core == 0, even, odd).astype(BF16)
+    other[part] = jnp.where(core == 0, odd, even).astype(BF16)
+
+
 def attention_grad_kernel(
-    place_ref, turned_normed, own_turned, wq, wk, wv, wo, q, k, v, o, arriving,
-    cosine, sine, starts, own_starts, grads, normed_grad, own_grad, dq_s, dk_s, dv_s,
+    place_ref, turned_normed, own_turned, wo, q, k, v, o, arriving, cosine, sine, starts, own_starts, *refs
 ):
+    *grads, dq_out, dk_out, dv_out = refs
+    grads = grads[-2:] if len(grads[-1].shape) == 4 else grads[-1:]
     rows = q.shape[0]
     place = pl.multiple_of(place_ref[0], rows)
     allowed = visible_keys(place, own_starts[...], starts[...])
@@ -287,48 +339,40 @@
         query_grad = product(scores_grad, keys, 1, 0) * factor
         keys_grad = product(scores_grad, query, 0, 0) * factor
         values_grad = product(weights.astype(BF16), incoming, 0, 0)
-        dq_s[:, lanes] = turn_head(query_grad, own_cosine, -own_sine).astype(BF16)
-        dk_s[:, lanes] = turn_head(keys_grad, cosine[...], -sine[...]).astype(BF16)
-        dv_s[:, lanes] = values_grad.astype(BF16)
-    dq, dk, dv = dq_s[...], dk_s[...], dv_s[...]
-    grads[0] = product(own_turned[...], dq, 1, 0).astype(BF16)
-    grads[1] = product(turned_normed[...], dk, 1, 0).astype(BF16)
-    grads[2] = product(turned_normed[...], dv, 1, 0).astype(BF16)
-    part = product(dk, wk[0], 1, 1) + product(dv, wv[0], 1, 1)
-    own_part = product(dq, wq[0], 1, 1)
-
-    @pl.when(pl.program_id(0) == 0)
-    def _():
-        normed_grad[...] = part
-        own_grad[...] = own_part
-
-    @pl.when(pl.program_id(0) > 0)
-    def _():
-        normed_grad[...] += part
-        own_grad[...] += own_part
-
-
-def attention_grad(place, normed, own_normed, projections, wo, q, k, v, o, arriving, cosine, sine, starts):
-    length, width = normed.shape
+        dq_out[:, lanes] = turn_head(query_grad, own_cosine, -own_sine).astype(BF16)
+        dk_out[:, lanes] = turn_head(keys_grad, cosine[...], -sine[...]).astype(BF16)
+        dv_out[:, lanes] = values_grad.astype(BF16)
+    core = place_ref[1]
+    store_split(product(own_turned[...], dq_out[...], 1, 0), core, 0, grads)
+    store_split(product(turned_normed[...], dk_out[...], 1, 0), core, 1, grads)
+    store_split(product(turned_normed[...], dv_out[...], 1, 0), core, 2, grads)
+
+
+def attention_grad(
+    place, turned, own_turned, wo, q, k, v, o, arriving, cosine, sine, starts, dense_rows, first, count, waits=()
+):
+    width, length = turned.shape
     rows = q.shape[0]
     span = 2 * HEAD_DIM
     own_starts = lax.dynamic_slice_in_dim(starts, place, rows)[:, None]
     starts = starts[None, :]
-    turned, own_turned = normed.T, own_normed.T
-    column = lambda index: pl.BlockSpec((1, width, span), lambda p, _: (index, 0, p))
-    blocks = lambda count: pl.BlockSpec((count, span), lambda p, _: (0, p))
+    place = jnp.stack([place, lax.axis_index("expert") % 2])
+    shapes = split_shapes(3, width, span * count, dense_rows)
+    grad_specs = [
+        pl.BlockSpec(shape[:-1] + (span,), lambda p, _, size=len(shape): (0,) * (size - 1) + (p,))
+        for shape in shapes
+    ]
+    blocks = lambda size: pl.BlockSpec((size, span), lambda p, _: (0, p + first))
+    column = lambda size: pl.BlockSpec((size, span), lambda p, _: (0, p))
     return pl.pallas_call(
         attention_grad_kernel,
         grid_spec=pltpu.PrefetchScalarGridSpec(
             num_scalar_prefetch=1,
-            grid=(width // span,),
+            grid=(count,),
             in_specs=[
                 whole(turned),
                 whole(own_turned),
-                column(0),
-                column(1),
-                column(2),
-                pl.BlockSpec((span, width), lambda p, _: (p, 0)),
+                pl.BlockSpec((span, width), lambda p, _: (p + first, 0)),
                 blocks(rows),
                 blocks(length),
                 blocks(length),
@@ -338,39 +382,97 @@
                 whole(sine),
                 whole(starts),
                 whole(own_starts),
-            ],
+            ]
+            + [pl.BlockSpec(memory_space=pl.ANY)] * len(waits),
+            out_specs=[*grad_specs, column(rows), column(length), column(length)],
+        ),
+        out_shape=[
+            *[jax.ShapeDtypeStruct(shape, BF16) for shape in shapes],
+            jax.ShapeDtypeStruct((rows, span * count), BF16),
+            jax.ShapeDtypeStruct((length, span * count), BF16),
+            jax.ShapeDtypeStruct((length, span * count), BF16),
+        ],
+        compiler_params=kernel_params(1),
+        cost_estimate=pl.CostEstimate(flops=32 * rows * length * width * count, bytes_accessed=1, transcendentals=0),
+        name="attention_backward",
+    )(
+        place, turned, own_turned, wo, q, k, v, o, arriving, cosine, sine, starts, own_starts, *waits
+    )
+
+
+def normed_grad_kernel(parts, waits, *refs):
+    level_ref, sequence, projections = refs[:3]
+    grads = refs[3 : 3 + 3 * parts]
+    low_out, own_out, gain_out = refs[3 + 3 * parts + waits :]
+    step = pl.program_id(0)
+    begin = 0
+    total = None
+    own = None
+    for part in range(parts):
+        dq, dk, dv = grads[3 * part : 3 * part + 3]
+        lanes = slice(begin, begin + dk.shape[1])
+        begin += dk.shape[1]
+        term = product(dk[...], projections[1, :, lanes], 1, 1) + product(
+            dv[...], projections[2, :, lanes], 1, 1
+        )
+        total = term if total is None else total + term
+    low_out[0] = total.astype(BF16)
+    values = sequence[...].astype(F32)
+    scaled = values * lax.rsqrt(jnp.mean(values * values, axis=-1, keepdims=True) + NORM_EPS)
+
+    @pl.when(step == 0)
+    def _():
+        gain_out[...] = jnp.zeros_like(gain_out)
+
+    gain_out[...] += jnp.sum(total * scaled, axis=0, keepdims=True)
+
+    @pl.when(step == level_ref[0])
+    def _():
+        begin = 0
+        own = total
+        for part in range(parts):
+            dq = grads[3 * part]
+            lanes = slice(begin, begin + dq.shape[1])
+            begin += dq.shape[1]
+            own = own + product(dq[...], projections[0, :, lanes], 1, 1)
+        own_out[...] = own
+        gain_out[...] += jnp.sum((own - total) * scaled, axis=0, keepdims=True)
+
+
+def normed_grad(sequence, projections, grads, rows, waits):
+    length, width = sequence.shape
+    in_specs = [pl.BlockSpec((rows, width), lambda t, _: (t, 0)), whole(projections)]
+    operands = [sequence, projections]
+    for dq, dk, dv in grads:
+        tile = pl.BlockSpec((rows, dk.shape[1]), lambda t, _: (t, 0))
+        in_specs += [whole(dq), tile, tile]
+        operands += [dq, dk, dv]
+    return pl.pallas_call(
+        functools.partial(normed_grad_kernel, len(grads), len(waits)),
+        grid_spec=pltpu.PrefetchScalarGridSpec(
+            num_scalar_prefetch=1,
+            grid=(length // rows,),
+            in_specs=in_specs + [pl.BlockSpec(memory_space=pl.ANY)] * len(waits),
             out_specs=[
-                pl.BlockSpec((3, width, span), lambda p, _: (0, 0, p)),
-                pl.BlockSpec((length, width), lambda p, _: (0, 0)),
-                pl.BlockSpec((rows, width), lambda p, _: (0, 0)),
-            ],
-            scratch_shapes=[
-                pltpu.VMEM((rows, span), BF16),
-                pltpu.VMEM((length, span), BF16),
-                pltpu.VMEM((length, span), BF16),
+                pl.BlockSpec((1, rows, width), lambda t, _: (t, 0, 0)),
+                pl.BlockSpec((rows, width), lambda t, _: (0, 0)),
+                pl.BlockSpec((1, width), lambda t, _: (0, 0)),
             ],
         ),
         out_shape=[
-            jax.ShapeDtypeStruct((3, width, width), BF16),
-            jax.ShapeDtypeStruct((length, width), F32),
+            jax.ShapeDtypeStruct((length // rows, rows, width), BF16),
             jax.ShapeDtypeStruct((rows, width), F32),
+            jax.ShapeDtypeStruct((1, width), F32),
         ],
         compiler_params=kernel_params(1),
-        cost_estimate=pl.CostEstimate(
-            flops=4 * width * width * (rows + 2 * length) + 10 * rows * length * width,
-            bytes_accessed=14 * width * width + 14 * length * width,
-            transcendentals=rows * length * width // HEAD_DIM,
-        ),
-        name="attention_backward",
-    )(
-        place[None], turned, own_turned, projections, projections, projections, wo,
-        q, k, v, o, arriving, cosine, sine, starts, own_starts,
-    )
-
-
-def expert_kernel(has_before, split, part_rows, *refs):
+        cost_estimate=pl.CostEstimate(flops=24 * length * width * width, bytes_accessed=1, transcendentals=0),
+        name="normed_grad",
+    )(lax.axis_index("dp")[None], *operands, *waits)
+
+
+def expert_kernel(has_before, split, part_rows, waits, *refs):
     odd_n, even_n, odd_c, even_c, gates, weights = refs[:6]
-    refs = refs[6:]
+    refs = refs[6 + waits :]
     if has_before:
         routed_in, entry_in = refs[:2]
         refs = refs[2:]
@@ -446,7 +548,7 @@
         entry_out[...] = entry
 
 
-def expert_pass(tokens, grads, gates, weights, part_rows, before, split):
+def expert_pass(tokens, grads, gates, weights, part_rows, before, split, waits=()):
     even_n, odd_n = tokens
     even_c, odd_c = grads
     count, rows, width = even_n.shape
@@ -457,7 +559,8 @@
     even = pl.BlockSpec((1, rows, width), lambda t: (jnp.maximum(t - count, 0), 0, 0))
     tile = lambda size: pl.BlockSpec((rows, size), lambda t: (t, 0))
     in_specs = [odd, even, odd, even, tile(1), pl.BlockSpec(memory_space=pl.ANY)]
-    operands = [odd_n, even_n, odd_c, even_c, gates, weights]
+    operands = [odd_n, even_n, odd_c, even_c, gates, weights, *waits]
+    in_specs += [pl.BlockSpec(memory_space=pl.ANY)] * len(waits)
     if before is not None:
         in_specs += [tile(width), tile(width)]
         operands += list(before)
@@ -474,7 +577,7 @@
         jax.ShapeDtypeStruct((total, 2 * hidden_width), BF16),
     ]
     return pl.pallas_call(
-        functools.partial(expert_kernel, before is not None, split, part_rows),
+        functools.partial(expert_kernel, before is not None, split, part_rows, len(waits)),
         grid=(tiles,),
         in_specs=in_specs,
         out_specs=out_specs,
@@ -485,16 +588,52 @@
             pltpu.SemaphoreType.DMA((weights.shape[0], 3)),
         ],
         compiler_params=kernel_params(1),
-        cost_estimate=pl.CostEstimate(
-            flops=12 * total * width * hidden_width,
-            bytes_accessed=total * (8 * width + 6 * hidden_width) + 6 * width * hidden_width,
-            transcendentals=total * hidden_width,
-        ),
+        cost_estimate=LIGHT,
         name="expert_pass",
     )(*operands)
 
 
-def expert_grad_kernel(odd_n, even_n, odd_c, even_c, gates, hidden, pair, out):
+def shared_kernel(place_ref, tokens_ref, incoming_ref, weights, result_out, entry_out, *targets):
+    tokens, incoming = tokens_ref[...], incoming_ref[...]
+    core = place_ref[0]
+    gate_part = product(tokens, weights[0], 1, 0)
+    up_part = product(tokens, weights[1], 1, 0)
+    sigma = 1.0 / (1.0 + jnp.exp(-gate_part))
+    smooth = gate_part * sigma
+    hidden = (smooth * up_part).astype(BF16)
+    result_out[...] = product(hidden, weights[2], 1, 1)
+    grad_hidden = product(incoming, weights[2], 1, 0)
+    grad_gate = (grad_hidden * up_part * sigma * (1.0 + gate_part * (1.0 - sigma))).astype(BF16)
+    grad_up = (grad_hidden * smooth).astype(BF16)
+    entry_out[...] = product(grad_gate, weights[0], 1, 1) + product(grad_up, weights[1], 1, 1)
+    store_split(product(tokens, grad_gate, 0, 0), core, 0, targets)
+    store_split(product(tokens, grad_up, 0, 0), core, 1, targets)
+    store_split(product(incoming, hidden, 0, 0), core, 2, targets)
+
+
+def shared_pass(tokens, incoming, weights, dense_rows):
+    rows, width = tokens.shape
+    hidden_width = weights.shape[2]
+    shapes = split_shapes(3, width, hidden_width, dense_rows)
+    out_shape = [jax.ShapeDtypeStruct((rows, width), F32)] * 2
+    out_shape += [jax.ShapeDtypeStruct(shape, BF16) for shape in shapes]
+    return pl.pallas_call(
+        shared_kernel,
+        grid_spec=pltpu.PrefetchScalarGridSpec(
+            num_scalar_prefetch=1,
+            grid=(1,),
+            in_specs=[whole(tokens), whole(incoming), whole(weights)],
+            out_specs=[whole(shape) for shape in out_shape],
+        ),
+        out_shape=out_shape,
+        compiler_params=kernel_params(1),
+        cost_estimate=LIGHT,
+        name="shared_pass",
+    )(lax.axis_index("expert")[None] % 2, tokens, incoming, weights)
+
+
+def expert_grad_kernel(odd_n, even_n, odd_c, even_c, gates, hidden, pair, *refs):
+    out = refs[-1]
     count, rows, span = odd_n.shape
     half = count * rows
     hidden_width = hidden.shape[1]
@@ -511,7 +650,7 @@
     out[2] = product(grad_pair, hidden[...], 0, 0).astype(BF16)
 
 
-def expert_grad(tokens, grads, gates, hidden, pair):
+def expert_grad(tokens, grads, gates, hidden, pair, waits=()):
     even_n, odd_n = tokens
     even_c, odd_c = grads
     count, rows, width = even_n.shape
@@ -521,17 +660,14 @@
     return pl.pallas_call(
         expert_grad_kernel,
         grid=(width // span,),
-        in_specs=[stack, stack, stack, stack, whole(gates), whole(hidden), whole(pair)],
+        in_specs=[stack, stack, stack, stack, whole(gates), whole(hidden), whole(pair)]
+        + [pl.BlockSpec(memory_space=pl.ANY)] * len(waits),
         out_specs=pl.BlockSpec((3, span, hidden_width), lambda t: (0, t, 0)),
         out_shape=jax.ShapeDtypeStruct((3, width, hidden_width), BF16),
         compiler_params=kernel_params(1),
-        cost_estimate=pl.CostEstimate(
-            flops=12 * count * rows * width * hidden_width,
-            bytes_accessed=8 * count * rows * (width + 2 * hidden_width) + 6 * width * hidden_width,
-            transcendentals=0,
-        ),
+        cost_estimate=LIGHT,
         name="expert_weight_grad",
-    )(odd_n, even_n, odd_c, even_c, gates, hidden, pair)
+    )(odd_n, even_n, odd_c, even_c, gates, hidden, pair, *waits)
 
 
 def body(
@@ -605,13 +741,21 @@
     grad_out = grad_low.astype(F32)
     attn_column = lax.all_gather(attn_own, "dp")
     projection_fan = fan(attn_column[:, :3])
-    sequence = lax.all_gather(after(inputs_low, attn_column), "dp", axis=0, tiled=True)
-    sequence, *projection_fan = lax.optimization_barrier((sequence, *projection_fan))
-    expert_parts = [
-        lax.all_gather(
-            after(jnp.concatenate([expert_own[0], shared_own], 1), sequence), "dp"
-        )
-    ]
+    shared_size = shared_own.size
+    shared_rows = -(-shared_size // (8 * width)) * 8
+    shared_flat = jnp.pad(shared_own.reshape(-1), (0, shared_rows * width - shared_size))
+    column = lax.all_gather(
+        after(
+            jnp.concatenate([inputs_low, shared_flat.reshape(shared_rows, width)], 0), attn_column
+        ),
+        "dp",
+    )
+    column, *projection_fan = lax.optimization_barrier((column, *projection_fan))
+    sequence = column[:, :token_rows].reshape(length, width)
+    shared_column = column[:, token_rows:].reshape(deep, -1)[:, :shared_size].reshape(
+        deep, 3, dense_rows, hidden_width
+    )
+    expert_parts = [lax.all_gather(after(expert_own[0], sequence), "dp")]
     projection_even = jnp.stack(projection_fan)
     projection_odd = swap(projection_even, 1)
     out_even, out_odd = gather_swaps(attn_column[:, 3:], sequence)
@@ -621,14 +765,13 @@
         )
     projections = assemble(projection_even, projection_odd)
     out_low = assemble(out_even, out_odd)[0]
-    grads_plane = gather_swaps(grad_low, out_even)
-    shared_low = assemble(*gather_swaps(expert_parts[0][:, :, part_rows:]))
+    grads_fan = fan(hold([grad_low], projections)[0])
     gain_one = gain_low[0].astype(F32)
     gain_two = gain_low[1].astype(F32)
 
-    sequence = sequence.astype(F32)
-
-    normed_all, scaled_all, _ = norm_forward(sequence, gain_one)
+    sequence_low, sequence = sequence, sequence.astype(F32)
+
+    normed_all, _, _ = norm_forward(sequence, gain_one)
     inputs = inputs_low.astype(F32)
     normed, scaled_one, inverse_one = norm_forward(inputs, gain_one)
     place = level * token_rows
@@ -637,6 +780,9 @@
     query, keys, values, mixed, mixed_low = attention(
         place, normed_all, projections, cosine_all, sine_all, starts, token_rows
     )
+    mixed_low = hold([mixed_low], *grads_fan[1:])[0]
+    grads_even = jnp.stack(grads_fan)
+    grads_plane = (grads_even, swap(grads_even, 1))
     middle = inputs + contract(mixed_low, out_low, 1, 0)
     second, scaled_two, inverse_two = norm_forward(middle, gain_two)
 
@@ -658,143 +804,179 @@
     gates_plane = gates_received[relative].reshape(groups * token_rows, expert_local)
 
     tokens = gather_swaps(second)
+    expert_parts[0] = after(expert_parts[0], tokens[1], grads_plane[1], gates_plane)
+
+    shared_fan = fan(hold([shared_column], tokens[1], expert_parts[0])[0])
+
+    def shared_step(shared_even, shared_odd):
+        shared_low = assemble(shared_even, shared_odd)
+        out, entry, *grad = shared_pass(second, grad_low, shared_low, dense_rows)
+        if len(grad) == 1:
+            grad = core_split(grad[0], dense_rows)
+        return out, entry, chip_sums(grad[0], swap(grad[1], 1))
+
+    def spread_after(sums, *others):
+        lows = hold([part.astype(BF16) for part in sums[1:]], *others)
+        return [swap(part, 2 * index + 2) for index, part in enumerate(lows)]
+
+    mask = here ^ jnp.arange(groups)
+    back = mask // 2 + jnp.where(mask % 2 == 1, 0, groups // 2)
+
+    def return_gates(gate_grads):
+        sent = jnp.concatenate(gate_grads, -1).reshape(groups, token_rows, expert_local)[back]
+        return lax.all_to_all(sent, "expert", 0, 0, tiled=True)
 
     gate_grads = []
     expert_sums = []
+    part_sums = []
     before = None
+    turned, own_turned = normed_all.T, normed.T
     for number in range(expert_local):
         last = number == expert_local - 1
         gate_column = gates_plane[:, number : number + 1]
         parts = expert_pass(
-            tokens, grads_plane, gate_column, expert_parts[number], part_rows, before, last
+            tokens, grads_plane, gate_column, expert_parts[number], part_rows, before, last,
+            (turned, own_turned) if number == 1 else (),
         )
         before, (gate_grad, hidden, pair) = parts[:-3], parts[-3:]
         gate_grads.append(gate_grad)
+        if number == 0:
+            shared_even = hold([jnp.stack(shared_fan)], hidden)[0]
+            shared_odd = swap(shared_even, 1)
         if last:
             routed_odd, routed_even, entry_odd, entry_even = before
+            entry_odd = hold([entry_odd], *shared_parts)[0]
             entry_other = swap(entry_odd, 1)
-            routed_other = swap(after(routed_odd, entry_other), 1)
-            hidden = after(hidden, entry_other)
-        expert_sums.append(
-            lax.psum_scatter(
-                expert_grad(tokens, grads_plane, gate_column, hidden, pair),
-                "dp",
-                scatter_dimension=1,
-                tiled=True,
-            ).astype(F32)
+            gate_grad_back = return_gates(gate_grads)
+            entry_sums = join_cores(entry_even, entry_other)
+            entry_parts = spread_chips(entry_sums)
+            routed_other = swap(hold([routed_odd], entry_sums[1].astype(BF16))[0], 1)
+        expert_part = expert_grad(
+            tokens,
+            grads_plane,
+            gate_column,
+            hidden,
+            pair,
+            [routed_other, gate_grad_back] if last else shared_fan[1:],
         )
+        if number == 0:
+            shared_odd = hold([shared_odd], expert_part)[0]
+            shared_out, shared_entry, shared_sums = shared_step(shared_even, shared_odd)
+            shared_parts = spread_after(shared_sums, *expert_parts[1:2])
+        expert_part = expert_part.reshape(3, deep, part_rows, hidden_width)
+        if last:
+            shared_total = add_up(shared_sums[0], shared_parts)
+            extra = -(part_rows + dense_rows) % 16
+            shared_total = jnp.pad(shared_total.astype(BF16), ((0, 0), (0, 0), (0, extra), (0, 0)))
+            expert_part = jnp.concatenate([expert_part, shared_total], 2)
+        part_sum = lax.psum_scatter(
+            expert_part.reshape(3, -1, hidden_width), "dp", scatter_dimension=1, tiled=True
+        )
+        part_sums.append(part_sum)
+        expert_sums.append(part_sum[:, :part_rows].astype(F32))
+    shared_sum = part_sum[:, part_rows : part_rows + dense_rows].astype(F32)
     expert_sum = jnp.stack(expert_sums)
 
-    grad_second = join_chips(join_cores(entry_even, entry_other))
-    routed_even, routed_other = lax.optimization_barrier((routed_even, routed_other, grad_second))[:2]
-    routed = join_chips(join_cores(routed_even, routed_other))
-    mask = here ^ jnp.arange(groups)
-    back = mask // 2 + jnp.where(mask % 2 == 1, 0, groups // 2)
-    gate_grad_sent = jnp.concatenate(gate_grads, -1).reshape(groups, token_rows, expert_local)[back]
-    gate_grad_back = lax.all_to_all(gate_grad_sent, "expert", 0, 0, tiled=True)
+    entry_parts = hold(entry_parts, expert_part)
+    grad_second = add_up(entry_sums[0], entry_parts)
+    routed_sums = join_cores(routed_even, routed_other)
     gate_grad_stored = gate_grad_back.transpose(1, 0, 2).reshape(token_rows, specialist_total)
     grad_prob = jnp.sum(gate_grad_stored[:, None, :] * to_storage[None], axis=-1)
     grad_prob = jnp.where(kept, grad_prob, 0.0)
 
-    gate_shared = contract(second, shared_low[0], 1, 0)
-    up_shared = contract(second, shared_low[1], 1, 0)
-    hidden_shared = (jax.nn.silu(gate_shared) * up_shared).astype(BF16)
-    shared_out = contract(hidden_shared, shared_low[2], 1, 1)
-    grad_hidden_shared = contract(grad_low, shared_low[2], 1, 0)
-    sigma = jax.nn.sigmoid(gate_shared)
-    grad_gate_shared = (
-        grad_hidden_shared * up_shared * sigma * (1.0 + gate_shared * (1.0 - sigma))
-    ).astype(BF16)
-    grad_up_shared = (grad_hidden_shared * gate_shared * sigma).astype(BF16)
-    shared_entry = contract(grad_gate_shared, shared_low[0], 1, 1) + contract(
-        grad_up_shared, shared_low[1], 1, 1
-    )
-    block_out = (middle + shared_out + routed).astype(BF16)
 
     grad_logit = (probs * (grad_prob - jnp.sum(probs * grad_prob, axis=-1, keepdims=True))).astype(
         BF16
     )
     router_grad = contract(second, grad_logit, 0, 0)
     grad_second = grad_second + contract(grad_logit, router_low, 1, 1) + shared_entry
-    shared_grad = jnp.stack(
-        [
-            contract(second, grad_gate_shared, 0, 0),
-            contract(second, grad_up_shared, 0, 0),
-            contract(grad_low, hidden_shared, 0, 0),
-        ]
-    )
     gain_two_grad = jnp.sum(grad_second * scaled_two, axis=0)
     grad_middle = norm_backward(grad_second, scaled_two, inverse_two, gain_two) + grad_out
     grad_attn_out = grad_middle.astype(BF16)
-    out_grad = contract(mixed_low, grad_attn_out, 0, 0)
-    projection_grad, grad_normed_all, grad_normed_own = attention_grad(
-        place,
-        normed_all,
-        normed,
+    out_grad = contract(mixed_low, grad_attn_out, 0, 0).astype(BF16)
+    out_mine, out_other = core_split(out_grad[None], dense_rows)
+    out_received = swap(out_other, 1)
+
+    def grad_part(first, count, waits=()):
+        *grads, dq, dk, dv = attention_grad(
+            place,
+            turned,
+            own_turned,
+            out_low,
+            query,
+            keys,
+            values,
+            mixed,
+            grad_attn_out,
+            cosine_all,
+            sine_all,
+            starts,
+            dense_rows,
+            first,
+            count,
+            waits,
+        )
+        if len(grads) == 1:
+            grads = core_split(grads[0], dense_rows)
+        return grads[0], grads[1], (dq, dk, dv)
+
+    pairs = width // (2 * head_dim)
+    early = (pairs + 1) // 2
+    first_mine, first_other, first_terms = grad_part(0, early)
+    last_mine, last_other, last_terms = grad_part(
+        early, pairs - early, [first_other, part_sums[0]]
+    )
+    cut = first_mine.shape[-1]
+    first_sums = chip_sums(
+        jnp.concatenate([first_mine, out_mine[..., :cut]], 0),
+        jnp.concatenate([swap(first_other, 1), out_received[..., :cut]], 0),
+    )
+    first_parts = spread_chips(first_sums)
+    last_sums = chip_sums(
+        jnp.concatenate([last_mine, out_mine[..., cut:]], 0),
+        jnp.concatenate([swap(last_other, 1), out_received[..., cut:]], 0),
+    )
+    last_parts = spread_after(last_sums, *first_parts)
+    routed_parts = spread_after(routed_sums, *last_parts)
+    normed_low, grad_normed, gain_one_grad = normed_grad(
+        sequence_low,
         projections,
-        out_low,
-        query,
-        keys,
-        values,
-        mixed,
-        after(grad_attn_out, routed_other),
-        cosine_all,
-        sine_all,
-        starts,
-    )
-    gain_one_grad = jnp.sum(grad_normed_all * scaled_all, axis=0) + jnp.sum(
-        grad_normed_own * scaled_one, axis=0
-    )
-    normed_low = grad_normed_all.astype(BF16).reshape(deep, token_rows, width)
-    grad_normed = grad_normed_own + pick(
-        grad_normed_all.reshape(deep, token_rows, width), level, 0
-    )
-    for step in range(1, deep):
-        grad_normed = grad_normed + shift(pick(normed_low, (level - step) % deep, 0), -step).astype(
-            F32
-        )
-    grad_inputs = norm_backward(grad_normed, scaled_one, inverse_one, gain_one) + grad_middle
-
-    fill_rows = -(-(dense_rows * (specialist_total + 2)) // (8 * width)) * 8
-    def by_owner(grad):
-        return grad.reshape(grad.shape[0], deep, groups, dense_rows, grad.shape[-1]).transpose(
-            1, 2, 0, 3, 4
-        )
-
+        (first_terms, last_terms),
+        token_rows,
+        [first_sums[1].astype(BF16)],
+    )
+    gain_one_grad = gain_one_grad[0]
     small_grad = jnp.concatenate(
         [
-            router_grad.reshape(deep, groups, dense_rows * specialist_total),
+            router_grad.reshape(everyone, router_size),
             jnp.stack([gain_one_grad, gain_two_grad])
-            .reshape(2, deep, groups, dense_rows)
-            .transpose(1, 2, 0, 3)
-            .reshape(deep, groups, 2 * dense_rows),
+            .reshape(2, everyone, dense_rows)
+            .transpose(1, 0, 2)
+            .reshape(everyone, 2 * dense_rows),
         ],
         -1,
     )
-    small_grad = jnp.pad(
-        small_grad, ((0, 0), (0, 0), (0, fill_rows * width - small_grad.shape[-1]))
-    ).reshape(deep, groups, fill_rows, width)
-    projection_sums = scatter_dense(
-        jnp.concatenate(
-            [
-                by_owner(projection_grad).reshape(deep, groups, 3 * dense_rows, width),
-                small_grad,
-            ],
-            2,
-        )
-    )
-    out_sum = scatter_dense(out_grad.reshape(deep, groups, dense_rows, width))
-    shared_sum = scatter_dense(
-        by_owner(shared_grad).reshape(deep, groups, 3 * dense_rows, hidden_width)
-    ).reshape(3, dense_rows, hidden_width)
-    attn_sum = jnp.concatenate(
-        [projection_sums[: 3 * dense_rows].reshape(3, dense_rows, width), out_sum[None]], 0
-    )
-    small_sum = projection_sums[3 * dense_rows :].reshape(-1)
-    router_sum = small_sum[: dense_rows * specialist_total].reshape(dense_rows, specialist_total)
-    gain_sum = small_sum[
-        dense_rows * specialist_total : dense_rows * (specialist_total + 2)
-    ].reshape(2, dense_rows)
+    small_grad = jnp.pad(small_grad, ((0, 0), (0, small_rows * 128 - small_size)))
+    small_received = lax.all_to_all(
+        small_grad.reshape(everyone, small_rows, 128), ("dp", "expert"), 0, 0, tiled=True
+    )
+    small_sum = jnp.sum(hold([small_received], *last_parts)[0], axis=0).reshape(-1)
+    first_total = add_up(first_sums[0], hold(first_parts, grad_normed))
+    last_total = add_up(last_sums[0], last_parts)
+    first_sum = column_sum(first_total, 1)
+    last_sum = column_sum(last_total, 1)
+    grad_normed = grad_normed - pick(normed_low, level, 0).astype(F32)
+    arrived = lax.psum_scatter(
+        hold([normed_low.reshape(length, width)], part_sums[-1])[0],
+        "dp",
+        scatter_dimension=0,
+        tiled=True,
+    )
+    grad_normed = grad_normed + arrived.astype(F32)
+    grad_inputs = norm_backward(grad_normed, scaled_one, inverse_one, gain_one) + grad_middle
+    attn_sum = jnp.concatenate([first_sum, last_sum], -1)
+    router_sum = small_sum[:router_size].reshape(dense_rows, specialist_total)
+    gain_sum = small_sum[router_size:small_size].reshape(2, dense_rows)
 
     local_squares = (
         jnp.sum(attn_sum * attn_sum)
@@ -806,6 +988,8 @@
     spread = jnp.broadcast_to(local_squares, (everyone, 8, 128))
     squares = lax.all_to_all(spread, ("dp", "expert"), 0, 0, tiled=True)
     grad_norm = jnp.sqrt(jnp.sum(squares[:, 0, 0]))
+    routed = add_up(routed_sums[0], hold(routed_parts, squares))
+    block_out = (middle + shared_out + routed).astype(BF16)
     scale = jnp.minimum(1.0, CLIP_VALUE / (grad_norm + 1e-06))
     attn_new, attn_moment, attn_square = adam(
         mixer_projection_matrices,

time: 915 us -> 756 us (0.83)
  waiting for transfers between devices: 392 us -> 238 us
  Pallas kernels: 214 us -> 239 us
  matrix products: 23.3 us -> 9.3 us
    ppermute x3 -> x0, waiting for transfers between devices: 93.1 us -> none  [shift(): lax.ppermute(value, 'dp', [(i, i + step) for i in range(size) if 0 <= i +...]
    ppermute x40 -> x41, waiting for transfers between devices: 215 us -> 151 us  [swap(): return lax.ppermute(value, 'expert', [(i, i ^ mask) for i in range(size)])]
    pallas_call x0 -> x19, Pallas kernels: none -> 29.2 us  [the longest x1 16.4 us: normed_grad(): pl.pallas_call(functools.partial(normed_grad_kernel, len(grads), len(wait...]
    dot_general x15 -> x6, matrix products: 23.3 us -> 9.3 us  [contract(): lax.dot_general(left, right, (((left_dim,), (right_dim,)), ((), ())), pre...]
    concatenate x3 -> x7, other arithmetic: 1.49 us -> 14.1 us  [the longest x1 6.57 us: body(): expert_part = jnp.concatenate([expert_part, shared_total], 2)]
    convert_element_type x2 -> x0, local copies, waits for them, and re-layouts: 11.9 us -> none  [the longest x1 8.41 us: body(): jnp.concatenate([by_owner(projection_grad).reshape(deep, groups, 3 * dens...]
    unnamed x130 -> x163, local copies, waits for them, and re-layouts: 8.56 us -> 20.1 us
    pallas_call x1 -> x2, Pallas kernels: 38.9 us -> 33.5 us  [attention_grad(): pl.pallas_call(attention_grad_kernel, grid_spec=pltpu.PrefetchScalarGridS...]
  transfers between devices with their start and end apart: 62 -> 59, of which waited for: 27 -> 24; matrix products, arithmetic and copies ran while one was open for 19% -> 22% of each run, Pallas kernels for 24% -> 32%
where the time goes in v3:
time: 756 us; the launch traced here: 751 us
  Pallas kernels  239 us (32%)
  waiting for transfers between devices  238 us (31%)
  other arithmetic  118 us (16%)
  local copies, waits for them, and re-layouts  63 us (8%)
  starting transfers between devices  62.8 us (8%)
  between operations  20.8 us (3%)
  matrix products  9.3 us (1%)
    ppermute x41, waiting for transfers between devices, swap(): return lax.ppermute(value, 'expert', [(i, i ^ mask) for i in range(size)])  151 us
    pallas_call x2, Pallas kernels, expert_pass(): pl.pallas_call(functools.partial(expert_kernel, before is not None, split...  92.8 us
    pallas_call x2, Pallas kernels, expert_grad(): pl.pallas_call(expert_grad_kernel, grid=(width // span,), in_specs=[stack...  45.1 us
    all_gather x1, waiting for transfers between devices, body(): attn_column = lax.all_gather(attn_own, 'dp')  39.2 us
    ppermute x41, starting transfers between devices, swap(): return lax.ppermute(value, 'expert', [(i, i ^ mask) for i in range(size)])  36.9 us
    pallas_call x2, Pallas kernels, attention_grad(): pl.pallas_call(attention_grad_kernel, grid_spec=pltpu.PrefetchScalarGridS...  33.5 us
    unnamed x163, local copies, waits for them, and re-layouts  20.1 us
    pallas_call x1, Pallas kernels, attention(): pl.pallas_call(attention_kernel, grid_spec=pltpu.PrefetchScalarGridSpec(n...  19.6 us
  transfers between devices with their start and end apart: 59, of which 24 were waited for; matrix products, arithmetic and copies ran while one was open for 22% of the time, Pallas kernels for 32%

profile of v3, /device:TPU:0, one launch (start us, length us, event | category | flops | bytes accessed | tf_op | source)
XLA Modules:
  0.0 751.0 jit_solution(5248503765254748801)
XLA Ops:
  11.9 39.2 %all-gather.9.cloned.1.call-done = bf16[16,40,1280]{2,1,0:T(8,128)(2,1)} async-done(((bf16[4,40,1280]{2,1,0:T(8,128)(2,1)}), bf16[16,40,1280]{2,1,0:T(8,128)(2,1)}) %all-gather.9.cloned.1.call-update) | async-done | bytes 1638416 | tf_op jit(solution)/shard_map/all_gather | solution.py:742
  56.1 3.6 convert_element_type.448
  61.7 21.7 %collective-permute-done.2 = bf16[4,3,40,1280]{3,2,1,0:T(8,128)(2,1)S(1)} collective-permute-done((bf16[4,3,40,1280]{3,2,1,0:T(8,128)(2,1)S(1)}, bf16[4,3,40,1280]{3,2,1,0:T(8,128)(2,1)S(1)}, u32[]{:S(2)}, u32[]{:S(2)}) %collective-permute-start.2) | collective-permute-done | bytes 1228832 | tf_op jit(solution)/shard_map/ppermute | solution.py:88
  83.5 25.1 %collective-permute-done.1 = bf16[4,3,40,1280]{3,2,1,0:T(8,128)(2,1)S(1)} collective-permute-done((bf16[4,3,40,1280]{3,2,1,0:T(8,128)(2,1)S(1)}, bf16[4,3,40,1280]{3,2,1,0:T(8,128)(2,1)S(1)}, u32[]{:S(2)}, u32[]{:S(2)}) %collective-permute-start.1) | collective-permute-done | bytes 1228832 | tf_op jit(solution)/shard_map/ppermute | solution.py:88
  109.6 12.3 %all-gather.11.cloned.1.call-done = bf16[1376,1280]{1,0:T(8,128)(2,1)} async-done(((bf16[344,1280]{1,0:T(8,128)(2,1)}), bf16[1376,1280]{1,0:T(8,128)(2,1)}) %all-gather.11.cloned.1.call-update) | async-done | bytes 3522576 | tf_op jit(solution)/shard_map/all_gather | solution.py:747
  121.8 3.4 slice.118
  130.3 8.2 %collective-permute-done.3.odd = bf16[4,4,3,40,1280]{4,3,2,1,0:T(8,128)(2,1)S(1)} collective-permute-done((bf16[4,4,3,40,1280]{4,3,2,1,0:T(8,128)(2,1)S(1)}, bf16[4,4,3,40,1280]{4,3,2,1,0:T(8,128)(2,1)S(1)}, u32[]{:S(2)}, u32[]{:S(2)}) %collective-permute-start.3) | collective-permute-done | bytes 4915232 | tf_op jit(solution)/shard_map/ppermute | solution.py:88
  141.7 3.4 all-to-all-start
  153.4 6.5 collective-permute-done.9
  159.8 8.3 %collective-permute-done.8 = bf16[4,1,40,1280]{3,2,0,1:T(8,128)(2,1)S(1)} collective-permute-done((bf16[4,1,40,1280]{3,2,0,1:T(8,128)(2,1)S(1)}, bf16[4,1,40,1280]{3,2,0,1:T(8,128)(2,1)S(1)}, u32[]{:S(2)}, u32[]{:S(2)}) %collective-permute-start.8) | collective-permute-done | bytes 409632 | tf_op jit(solution)/shard_map/ppermute | solution.py:88
  174.3 7.9 %assemble.3 = bf16[3,4,8,40,1280]{4,3,2,1,0:T(8,128)(2,1)} custom-call(s32[1]{0:T(128)} %bitcast.7.place_ref, bf16[4,4,3,40,1280]{4,3,2,1,0:T(8,128)(2,1)} %copy-done.4, bf16[4,4,3,40,1280]{4,3,2,1,0:T(8,128)(2,1)} %copy-done.35), custom_call_target="tpu_custom_call" | custom-call | flops 1 | bytes 1 | tf_op jit(solution)/shard_map/assemble/pallas_call | solution.py:204
  187.8 4.3 assemble.4
  192.1 19.6 %attention_forward.1 = (bf16[256,1280]{1,0:T(8,128)(2,1)}, bf16[1024,1280]{1,0:T(8,128)(2,1)}, bf16[1024,1280]{1,0:T(8,128)(2,1)}, f32[256,1280]{1,0:T(8,128)}, bf16[256,1280]{1,0:T(8,128)(2,1)}) custom-call(s32[1]{0:T(128)} %bitcast.1.place_ref, bf16[1024,1280]{1,0:T(8,128)(2,1)} %multiply_convert_fusion.normed, bf16[3,1280,1280]{2,1,0:T(8,128)(2,1)} %bitcast.299, ...), custom_call_target="tpu_custom_call" | custom-call | flops 1 | bytes 1 | tf_op jit(solution)/shard_map/attention_forward/pallas_call | solution.py:272
  223.7 12.9 %collective-permute-done.13 = bf16[256,1280]{1,0:T(8,128)(2,1)S(1)} collective-permute-done((bf16[256,1280]{1,0:T(8,128)(2,1)S(1)}, bf16[256,1280]{1,0:T(8,128)(2,1)S(1)}, u32[]{:S(2)}, u32[]{:S(2)}) %collective-permute-start.13) | collective-permute-done | bytes 655392 | tf_op jit(solution)/shard_map/ppermute | solution.py:88
  236.7 13.1 %collective-permute-done.12 = bf16[256,1280]{1,0:T(8,128)(2,1)S(1)} collective-permute-done((bf16[256,1280]{1,0:T(8,128)(2,1)S(1)}, bf16[256,1280]{1,0:T(8,128)(2,1)S(1)}, u32[]{:S(2)}, u32[]{:S(2)}) %collective-permute-start.12) | collective-permute-done | bytes 655392 | tf_op jit(solution)/shard_map/ppermute | solution.py:88
  270.6 44.5 %expert_pass.2 = (f32[2048,1280]{1,0:T(8,128)}, f32[2048,1280]{1,0:T(8,128)}, f32[2048,1]{1,0:T(8,128)}, bf16[2048,896]{1,0:T(8,128)(2,1)}, bf16[2048,1792]{1,0:T(8,128)(2,1)}) custom-call(bf16[4,256,1280]{2,1,0:T(8,128)(2,1)} %collective-permute-done.14.__1_.refs_0_.odd_n, bf16[4,256,1280]{2,1,0:T(8,128)(2,1)} %pad_maximum_fusion.5.refs_1_.even_n, ...), custom_call_target="tpu_custom_call" | custom-call | flops 1 | bytes 1 | tf_op jit(solution)/shard_map/expert_pass/pallas_call | solution.py:579
  315.2 3.3 pad_maximum_fusion.3.__0_
  318.6 22.5 %expert_weight_grad.2.__1_ = bf16[3,1280,896]{2,1,0:T(8,128)(2,1)} custom-call(bf16[4,256,1280]{2,1,0:T(8,128)(2,1)} %collective-permute-done.14.__1_.refs_0_.odd_n, bf16[4,256,1280]{2,1,0:T(8,128)(2,1)} %pad_maximum_fusion.5.refs_1_.even_n, bf16[4,256,1280]{2,1,0:T(8,128)(2,1)} %collective-permute-done.15.refs_2_.odd_c, bf16[4,256,1280]{2,1,0:T(8,128)(2,1)} %copy-done, ...), custom_call_target="tpu_custom_call" | custom-call | flops 1 | bytes 1 | tf_op jit(solution)/shard_map/expert_weight_grad/pallas_call | solution.py:660
  341.2 6.5 assemble.5
  347.7 12.7 %shared_pass.1 = (f32[256,1280]{1,0:T(8,128)}, f32[256,1280]{1,0:T(8,128)}, bf16[3,16,40,896]{3,2,1,0:T(8,128)(2,1)}, bf16[3,16,40,896]{3,2,1,0:T(8,128)(2,1)}) custom-call(s32[1]{0:T(128)S(6)} %select_n.174.place_ref, bf16[256,1280]{1,0:T(8,128)(2,1)} %copy-done.19, bf16[256,1280]{1,0:T(8,128)(2,1)} %bitcast.321, bf16[3,1280,896]{2,1,0:T(8,128)(2,1)} %bitcast.310), custom_call_target="tpu_custom_call" | custom-call | flops 1 | bytes 1 | tf_op jit(solution)/shard_map/shared_pass/pallas_call | solution.py:620
  360.9 6.0 collective-permute-done.20
  367.0 4.3 fusion.39
  371.3 3.7 all-gather.15.cloned.1.call-done
  384.6 48.2 %expert_pass.3 = (bf16[4,256,1280]{2,1,0:T(8,128)(2,1)}, bf16[4,256,1280]{2,1,0:T(8,128)(2,1)}, bf16[4,256,1280]{2,1,0:T(8,128)(2,1)}, bf16[4,256,1280]{2,1,0:T(...) custom-call(bf16[4,256,1280]{2,1,0:T(8,128)(2,1)} %collective-permute-done.14.__1_.refs_0_.odd, ...), custom_call_target="tpu_custom_call" | custom-call | flops 1 | bytes 1 | tf_op jit(solution)/shard_map/expert_pass/pallas_call | solution.py:579
  433.0 5.1 collective-permute-done.24
  444.7 3.7 all-to-all-start.2
  449.1 4.1 all-to-all-done.2
  462.6 22.6 %expert_weight_grad.3 = bf16[3,1280,896]{2,1,0:T(8,128)(2,1)} custom-call(bf16[4,256,1280]{2,1,0:T(8,128)(2,1)} %collective-permute-done.14.__1_.refs_0_.odd_n, bf16[4,256,1280]{2,1,0:T(8,128)(2,1)} %pad_maximum_fusion.5.refs_1_.even_n, bf16[4,256,1280]{2,1,0:T(8,128)(2,1)} %collective-permute-done.15.refs_2_.odd_c, bf16[4,256,1280]{2,1,0:T(8,128)(2,1)} %copy-done, ...), custom_call_target="tpu_custom_call" | custom-call | flops 1 | bytes 1 | tf_op jit(solution)/shard_map/expert_weight_grad/pallas_call | solution.py:660
  485.2 6.6 fusion.2.__3_
  499.0 19.1 %attention_backward.2 = (bf16[3,16,40,768]{3,2,1,0:T(8,128)(2,1)}, bf16[3,16,40,768]{3,2,1,0:T(8,128)(2,1)}, bf16[256,768]{1,0:T(8,128)(2,1)}, bf16[1024,768]{1,0:T(8,128)(2,1)}, bf16[1024,768]{1,0:T(8,128)(2,1)}) custom-call(s32[2]{0:T(128)} %pad_add_fusion.place_ref, bf16[1280,1024]{1,0:T(8,128)(2,1)} %copy.318.refs_6_.turned_normed, ...), custom_call_target="tpu_custom_call" | custom-call | flops 32212254720 | bytes 1 | tf_op jit(solution)/shard_map/attention_backward/pallas_call | solution.py:367
  520.9 14.4 %attention_backward.3 = (bf16[3,16,40,512]{3,2,1,0:T(8,128)(2,1)}, bf16[3,16,40,512]{3,2,1,0:T(8,128)(2,1)}, bf16[256,512]{1,0:T(8,128)(2,1)}, bf16[1024,512]{1,0:T(8,128)(2,1)}, bf16[1024,512]{1,0:T(8,128)(2,1)}) custom-call(s32[2]{0:T(128)} %pad_add_fusion.place_ref, bf16[1280,1024]{1,0:T(8,128)(2,1)} %copy.318.refs_6_.turned_normed, ...), custom_call_target="tpu_custom_call" | custom-call | flops 21474836480 | bytes 1 | tf_op jit(solution)/shard_map/attention_backward/pallas_call | solution.py:367
  535.8 3.9 dynamic-slice_bitcast_fusion.1
  563.0 16.4 %normed_grad.1 = (bf16[4,256,1280]{2,1,0:T(8,128)(2,1)}, f32[256,1280]{1,0:T(8,128)}, f32[1,1280]{1,0:T(1,128)}) custom-call(s32[1]{0:T(128)} %bitcast.81.refs_0_, bf16[1024,1280]{1,0:T(8,128)(2,1)} %bitcast.323, bf16[3,1280,1280]{2,1,0:T(8,128)(2,1)} %bitcast.302, bf16[256,768]{1,0:T(8,128)(2,1)} %get-tuple-element.131.refs_3_, ...), custom_call_target="tpu_custom_call" | custom-call | flops 40265318400 | bytes 1 | tf_op jit(solution)/shard_map/normed_grad/pallas_call | solution.py:450
  579.4 5.8 collective-permute-done.34.__5_.__2_
  585.2 19.8 %collective-permute-done.33.__4_.__1_ = bf16[4,4,40,768]{3,2,1,0:T(8,128)(2,1)S(1)} collective-permute-done((bf16[4,4,40,768]{3,2,1,0:T(8,128)(2,1)}, bf16[4,4,40,768]{3,2,1,0:T(8,128)(2,1)S(1)}, u32[]{:S(2)}, u32[]{:S(2)}) %collective-permute-start.33) | collective-permute-done | bytes 983072 | tf_op jit(solution)/shard_map/ppermute | solution.py:88
  605.9 4.4 fusion.90
  620.4 5.0 all-to-all-start.3
  625.4 3.5 copy.426.__0_
  628.8 3.6 collective-permute-start.43
  633.1 11.6 %collective-permute-done.36.__4_.__2_ = bf16[4,4,40,512]{3,2,1,0:T(8,128)(2,1)S(1)} collective-permute-done((bf16[4,4,40,512]{3,2,1,0:T(8,128)(2,1)}, bf16[4,4,40,512]{3,2,1,0:T(8,128)(2,1)S(1)}, u32[]{:S(2)}, u32[]{:S(2)}) %collective-permute-start.36) | collective-permute-done | bytes 655392 | tf_op jit(solution)/shard_map/ppermute | solution.py:88
  649.9 12.7 %collective-permute-done.42 = bf16[4,40,768]{2,1,0:T(8,128)(2,1)S(1)} collective-permute-done((bf16[4,40,768]{2,1,0:T(8,128)(2,1)}, bf16[4,40,768]{2,1,0:T(8,128)(2,1)S(1)}, u32[]{:S(2)}, u32[]{:S(2)}) %collective-permute-start.42) | collective-permute-done | bytes 245792 | tf_op jit(solution)/shard_map/ppermute | solution.py:93
  671.4 5.1 collective-permute-done.45
  684.5 4.0 fusion.4
  689.9 5.0 all-to-all-start.4
  695.0 3.6 collective-permute-done.39.__1_
  698.6 7.6 %all-to-all-done.4.__3_ = f32[32,8,128]{2,1,0:T(8,128)} async-done(((f32[32,8,128]{2,1,0:T(8,128)}), f32[32,8,128]{2,1,0:T(8,128)}, u32[]{:S(2)}, u32[]{:S(2)}) %all-to-all-start.4) | async-done | bytes 131104 | tf_op jit(solution)/shard_map/all_to_all | solution.py:989
  715.4 3.4 fusion.50
  718.9 18.0 %fusion.79 = (bf16[2,3,320,896]{3,2,1,0:T(8,128)(2,1)}, f32[2,3,320,896]{3,2,1,0:T(8,128)}, f32[2,3,320,896]{3,2,1,0:T(8,128)}, f32[2,3,320,896]{3,2,1,0:T(8,128)}) fusion(f32[2,3,320,896]{3,2,1,0:T(8,128)} %param.39, f32[]{:T(128)S(6)} %min.3, bf16[1,3,320,896]{3,2,1,0:T(8,128)(2,1)S(1)} %copy-done.10, bf16[1,3,320,896]{3,2,1,0:T(8,128)(2,1)S(1)} %bitcast.332, ...), kind=kLoop, calls=%fused_computation.210 | loop fusion | flops 32686080 | bytes 48168964 | tf_op jit(solution)/shard_map/convert_element_type | solution.py:1056
  (405 shorter events, 180.1 us)
Async XLA Ops:
  7.2 43.9 %all-gather.9.cloned.1.call-start = ((), (), s32[]{:S(2)}) async-start(), calls=%async_computation.11 | async-start | bytes 2048000 | tf_op jit(solution)/shard_map/all_gather | solution.py:742
  9.3 112.6 %all-gather.11.cloned.1.call-start = ((), (), s32[]{:S(2)}) async-start(), calls=%async_computation.12 | async-start | bytes 4403200 | tf_op jit(solution)/shard_map/all_gather | solution.py:747
  51.1 214.3 %all-gather.13.cloned.1.call-start = ((), (), s32[]{:S(2)}) async-start(), calls=%async_computation.13 | async-start | bytes 8601600 | tf_op jit(solution)/shard_map/all_gather | solution.py:758
  52.5 30.9 %collective-permute-start.2 = (bf16[4,3,40,1280]{3,2,1,0:T(8,128)(2,1)S(1)}, bf16[4,3,40,1280]{3,2,1,0:T(8,128)(2,1)S(1)}, u32[]{:S(2)}, u32[]{:S(2)}) collective-permute-start(bf16[4,3,40,1280]{3,2,1,0:T(8,128)(2,1)S(1)} %slice.159), channel_id=1, source_target_pairs={{0,6},{1,7},{2,4},{3,5},{4,2},{5,3},{6,0},{7,1},{8,14},{9,15},{10,... | collective-permute-start | bytes 3686408 | tf_op jit(solution)/shard_map/ppermute | solution.py:88
  55.0 53.5 %collective-permute-start.1 = (bf16[4,3,40,1280]{3,2,1,0:T(8,128)(2,1)S(1)}, bf16[4,3,40,1280]{3,2,1,0:T(8,128)(2,1)S(1)}, u32[]{:S(2)}, u32[]{:S(2)}) collective-permute-start(bf16[4,3,40,1280]{3,2,1,0:T(8,128)(2,1)S(1)} %slice.159), channel_id=1, source_target_pairs={{0,4},{1,5},{2,6},{3,7},{4,0},{5,1},{6,2},{7,3},{8,12},{9,13},{10,... | collective-permute-start | bytes 3686408 | tf_op jit(solution)/shard_map/ppermute | solution.py:88
  55.5 54.0 %collective-permute-start = (bf16[4,3,40,1280]{3,2,1,0:T(8,128)(2,1)S(1)}, bf16[4,3,40,1280]{3,2,1,0:T(8,128)(2,1)}, u32[]{:S(2)}, u32[]{:S(2)}) collective-permute-start(bf16[4,3,40,1280]{3,2,1,0:T(8,128)(2,1)S(1)} %slice.159), channel_id=1, source_target_pairs={{0,2},{1,3},{2,0},{3,1},{4,6},{5,7},{6,4},{7,5},{8,10},{9,11},{10,... | collective-permute-start | bytes 3686408 | tf_op jit(solution)/shard_map/ppermute | solution.py:88
  125.2 249.7 %all-gather.15.cloned.1.call-start = ((), (), s32[]{:S(2)}) async-start(), calls=%async_computation.14 | async-start | bytes 8601600 | tf_op jit(solution)/shard_map/all_gather | solution.py:764
  141.7 29.8 %all-to-all-start = ((bf16[32,8,128]{2,1,0:T(8,128)(2,1)}), bf16[32,8,128]{2,1,0:T(8,128)(2,1)S(1)}, u32[]{:S(2)}, u32[]{:S(2)}) async-start(bf16[32,8,128]{2,1,0:T(8,128)(2,1)} %broadcast_in_dim.26), calls=%async_computation | async-start | bytes 131072 | tf_op jit(solution)/shard_map/all_to_all | solution.py:724
  149.0 19.1 %collective-permute-start.8 = (bf16[4,1,40,1280]{3,2,0,1:T(8,128)(2,1)S(1)}, bf16[4,1,40,1280]{3,2,0,1:T(8,128)(2,1)S(1)}, u32[]{:S(2)}, u32[]{:S(2)}) collective-permute-start(bf16[4,1,40,1280]{3,2,0,1:T(8,128)(2,1)S(1)} %slice_bitcast_fusion.4), channel_id=1, source_target_pairs={{0,4},{1,5},{2,6},{3,7},{4,0},{5,1},{6,2},{7,3},{8,12},{9,13},{10,... | collective-permute-start | bytes 1228808 | tf_op jit(solution)/shard_map/ppermute | solution.py:88
  149.5 18.6 %collective-permute-start.7 = (bf16[4,1,40,1280]{3,2,0,1:T(8,128)(2,1)S(1)}, bf16[4,1,40,1280]{3,2,0,1:T(8,128)(2,1)S(1)}, u32[]{:S(2)}, u32[]{:S(2)}) collective-permute-start(bf16[4,1,40,1280]{3,2,0,1:T(8,128)(2,1)S(1)} %slice_bitcast_fusion.4), channel_id=1, source_target_pairs={{0,2},{1,3},{2,0},{3,1},{4,6},{5,7},{6,4},{7,5},{8,10},{9,11},{10,... | collective-permute-start | bytes 1228808 | tf_op jit(solution)/shard_map/ppermute | solution.py:88
  169.6 18.3 %collective-permute-start.10 = (bf16[4,4,1,40,1280]{4,3,2,1,0:T(8,128)(2,1)}, bf16[4,4,1,40,1280]{4,3,2,1,0:T(8,128)(2,1)}, u32[]{:S(2)}, u32[]{:S(2)}) collective-permute-start(bf16[4,4,1,40,1280]{4,3,2,1,0:T(8,128)(2,1)} %pad_maximum_fusion.9.even), channel_id=1, source_target_pairs={{0,1},{1,0},{2,3},{3,2},{4,5},{5,4},{6,7},{7,6},{8,9},{9,8},{10,11... | collective-permute-start | bytes 4915208 | tf_op jit(solution)/shard_map/ppermute | solution.py:88
  182.2 29.5 %collective-permute-start.6 = (bf16[256,1280]{1,0:T(8,128)(2,1)}, bf16[256,1280]{1,0:T(8,128)(2,1)}, u32[]{:S(2)}, u32[]{:S(2)}) collective-permute-start(bf16[256,1280]{1,0:T(8,128)(2,1)} %hold.17), channel_id=1, source_target_pairs={{0,6},{1,7},{2,4},{3,5},{4,2},{5,3},{6,0},{7,1},{8,14},{9,15},{10,... | collective-permute-start | bytes 1966088 | tf_op jit(solution)/shard_map/ppermute | solution.py:88
  183.7 30.9 %collective-permute-start.5 = (bf16[256,1280]{1,0:T(8,128)(2,1)}, bf16[256,1280]{1,0:T(8,128)(2,1)}, u32[]{:S(2)}, u32[]{:S(2)}) collective-permute-start(bf16[256,1280]{1,0:T(8,128)(2,1)} %hold.17), channel_id=1, source_target_pairs={{0,4},{1,5},{2,6},{3,7},{4,0},{5,1},{6,2},{7,3},{8,12},{9,13},{10,... | collective-permute-start | bytes 1966088 | tf_op jit(solution)/shard_map/ppermute | solution.py:88
  185.2 29.4 %collective-permute-start.4 = (bf16[256,1280]{1,0:T(8,128)(2,1)}, bf16[256,1280]{1,0:T(8,128)(2,1)}, u32[]{:S(2)}, u32[]{:S(2)}) collective-permute-start(bf16[256,1280]{1,0:T(8,128)(2,1)} %hold.17), channel_id=1, source_target_pairs={{0,2},{1,3},{2,0},{3,1},{4,6},{5,7},{6,4},{7,5},{8,10},{9,11},{10,... | collective-permute-start | bytes 1966088 | tf_op jit(solution)/shard_map/ppermute | solution.py:88
  218.1 18.6 %collective-permute-start.13 = (bf16[256,1280]{1,0:T(8,128)(2,1)S(1)}, bf16[256,1280]{1,0:T(8,128)(2,1)S(1)}, u32[]{:S(2)}, u32[]{:S(2)}) collective-permute-start(bf16[256,1280]{1,0:T(8,128)(2,1)S(1)} %multiply_convert_fusion.1.tokens_ref), channel_id=1, source_target_pairs={{0,6},{1,7},{2,4},{3,5},{4,2},{5,3},{6,0},{7,1},{8,14},{9,15},{10,... | collective-permute-start | bytes 1966088 | tf_op jit(solution)/shard_map/ppermute | solution.py:88
  219.7 30.1 %collective-permute-start.12 = (bf16[256,1280]{1,0:T(8,128)(2,1)S(1)}, bf16[256,1280]{1,0:T(8,128)(2,1)S(1)}, u32[]{:S(2)}, u32[]{:S(2)}) collective-permute-start(bf16[256,1280]{1,0:T(8,128)(2,1)S(1)} %multiply_convert_fusion.1.tokens_ref), channel_id=1, source_target_pairs={{0,4},{1,5},{2,6},{3,7},{4,0},{5,1},{6,2},{7,3},{8,12},{9,13},{10,... | collective-permute-start | bytes 1966088 | tf_op jit(solution)/shard_map/ppermute | solution.py:88
  221.1 28.7 %collective-permute-start.11 = (bf16[256,1280]{1,0:T(8,128)(2,1)S(1)}, bf16[256,1280]{1,0:T(8,128)(2,1)S(1)}, u32[]{:S(2)}, u32[]{:S(2)}) collective-permute-start(bf16[256,1280]{1,0:T(8,128)(2,1)S(1)} %multiply_convert_fusion.1.tokens_ref), channel_id=1, source_target_pairs={{0,2},{1,3},{2,0},{3,1},{4,6},{5,7},{6,4},{7,5},{8,10},{9,11},{10,... | collective-permute-start | bytes 1966088 | tf_op jit(solution)/shard_map/ppermute | solution.py:88
  223.5 41.9 %collective-permute-start.15 = (bf16[4,256,1280]{2,1,0:T(8,128)(2,1)S(1)}, bf16[4,256,1280]{2,1,0:T(8,128)(2,1)}, u32[]{:S(2)}, u32[]{:S(2)}) collective-permute-start(bf16[4,256,1280]{2,1,0:T(8,128)(2,1)S(1)} %pad_maximum_fusion.6.refs_3_.even_c), channel_id=1, source_target_pairs={{0,1},{1,0},{2,3},{3,2},{4,5},{5,4},{6,7},{7,6},{8,9},{9,8},{10,11... | collective-permute-start | bytes 7864328 | tf_op jit(solution)/shard_map/ppermute | solution.py:88
  258.7 262.2 %reduce-scatter.4.cloned.1.call-start = ((), (), s32[]{:S(2)}) async-start(), calls=%async_computation.8 | async-start | bytes 8601600 | tf_op jit(solution)/shard_map/reduce_scatter | solution.py:872
  265.4 49.8 %collective-permute-start.18 = (bf16[4,3,40,896]{3,2,1,0:T(8,128)(2,1)}, bf16[4,3,40,896]{3,2,1,0:T(8,128)(2,1)S(1)}, u32[]{:S(2)}, u32[]{:S(2)}) collective-permute-start(bf16[4,3,40,896]{3,2,1,0:T(8,128)(2,1)} %hold.19), channel_id=1, source_target_pairs={{0,6},{1,7},{2,4},{3,5},{4,2},{5,3},{6,0},{7,1},{8,14},{9,15},{10,... | collective-permute-start | bytes 2580488 | tf_op jit(solution)/shard_map/ppermute | solution.py:88
  266.8 48.3 %collective-permute-start.17 = (bf16[4,3,40,896]{3,2,1,0:T(8,128)(2,1)}, bf16[4,3,40,896]{3,2,1,0:T(8,128)(2,1)S(1)}, u32[]{:S(2)}, u32[]{:S(2)}) collective-permute-start(bf16[4,3,40,896]{3,2,1,0:T(8,128)(2,1)} %hold.19), channel_id=1, source_target_pairs={{0,4},{1,5},{2,6},{3,7},{4,0},{5,1},{6,2},{7,3},{8,12},{9,13},{10,... | collective-permute-start | bytes 2580488 | tf_op jit(solution)/shard_map/ppermute | solution.py:88
  267.5 47.7 %collective-permute-start.16 = (bf16[4,3,40,896]{3,2,1,0:T(8,128)(2,1)}, bf16[4,3,40,896]{3,2,1,0:T(8,128)(2,1)}, u32[]{:S(2)}, u32[]{:S(2)}) collective-permute-start(bf16[4,3,40,896]{3,2,1,0:T(8,128)(2,1)} %hold.19), channel_id=1, source_target_pairs={{0,2},{1,3},{2,0},{3,1},{4,6},{5,7},{6,4},{7,5},{8,10},{9,11},{10,... | collective-permute-start | bytes 2580488 | tf_op jit(solution)/shard_map/ppermute | solution.py:88
  318.6 22.6 %collective-permute-start.19 = (bf16[4,4,3,40,896]{4,3,2,1,0:T(8,128)(2,1)}, bf16[4,4,3,40,896]{4,3,2,1,0:T(8,128)(2,1)}, u32[]{:S(2)}, u32[]{:S(2)}) collective-permute-start(bf16[4,4,3,40,896]{4,3,2,1,0:T(8,128)(2,1)} %hold.20.even), channel_id=1, source_target_pairs={{0,1},{1,0},{2,3},{3,2},{4,5},{5,4},{6,7},{7,6},{8,9},{9,8},{10,11... | collective-permute-start | bytes 10321928 | tf_op jit(solution)/shard_map/ppermute | solution.py:88
  375.0 57.9 %collective-permute-start.21 = (bf16[3,4,40,896]{3,2,1,0:T(8,128)(2,1)}, bf16[3,4,40,896]{3,2,1,0:T(8,128)(2,1)}, u32[]{:S(2)}, u32[]{:S(2)}) collective-permute-start(bf16[3,4,40,896]{3,2,1,0:T(8,128)(2,1)} %get-tuple-element.106), channel_id=1, source_target_pairs={{0,2},{1,3},{2,0},{3,1},{4,6},{5,7},{6,4},{7,5},{8,10},{9,11},{10,... | collective-permute-start | bytes 2580488 | tf_op jit(solution)/shard_map/ppermute | solution.py:88
  376.4 56.5 %collective-permute-start.22 = (bf16[3,4,40,896]{3,2,1,0:T(8,128)(2,1)}, bf16[3,4,40,896]{3,2,1,0:T(8,128)(2,1)}, u32[]{:S(2)}, u32[]{:S(2)}) collective-permute-start(bf16[3,4,40,896]{3,2,1,0:T(8,128)(2,1)} %get-tuple-element.107), channel_id=1, source_target_pairs={{0,4},{1,5},{2,6},{3,7},{4,0},{5,1},{6,2},{7,3},{8,12},{9,13},{10,... | collective-permute-start | bytes 2580488 | tf_op jit(solution)/shard_map/ppermute | solution.py:88
  377.9 55.0 %collective-permute-start.23 = (bf16[3,4,40,896]{3,2,1,0:T(8,128)(2,1)}, bf16[3,4,40,896]{3,2,1,0:T(8,128)(2,1)}, u32[]{:S(2)}, u32[]{:S(2)}) collective-permute-start(bf16[3,4,40,896]{3,2,1,0:T(8,128)(2,1)} %get-tuple-element.108), channel_id=1, source_target_pairs={{0,6},{1,7},{2,4},{3,5},{4,2},{5,3},{6,0},{7,1},{8,14},{9,15},{10,... | collective-permute-start | bytes 2580488 | tf_op jit(solution)/shard_map/ppermute | solution.py:88
  440.3 20.8 %collective-permute-start.25 = (bf16[4,256,1280]{2,1,0:T(8,128)(2,1)}, bf16[4,256,1280]{2,1,0:T(8,128)(2,1)S(1)}, u32[]{:S(2)}, u32[]{:S(2)}) collective-permute-start(bf16[4,256,1280]{2,1,0:T(8,128)(2,1)} %hold.24), channel_id=1, source_target_pairs={{0,1},{1,0},{2,3},{3,2},{4,5},{5,4},{6,7},{7,6},{8,9},{9,8},{10,11... | collective-permute-start | bytes 7864328 | tf_op jit(solution)/shard_map/ppermute | solution.py:88
  448.5 229.9 %reduce-scatter.6.cloned.1.call-start = ((), (), s32[]{:S(2)}) async-start(), calls=%async_computation.9 | async-start | bytes 9891840 | tf_op jit(solution)/shard_map/reduce_scatter | solution.py:872
  457.6 35.6 %collective-permute-start.26 = (bf16[256,1280]{1,0:T(8,128)(2,1)}, bf16[256,1280]{1,0:T(8,128)(2,1)}, u32[]{:S(2)}, u32[]{:S(2)}) collective-permute-start(bf16[256,1280]{1,0:T(8,128)(2,1)} %get-tuple-element.273.__1_), channel_id=1, source_target_pairs={{0,2},{1,3},{2,0},{3,1},{4,6},{5,7},{6,4},{7,5},{8,10},{9,11},{10,... | collective-permute-start | bytes 1966088 | tf_op jit(solution)/shard_map/ppermute | solution.py:88
  458.1 34.9 %collective-permute-start.28 = (bf16[256,1280]{1,0:T(8,128)(2,1)}, bf16[256,1280]{1,0:T(8,128)(2,1)}, u32[]{:S(2)}, u32[]{:S(2)}) collective-permute-start(bf16[256,1280]{1,0:T(8,128)(2,1)} %get-tuple-element.271), channel_id=1, source_target_pairs={{0,6},{1,7},{2,4},{3,5},{4,2},{5,3},{6,0},{7,1},{8,14},{9,15},{10,... | collective-permute-start | bytes 1966088 | tf_op jit(solution)/shard_map/ppermute | solution.py:88
  459.6 33.5 %collective-permute-start.27 = (bf16[256,1280]{1,0:T(8,128)(2,1)}, bf16[256,1280]{1,0:T(8,128)(2,1)}, u32[]{:S(2)}, u32[]{:S(2)}) collective-permute-start(bf16[256,1280]{1,0:T(8,128)(2,1)} %get-tuple-element.272), channel_id=1, source_target_pairs={{0,4},{1,5},{2,6},{3,7},{4,0},{5,1},{6,2},{7,3},{8,12},{9,13},{10,... | collective-permute-start | bytes 1966088 | tf_op jit(solution)/shard_map/ppermute | solution.py:88
  518.0 36.4 %collective-permute-start.31 = (bf16[3,16,40,768]{3,2,1,0:T(8,128)(2,1)}, bf16[3,16,40,768]{3,2,1,0:T(8,128)(2,1)}, u32[]{:S(2)}, u32[]{:S(2)}) collective-permute-start(bf16[3,16,40,768]{3,2,1,0:T(8,128)(2,1)} %get-tuple-element.121.refs_0_), channel_id=1, source_target_pairs={{0,1},{1,0},{2,3},{3,2},{4,5},{5,4},{6,7},{7,6},{8,9},{9,8},{10,11... | collective-permute-start | bytes 8847368 | tf_op jit(solution)/shard_map/ppermute | solution.py:88
  559.4 25.7 %collective-permute-start.34 = (bf16[4,4,40,768]{3,2,1,0:T(8,128)(2,1)}, bf16[4,4,40,768]{3,2,1,0:T(8,128)(2,1)S(1)}, u32[]{:S(2)}, u32[]{:S(2)}) collective-permute-start(bf16[4,4,40,768]{3,2,1,0:T(8,128)(2,1)} %get-tuple-element.262), channel_id=1, source_target_pairs={{0,6},{1,7},{2,4},{3,5},{4,2},{5,3},{6,0},{7,1},{8,14},{9,15},{10,... | collective-permute-start | bytes 2949128 | tf_op jit(solution)/shard_map/ppermute | solution.py:88
  559.9 45.1 %collective-permute-start.33 = (bf16[4,4,40,768]{3,2,1,0:T(8,128)(2,1)}, bf16[4,4,40,768]{3,2,1,0:T(8,128)(2,1)S(1)}, u32[]{:S(2)}, u32[]{:S(2)}) collective-permute-start(bf16[4,4,40,768]{3,2,1,0:T(8,128)(2,1)} %get-tuple-element.263), channel_id=1, source_target_pairs={{0,4},{1,5},{2,6},{3,7},{4,0},{5,1},{6,2},{7,3},{8,12},{9,13},{10,... | collective-permute-start | bytes 2949128 | tf_op jit(solution)/shard_map/ppermute | solution.py:88
  561.2 43.7 %collective-permute-start.32 = (bf16[4,4,40,768]{3,2,1,0:T(8,128)(2,1)}, bf16[4,4,40,768]{3,2,1,0:T(8,128)(2,1)}, u32[]{:S(2)}, u32[]{:S(2)}) collective-permute-start(bf16[4,4,40,768]{3,2,1,0:T(8,128)(2,1)} %get-tuple-element.264.refs_9_), channel_id=1, source_target_pairs={{0,2},{1,3},{2,0},{3,1},{4,6},{5,7},{6,4},{7,5},{8,10},{9,11},{10,... | collective-permute-start | bytes 2949128 | tf_op jit(solution)/shard_map/ppermute | solution.py:88
  611.2 21.2 %collective-permute-start.41 = (bf16[4,40,768]{2,1,0:T(8,128)(2,1)}, bf16[4,40,768]{2,1,0:T(8,128)(2,1)S(1)}, u32[]{:S(2)}, u32[]{:S(2)}) collective-permute-start(bf16[4,40,768]{2,1,0:T(8,128)(2,1)} %get-tuple-element.283), channel_id=1, source_target_pairs={{0,8},{8,16},{16,24},{24,0},{1,9},{9,17},{17,25},{25,1},{2,10},{10... | collective-permute-start | bytes 737288 | tf_op jit(solution)/shard_map/ppermute | solution.py:93
  611.4 21.7 %collective-permute-start.35 = (bf16[4,4,40,512]{3,2,1,0:T(8,128)(2,1)}, bf16[4,4,40,512]{3,2,1,0:T(8,128)(2,1)S(1)}, u32[]{:S(2)}, u32[]{:S(2)}) collective-permute-start(bf16[4,4,40,512]{3,2,1,0:T(8,128)(2,1)} %get-tuple-element.125), channel_id=1, source_target_pairs={{0,2},{1,3},{2,0},{3,1},{4,6},{5,7},{6,4},{7,5},{8,10},{9,11},{10,... | collective-permute-start | bytes 1966088 | tf_op jit(solution)/shard_map/ppermute | solution.py:88
  612.7 32.1 %collective-permute-start.36 = (bf16[4,4,40,512]{3,2,1,0:T(8,128)(2,1)}, bf16[4,4,40,512]{3,2,1,0:T(8,128)(2,1)S(1)}, u32[]{:S(2)}, u32[]{:S(2)}) collective-permute-start(bf16[4,4,40,512]{3,2,1,0:T(8,128)(2,1)} %get-tuple-element.126), channel_id=1, source_target_pairs={{0,4},{1,5},{2,6},{3,7},{4,0},{5,1},{6,2},{7,3},{8,12},{9,13},{10,... | collective-permute-start | bytes 1966088 | tf_op jit(solution)/shard_map/ppermute | solution.py:88
  613.4 31.4 %collective-permute-start.37 = (bf16[4,4,40,512]{3,2,1,0:T(8,128)(2,1)}, bf16[4,4,40,512]{3,2,1,0:T(8,128)(2,1)S(1)}, u32[]{:S(2)}, u32[]{:S(2)}) collective-permute-start(bf16[4,4,40,512]{3,2,1,0:T(8,128)(2,1)} %get-tuple-element.127), channel_id=1, source_target_pairs={{0,6},{1,7},{2,4},{3,5},{4,2},{5,3},{6,0},{7,1},{8,14},{9,15},{10,... | collective-permute-start | bytes 1966088 | tf_op jit(solution)/shard_map/ppermute | solution.py:88
  620.4 43.6 %all-to-all-start.3 = ((f32[32,8,128]{2,1,0:T(8,128)}), f32[32,8,128]{2,1,0:T(8,128)}, u32[]{:S(2)}, u32[]{:S(2)}) async-start(f32[32,8,128]{2,1,0:T(8,128)} %bitcast.353), calls=%async_computation.5 | async-start | bytes 262144 | tf_op jit(solution)/shard_map/all_to_all | solution.py:960
  625.3 111.6 %reduce-scatter.8.cloned.1.call-start = ((), (), s32[]{:S(2)}) async-start(), calls=%async_computation.10 | async-start | bytes 3276800 | tf_op jit(solution)/shard_map/reduce_scatter | solution.py:969
  628.8 21.1 %collective-permute-start.43 = (bf16[4,40,768]{2,1,0:T(8,128)(2,1)}, bf16[4,40,768]{2,1,0:T(8,128)(2,1)}, u32[]{:S(2)}, u32[]{:S(2)}) collective-permute-start(bf16[4,40,768]{2,1,0:T(8,128)(2,1)} %get-tuple-element.284), channel_id=1, source_target_pairs={{0,24},{8,0},{16,8},{24,16},{1,25},{9,1},{17,9},{25,17},{2,26},{10... | collective-permute-start | bytes 737288 | tf_op jit(solution)/shard_map/ppermute | solution.py:93
  633.1 29.5 %collective-permute-start.42 = (bf16[4,40,768]{2,1,0:T(8,128)(2,1)}, bf16[4,40,768]{2,1,0:T(8,128)(2,1)S(1)}, u32[]{:S(2)}, u32[]{:S(2)}) collective-permute-start(bf16[4,40,768]{2,1,0:T(8,128)(2,1)} %hold.29), channel_id=1, source_target_pairs={{0,16},{8,24},{16,0},{24,8},{1,17},{9,25},{17,1},{25,9},{2,18},{10... | collective-permute-start | bytes 737288 | tf_op jit(solution)/shard_map/ppermute | solution.py:93
  648.8 16.1 %collective-permute-start.44 = (bf16[4,40,512]{2,1,0:T(8,128)(2,1)S(1)}, bf16[4,40,512]{2,1,0:T(8,128)(2,1)S(1)}, u32[]{:S(2)}, u32[]{:S(2)}) collective-permute-start(bf16[4,40,512]{2,1,0:T(8,128)(2,1)S(1)} %get-tuple-element.286), channel_id=1, source_target_pairs={{0,8},{8,16},{16,24},{24,0},{1,9},{9,17},{17,25},{25,1},{2,10},{10... | collective-permute-start | bytes 491528 | tf_op jit(solution)/shard_map/ppermute | solution.py:93
  666.2 28.8 %collective-permute-start.38 = (bf16[256,1280]{1,0:T(8,128)(2,1)}, bf16[256,1280]{1,0:T(8,128)(2,1)}, u32[]{:S(2)}, u32[]{:S(2)}) collective-permute-start(bf16[256,1280]{1,0:T(8,128)(2,1)} %get-tuple-element.128), channel_id=1, source_target_pairs={{0,2},{1,3},{2,0},{3,1},{4,6},{5,7},{6,4},{7,5},{8,10},{9,11},{10,... | collective-permute-start | bytes 1966088 | tf_op jit(solution)/shard_map/ppermute | solution.py:88
  667.7 30.9 %collective-permute-start.39 = (bf16[256,1280]{1,0:T(8,128)(2,1)}, bf16[256,1280]{1,0:T(8,128)(2,1)}, u32[]{:S(2)}, u32[]{:S(2)}) collective-permute-start(bf16[256,1280]{1,0:T(8,128)(2,1)} %get-tuple-element.129), channel_id=1, source_target_pairs={{0,4},{1,5},{2,6},{3,7},{4,0},{5,1},{6,2},{7,3},{8,12},{9,13},{10,... | collective-permute-start | bytes 1966088 | tf_op jit(solution)/shard_map/ppermute | solution.py:88
  669.1 29.4 %collective-permute-start.40 = (bf16[256,1280]{1,0:T(8,128)(2,1)}, bf16[256,1280]{1,0:T(8,128)(2,1)}, u32[]{:S(2)}, u32[]{:S(2)}) collective-permute-start(bf16[256,1280]{1,0:T(8,128)(2,1)} %get-tuple-element.130), channel_id=1, source_target_pairs={{0,6},{1,7},{2,4},{3,5},{4,2},{5,3},{6,0},{7,1},{8,14},{9,15},{10,... | collective-permute-start | bytes 1966088 | tf_op jit(solution)/shard_map/ppermute | solution.py:88
  689.9 16.2 %all-to-all-start.4 = ((f32[32,8,128]{2,1,0:T(8,128)}), f32[32,8,128]{2,1,0:T(8,128)}, u32[]{:S(2)}, u32[]{:S(2)}) async-start(f32[32,8,128]{2,1,0:T(8,128)} %broadcast_in_dim.34), calls=%async_computation.6 | async-start | bytes 262144 | tf_op jit(solution)/shard_map/all_to_all | solution.py:989
  (88 other events, 1519.5 us)
Sparse Core Ops, SparseCore 0:
  10.2 40.8 all-gather.8
  53.2 68.5 all-gather.10
  125.4 124.9 all-gather.12
  251.8 123.1 all-gather.14
  377.7 118.5 reduce-scatter.3
  498.6 150.2 reduce-scatter.5
  678.5 54.5 reduce-scatter.7

commit v4 on v3

--- a/solution.py
+++ b/solution.py
@@ -154,18 +154,19 @@
     ]
 
 
-def column_sum(total, axis):
+def column_sum(total, axis, later, *others):
     deep, level = lax.axis_size("dp"), lax.axis_index("dp")
     low = total.astype(BF16)
     result = pick(total, level, axis)
-    arrived = low
+    parts = []
     for step in range(1, deep):
         block = pick(low, (level + step) % deep, axis)
-        if step == 2:
-            block = hold([block], arrived)[0]
-        arrived = rotate(block, step)
-        result = result + arrived.astype(F32)
-    return result
+        if later is not None and step == 2:
+            block = hold([block], later)[0]
+        parts.append(rotate(block, step))
+    if others:
+        parts = hold(parts, *others)
+    return add_up(result, parts), parts
 
 
 VMEM_LIMIT = 60 * 1024 * 1024
@@ -318,7 +319,8 @@
 
 
 def attention_grad_kernel(
-    place_ref, turned_normed, own_turned, wo, q, k, v, o, arriving, cosine, sine, starts, own_starts, *refs
+    place_ref, turned_normed, own_turned, mixed_turned, wo, q, k, v, o, arriving, arriving_columns,
+    cosine, sine, starts, own_starts, *refs
 ):
     *grads, dq_out, dk_out, dv_out = refs
     grads = grads[-2:] if len(grads[-1].shape) == 4 else grads[-1:]
@@ -346,10 +348,12 @@
     store_split(product(own_turned[...], dq_out[...], 1, 0), core, 0, grads)
     store_split(product(turned_normed[...], dk_out[...], 1, 0), core, 1, grads)
     store_split(product(turned_normed[...], dv_out[...], 1, 0), core, 2, grads)
+    store_split(product(mixed_turned[...], arriving_columns[...], 1, 0), core, 3, grads)
 
 
 def attention_grad(
-    place, turned, own_turned, wo, q, k, v, o, arriving, cosine, sine, starts, dense_rows, first, count, waits=()
+    place, turned, own_turned, mixed_turned, wo, q, k, v, o, arriving, cosine, sine, starts, dense_rows,
+    first, count, waits=(),
 ):
     width, length = turned.shape
     rows = q.shape[0]
@@ -357,7 +361,7 @@
     own_starts = lax.dynamic_slice_in_dim(starts, place, rows)[:, None]
     starts = starts[None, :]
     place = jnp.stack([place, lax.axis_index("expert") % 2])
-    shapes = split_shapes(3, width, span * count, dense_rows)
+    shapes = split_shapes(4, width, span * count, dense_rows)
     grad_specs = [
         pl.BlockSpec(shape[:-1] + (span,), lambda p, _, size=len(shape): (0,) * (size - 1) + (p,))
         for shape in shapes
@@ -372,12 +376,14 @@
             in_specs=[
                 whole(turned),
                 whole(own_turned),
+                whole(mixed_turned),
                 pl.BlockSpec((span, width), lambda p, _: (p + first, 0)),
                 blocks(rows),
                 blocks(length),
                 blocks(length),
                 blocks(rows),
                 whole(arriving),
+                blocks(rows),
                 whole(cosine),
                 whole(sine),
                 whole(starts),
@@ -393,10 +399,11 @@
             jax.ShapeDtypeStruct((length, span * count), BF16),
         ],
         compiler_params=kernel_params(1),
-        cost_estimate=pl.CostEstimate(flops=32 * rows * length * width * count, bytes_accessed=1, transcendentals=0),
+        cost_estimate=pl.CostEstimate(flops=64 * rows * length * width * count, bytes_accessed=1, transcendentals=0),
         name="attention_backward",
     )(
-        place, turned, own_turned, wo, q, k, v, o, arriving, cosine, sine, starts, own_starts, *waits
+        place, turned, own_turned, mixed_turned, wo, q, k, v, o, arriving, arriving, cosine, sine, starts,
+        own_starts, *waits
     )
 
 
@@ -465,7 +472,7 @@
             jax.ShapeDtypeStruct((1, width), F32),
         ],
         compiler_params=kernel_params(1),
-        cost_estimate=pl.CostEstimate(flops=24 * length * width * width, bytes_accessed=1, transcendentals=0),
+        cost_estimate=pl.CostEstimate(flops=48 * length * width * width, bytes_accessed=1, transcendentals=0),
         name="normed_grad",
     )(lax.axis_index("dp")[None], *operands, *waits)
 
@@ -803,7 +810,15 @@
     relative = here ^ jnp.concatenate([half + 1, half])
     gates_plane = gates_received[relative].reshape(groups * token_rows, expert_local)
 
-    tokens = gather_swaps(second)
+    turned, own_turned, mixed_turned = normed_all.T, normed.T, mixed_low.T
+    second_fan = fan(second)
+    second_even = jnp.stack(
+        list(second_fan[:1])
+        + list(hold(
+            second_fan[1:], shared_column, turned, own_turned, mixed_turned
+        ))
+    )
+    tokens = (second_even, swap(second_even, 1))
     expert_parts[0] = after(expert_parts[0], tokens[1], grads_plane[1], gates_plane)
 
     shared_fan = fan(hold([shared_column], tokens[1], expert_parts[0])[0])
@@ -822,21 +837,20 @@
     mask = here ^ jnp.arange(groups)
     back = mask // 2 + jnp.where(mask % 2 == 1, 0, groups // 2)
 
-    def return_gates(gate_grads):
+    def return_gates(gate_grads, *others):
         sent = jnp.concatenate(gate_grads, -1).reshape(groups, token_rows, expert_local)[back]
-        return lax.all_to_all(sent, "expert", 0, 0, tiled=True)
+        return lax.all_to_all(hold([sent], *others)[0], "expert", 0, 0, tiled=True)
 
     gate_grads = []
     expert_sums = []
     part_sums = []
     before = None
-    turned, own_turned = normed_all.T, normed.T
     for number in range(expert_local):
         last = number == expert_local - 1
         gate_column = gates_plane[:, number : number + 1]
         parts = expert_pass(
             tokens, grads_plane, gate_column, expert_parts[number], part_rows, before, last,
-            (turned, own_turned) if number == 1 else (),
+            (),
         )
         before, (gate_grad, hidden, pair) = parts[:-3], parts[-3:]
         gate_grads.append(gate_grad)
@@ -847,25 +861,28 @@
             routed_odd, routed_even, entry_odd, entry_even = before
             entry_odd = hold([entry_odd], *shared_parts)[0]
             entry_other = swap(entry_odd, 1)
-            gate_grad_back = return_gates(gate_grads)
             entry_sums = join_cores(entry_even, entry_other)
             entry_parts = spread_chips(entry_sums)
-            routed_other = swap(hold([routed_odd], entry_sums[1].astype(BF16))[0], 1)
+            routed_other = swap(
+                hold([routed_odd], *[part.astype(BF16) for part in entry_sums[1:]])[0], 1
+            )
         expert_part = expert_grad(
             tokens,
             grads_plane,
             gate_column,
             hidden,
             pair,
-            [routed_other, gate_grad_back] if last else shared_fan[1:],
+            [routed_other] if last else shared_fan[1:],
         )
         if number == 0:
             shared_odd = hold([shared_odd], expert_part)[0]
             shared_out, shared_entry, shared_sums = shared_step(shared_even, shared_odd)
             shared_parts = spread_after(shared_sums, *expert_parts[1:2])
+        expert_whole = expert_part
         expert_part = expert_part.reshape(3, deep, part_rows, hidden_width)
         if last:
-            shared_total = add_up(shared_sums[0], shared_parts)
+            gate_grad_back = return_gates(gate_grads, expert_whole)
+            shared_total = add_up(shared_sums[0], hold(shared_parts, expert_whole))
             extra = -(part_rows + dense_rows) % 16
             shared_total = jnp.pad(shared_total.astype(BF16), ((0, 0), (0, 0), (0, extra), (0, 0)))
             expert_part = jnp.concatenate([expert_part, shared_total], 2)
@@ -877,7 +894,7 @@
     shared_sum = part_sum[:, part_rows : part_rows + dense_rows].astype(F32)
     expert_sum = jnp.stack(expert_sums)
 
-    entry_parts = hold(entry_parts, expert_part)
+    entry_parts = hold(entry_parts, expert_whole)
     grad_second = add_up(entry_sums[0], entry_parts)
     routed_sums = join_cores(routed_even, routed_other)
     gate_grad_stored = gate_grad_back.transpose(1, 0, 2).reshape(token_rows, specialist_total)
@@ -893,15 +910,13 @@
     gain_two_grad = jnp.sum(grad_second * scaled_two, axis=0)
     grad_middle = norm_backward(grad_second, scaled_two, inverse_two, gain_two) + grad_out
     grad_attn_out = grad_middle.astype(BF16)
-    out_grad = contract(mixed_low, grad_attn_out, 0, 0).astype(BF16)
-    out_mine, out_other = core_split(out_grad[None], dense_rows)
-    out_received = swap(out_other, 1)
 
     def grad_part(first, count, waits=()):
         *grads, dq, dk, dv = attention_grad(
             place,
             turned,
             own_turned,
+            mixed_turned,
             out_low,
             query,
             keys,
@@ -926,18 +941,11 @@
     last_mine, last_other, last_terms = grad_part(
         early, pairs - early, [first_other, part_sums[0]]
     )
-    cut = first_mine.shape[-1]
-    first_sums = chip_sums(
-        jnp.concatenate([first_mine, out_mine[..., :cut]], 0),
-        jnp.concatenate([swap(first_other, 1), out_received[..., :cut]], 0),
-    )
+    first_sums = chip_sums(first_mine, swap(first_other, 1))
     first_parts = spread_chips(first_sums)
-    last_sums = chip_sums(
-        jnp.concatenate([last_mine, out_mine[..., cut:]], 0),
-        jnp.concatenate([swap(last_other, 1), out_received[..., cut:]], 0),
-    )
+    last_received = hold([swap(last_other, 1)], first_sums[1].astype(BF16))[0]
+    last_sums = chip_sums(last_mine, last_received)
     last_parts = spread_after(last_sums, *first_parts)
-    routed_parts = spread_after(routed_sums, *last_parts)
     normed_low, grad_normed, gain_one_grad = normed_grad(
         sequence_low,
         projections,
@@ -963,8 +971,12 @@
     small_sum = jnp.sum(hold([small_received], *last_parts)[0], axis=0).reshape(-1)
     first_total = add_up(first_sums[0], hold(first_parts, grad_normed))
     last_total = add_up(last_sums[0], last_parts)
-    first_sum = column_sum(first_total, 1)
-    last_sum = column_sum(last_total, 1)
+    first_sum, first_column = column_sum(
+        first_total, 1, last_parts[0], last_total.astype(BF16)
+    )
+    expert_squares = sum(jnp.sum(part * part) for part in expert_sums)
+    last_sum, _ = column_sum(last_total, 1, None, jnp.broadcast_to(expert_squares, (8, 128)))
+    routed_parts = spread_after(routed_sums, *first_column)
     grad_normed = grad_normed - pick(normed_low, level, 0).astype(F32)
     arrived = lax.psum_scatter(
         hold([normed_low.reshape(length, width)], part_sums[-1])[0],
@@ -983,7 +995,7 @@
         + jnp.sum(shared_sum * shared_sum)
         + jnp.sum(router_sum * router_sum)
         + jnp.sum(gain_sum * gain_sum)
-        + jnp.sum(expert_sum * expert_sum)
+        + expert_squares
     )
     spread = jnp.broadcast_to(local_squares, (everyone, 8, 128))
     squares = lax.all_to_all(spread, ("dp", "expert"), 0, 0, tiled=True)

time: 756 us -> 752 us (level)
  other arithmetic: 118 us -> 127 us
    ppermute x41 -> x40, waiting for transfers between devices: 151 us -> 138 us  [swap(): return lax.ppermute(value, 'expert', [(i, i ^ mask) for i in range(size)])]
    ppermute x6, waiting for transfers between devices: 18.9 us -> 29 us  [rotate(): lax.ppermute(value, 'dp', [(i, (i + step) % size) for i in range(size)])]
    another operation x0 -> x4, other arithmetic: none -> 9.79 us  [the longest x2 5.82 us: body(): jnp.stack(list(second_fan[:1]) + list(hold(second_fan[1:], shared_column,...]
    unnamed x163 -> x175, local copies, waits for them, and re-layouts: 20.1 us -> 23.1 us
    ppermute x41 -> x40, starting transfers between devices: 36.9 us -> 37 us  [swap(): return lax.ppermute(value, 'expert', [(i, i ^ mask) for i in range(size)])]
  transfers between devices with their start and end apart: 59 -> 58, of which waited for: 24 -> 21; matrix products, arithmetic and copies ran while one was open for 22% -> 22% of each run, Pallas kernels for 32% -> 32%
where the time goes in v4:
time: 752 us; the launch traced here: 744 us
  Pallas kernels  240 us (32%)
  waiting for transfers between devices  231 us (31%)
  other arithmetic  127 us (17%)
  starting transfers between devices  62.5 us (8%)
  local copies, waits for them, and re-layouts  56.7 us (8%)
  between operations  21.6 us (3%)
    ppermute x40, waiting for transfers between devices, swap(): return lax.ppermute(value, 'expert', [(i, i ^ mask) for i in range(size)])  138 us
    pallas_call x2, Pallas kernels, expert_pass(): pl.pallas_call(functools.partial(expert_kernel, before is not None, split...  93.8 us
    pallas_call x2, Pallas kernels, expert_grad(): pl.pallas_call(expert_grad_kernel, grid=(width // span,), in_specs=[stack...  44.9 us
    all_gather x1, waiting for transfers between devices, body(): attn_column = lax.all_gather(attn_own, 'dp')  39.2 us
    ppermute x40, starting transfers between devices, swap(): return lax.ppermute(value, 'expert', [(i, i ^ mask) for i in range(size)])  37 us
    pallas_call x2, Pallas kernels, attention_grad(): pl.pallas_call(attention_grad_kernel, grid_spec=pltpu.PrefetchScalarGridS...  33.5 us
    ppermute x6, waiting for transfers between devices, rotate(): lax.ppermute(value, 'dp', [(i, (i + step) % size) for i in range(size)])  29 us
    unnamed x175, local copies, waits for them, and re-layouts  23.1 us
  transfers between devices with their start and end apart: 58, of which 21 were waited for; matrix products, arithmetic and copies ran while one was open for 22% of the time, Pallas kernels for 32%

profile of v4, /device:TPU:0, one launch (start us, length us, event | category | flops | bytes accessed | tf_op | source)
XLA Modules:
  0.0 744.5 jit_solution(2734141705131614970)
XLA Ops:
  11.9 39.2 %all-gather.9.cloned.1.call-done = bf16[16,40,1280]{2,1,0:T(8,128)(2,1)} async-done(((bf16[4,40,1280]{2,1,0:T(8,128)(2,1)}), bf16[16,40,1280]{2,1,0:T(8,128)(2,1)}) %all-gather.9.cloned.1.call-update) | async-done | bytes 1638416 | tf_op jit(solution)/shard_map/all_gather | solution.py:749
  56.1 3.6 convert_element_type.452
  61.8 21.7 %collective-permute-done.2 = bf16[4,3,40,1280]{3,2,1,0:T(8,128)(2,1)S(1)} collective-permute-done((bf16[4,3,40,1280]{3,2,1,0:T(8,128)(2,1)S(1)}, bf16[4,3,40,1280]{3,2,1,0:T(8,128)(2,1)S(1)}, u32[]{:S(2)}, u32[]{:S(2)}) %collective-permute-start.2) | collective-permute-done | bytes 1228832 | tf_op jit(solution)/shard_map/ppermute | solution.py:88
  83.5 25.1 %collective-permute-done.1 = bf16[4,3,40,1280]{3,2,1,0:T(8,128)(2,1)S(1)} collective-permute-done((bf16[4,3,40,1280]{3,2,1,0:T(8,128)(2,1)S(1)}, bf16[4,3,40,1280]{3,2,1,0:T(8,128)(2,1)S(1)}, u32[]{:S(2)}, u32[]{:S(2)}) %collective-permute-start.1) | collective-permute-done | bytes 1228832 | tf_op jit(solution)/shard_map/ppermute | solution.py:88
  109.6 12.3 %all-gather.11.cloned.1.call-done = bf16[1376,1280]{1,0:T(8,128)(2,1)} async-done(((bf16[344,1280]{1,0:T(8,128)(2,1)}), bf16[1376,1280]{1,0:T(8,128)(2,1)}) %all-gather.11.cloned.1.call-update) | async-done | bytes 3522576 | tf_op jit(solution)/shard_map/all_gather | solution.py:754
  121.8 3.4 slice.106
  125.3 5.1 pad_maximum_fusion.even
  131.4 3.3 all-to-all-start
  140.6 5.1 all-to-all-done
  152.1 8.5 %collective-permute-done.9 = bf16[4,1,40,1280]{3,2,0,1:T(8,128)(2,1)S(1)} collective-permute-done((bf16[4,1,40,1280]{3,2,0,1:T(8,128)(2,1)S(1)}, bf16[4,1,40,1280]{3,2,0,1:T(8,128)(2,1)S(1)}, u32[]{:S(2)}, u32[]{:S(2)}) %collective-permute-start.9) | collective-permute-done | bytes 409632 | tf_op jit(solution)/shard_map/ppermute | solution.py:88
  160.5 7.8 %collective-permute-done.8 = bf16[4,1,40,1280]{3,2,0,1:T(8,128)(2,1)S(1)} collective-permute-done((bf16[4,1,40,1280]{3,2,0,1:T(8,128)(2,1)S(1)}, bf16[4,1,40,1280]{3,2,0,1:T(8,128)(2,1)S(1)}, u32[]{:S(2)}, u32[]{:S(2)}) %collective-permute-start.8) | collective-permute-done | bytes 409632 | tf_op jit(solution)/shard_map/ppermute | solution.py:88
  175.0 8.0 %assemble.3 = bf16[3,4,8,40,1280]{4,3,2,1,0:T(8,128)(2,1)} custom-call(s32[1]{0:T(128)} %bitcast.7.place_ref, bf16[4,4,3,40,1280]{4,3,2,1,0:T(8,128)(2,1)} %pad_maximum_fusion.even, bf16[4,4,3,40,1280]{4,3,2,1,0:T(8,128)(2,1)} %collective-permute-done.3.odd), custom_call_target="tpu_custom_call" | custom-call | flops 1 | bytes 1 | tf_op jit(solution)/shard_map/assemble/pallas_call | solution.py:205
  192.0 4.3 assemble.4
  196.3 19.5 %attention_forward.1 = (bf16[256,1280]{1,0:T(8,128)(2,1)}, bf16[1024,1280]{1,0:T(8,128)(2,1)}, bf16[1024,1280]{1,0:T(8,128)(2,1)}, f32[256,1280]{1,0:T(8,128)}, bf16[256,1280]{1,0:T(8,128)(2,1)}) custom-call(s32[1]{0:T(128)} %bitcast.1.place_ref, bf16[1024,1280]{1,0:T(8,128)(2,1)} %copy-done.4, bf16[3,1280,1280]{2,1,0:T(8,128)(2,1)} %bitcast.290, ...), custom_call_target="tpu_custom_call" | custom-call | flops 1 | bytes 1 | tf_op jit(solution)/shard_map/attention_forward/pallas_call | solution.py:273
  229.7 8.4 %collective-permute-done.13.__2_ = bf16[256,1280]{1,0:T(8,128)(2,1)} collective-permute-done((bf16[256,1280]{1,0:T(8,128)(2,1)S(1)}, bf16[256,1280]{1,0:T(8,128)(2,1)}, u32[]{:S(2)}, u32[]{:S(2)}) %collective-permute-start.13) | collective-permute-done | bytes 655392 | tf_op jit(solution)/shard_map/ppermute | solution.py:88
  238.1 12.6 %collective-permute-done.12.__1_ = bf16[256,1280]{1,0:T(8,128)(2,1)} collective-permute-done((bf16[256,1280]{1,0:T(8,128)(2,1)S(1)}, bf16[256,1280]{1,0:T(8,128)(2,1)}, u32[]{:S(2)}, u32[]{:S(2)}) %collective-permute-start.12) | collective-permute-done | bytes 655392 | tf_op jit(solution)/shard_map/ppermute | solution.py:88
  250.7 3.5 pad_maximum_fusion.2.refs_1_.even_n
  258.4 3.3 all-to-all-start.1
  261.8 4.6 all-to-all-done.1
  273.6 44.7 %expert_pass.2 = (f32[2048,1280]{1,0:T(8,128)}, f32[2048,1280]{1,0:T(8,128)}, f32[2048,1]{1,0:T(8,128)}, bf16[2048,896]{1,0:T(8,128)(2,1)}, bf16[2048,1792]{1,0:T(8,128)(2,1)}) custom-call(bf16[4,256,1280]{2,1,0:T(8,128)(2,1)} %collective-permute-done.14.__1_.refs_0_.odd_n, bf16[4,256,1280]{2,1,0:T(8,128)(2,1)} %pad_maximum_fusion.2.refs_1_.even_n, ...), custom_call_target="tpu_custom_call" | custom-call | flops 1 | bytes 1 | tf_op jit(solution)/shard_map/expert_pass/pallas_call | solution.py:586
  318.4 3.3 pad_maximum_fusion.1.__0_
  321.8 22.5 %expert_weight_grad.2.__1_ = bf16[3,1280,896]{2,1,0:T(8,128)(2,1)} custom-call(bf16[4,256,1280]{2,1,0:T(8,128)(2,1)} %collective-permute-done.14.__1_.refs_0_.odd_n, bf16[4,256,1280]{2,1,0:T(8,128)(2,1)} %pad_maximum_fusion.2.refs_1_.even_n, bf16[4,256,1280]{2,1,0:T(8,128)(2,1)} %collective-permute-done.15.refs_2_.odd_c, bf16[4,256,1280]{2,1,0:T(8,128)(2,1)} %copy-done, ...), custom_call_target="tpu_custom_call" | custom-call | flops 1 | bytes 1 | tf_op jit(solution)/shard_map/expert_weight_grad/pallas_call | solution.py:667
  346.1 6.7 assemble.5
  352.8 12.7 %shared_pass.1 = (f32[256,1280]{1,0:T(8,128)}, f32[256,1280]{1,0:T(8,128)}, bf16[3,16,40,896]{3,2,1,0:T(8,128)(2,1)}, bf16[3,16,40,896]{3,2,1,0:T(8,128)(2,1)}) custom-call(s32[1]{0:T(128)S(6)} %select_n.165.place_ref, bf16[256,1280]{1,0:T(8,128)(2,1)} %copy-done.18, bf16[256,1280]{1,0:T(8,128)(2,1)} %bitcast.310, bf16[3,1280,896]{2,1,0:T(8,128)(2,1)} %bitcast.301), custom_call_target="tpu_custom_call" | custom-call | flops 1 | bytes 1 | tf_op jit(solution)/shard_map/shared_pass/pallas_call | solution.py:627
  366.0 5.9 collective-permute-done.20
  371.9 4.8 fusion.38
  380.2 49.1 %expert_pass.3 = (bf16[4,256,1280]{2,1,0:T(8,128)(2,1)}, bf16[4,256,1280]{2,1,0:T(8,128)(2,1)}, bf16[4,256,1280]{2,1,0:T(8,128)(2,1)}, bf16[4,256,1280]{2,1,0:T(...) custom-call(bf16[4,256,1280]{2,1,0:T(8,128)(2,1)} %collective-permute-done.14.__1_.refs_0_.odd, ...), custom_call_target="tpu_custom_call" | custom-call | flops 1 | bytes 1 | tf_op jit(solution)/shard_map/expert_pass/pallas_call | solution.py:586
  430.8 5.1 collective-permute-done.24
  435.9 4.0 fusion.42
  449.3 22.4 %expert_weight_grad.3.__3_.__1_ = bf16[3,1280,896]{2,1,0:T(8,128)(2,1)} custom-call(bf16[4,256,1280]{2,1,0:T(8,128)(2,1)} %collective-permute-done.14.__1_.refs_0_.odd_n, bf16[4,256,1280]{2,1,0:T(8,128)(2,1)} %pad_maximum_fusion.2.refs_1_.even_n, bf16[4,256,1280]{2,1,0:T(8,128)(2,1)} %collective-permute-done.15.refs_2_.odd_c, bf16[4,256,1280]{2,1,0:T(8,128)(2,1)} %copy-done, ...), custom_call_target="tpu_custom_call" | custom-call | flops 1 | bytes 1 | tf_op jit(solution)/shard_map/expert_weight_grad/pallas_call | solution.py:667
  475.4 3.3 all-to-all-start.2
  481.5 6.6 fusion.1
  495.1 3.3 multiply_reduce_fusion.1
  499.6 18.9 %attention_backward.2 = (bf16[4,16,40,768]{3,2,1,0:T(8,128)(2,1)}, bf16[4,16,40,768]{3,2,1,0:T(8,128)(2,1)}, bf16[256,768]{1,0:T(8,128)(2,1)}, bf16[1024,768]{1,0:T(8,128)(2,1)}, bf16[1024,768]{1,0:T(8,128)(2,1)}) custom-call(s32[2]{0:T(128)} %pad_add_fusion.place_ref, bf16[1280,1024]{1,0:T(8,128)(2,1)} %copy.328.__4_.turned_normed, ...), custom_call_target="tpu_custom_call" | custom-call | flops 64424509440 | bytes 1 | tf_op jit(solution)/shard_map/attention_backward/pallas_call | solution.py:371
  519.6 14.6 %attention_backward.3 = (bf16[4,16,40,512]{3,2,1,0:T(8,128)(2,1)}, bf16[4,16,40,512]{3,2,1,0:T(8,128)(2,1)}, bf16[256,512]{1,0:T(8,128)(2,1)}, bf16[1024,512]{1,0:T(8,128)(2,1)}, bf16[1024,512]{1,0:T(8,128)(2,1)}) custom-call(s32[2]{0:T(128)} %pad_add_fusion.place_ref, bf16[1280,1024]{1,0:T(8,128)(2,1)} %copy.328.__4_.turned_normed, ...), custom_call_target="tpu_custom_call" | custom-call | flops 42949672960 | bytes 1 | tf_op jit(solution)/shard_map/attention_backward/pallas_call | solution.py:371
  541.1 3.9 fusion.35
  548.5 16.0 %normed_grad.1 = (bf16[4,256,1280]{2,1,0:T(8,128)(2,1)}, f32[256,1280]{1,0:T(8,128)}, f32[1,1280]{1,0:T(1,128)}) custom-call(s32[1]{0:T(128)} %bitcast.72.refs_0_, bf16[1024,1280]{1,0:T(8,128)(2,1)} %bitcast.312, bf16[3,1280,1280]{2,1,0:T(8,128)(2,1)} %bitcast.293, bf16[256,768]{1,0:T(8,128)(2,1)} %get-tuple-element.138.refs_3_, ...), custom_call_target="tpu_custom_call" | custom-call | flops 80530636800 | bytes 1 | tf_op jit(solution)/shard_map/normed_grad/pallas_call | solution.py:457
  566.2 3.7 fusion.48
  570.8 20.3 %collective-permute-done.31.__1_.__4_ = bf16[4,4,40,768]{3,2,1,0:T(8,128)(2,1)} collective-permute-done((bf16[4,4,40,768]{3,2,1,0:T(8,128)(2,1)}, bf16[4,4,40,768]{3,2,1,0:T(8,128)(2,1)}, u32[]{:S(2)}, u32[]{:S(2)}) %collective-permute-start.31) | collective-permute-done | bytes 983072 | tf_op jit(solution)/shard_map/ppermute | solution.py:88
  599.8 4.2 fusion.90
  604.8 3.6 collective-permute-start.37
  611.0 13.7 %collective-permute-done.38.__2_ = bf16[4,4,40,512]{3,2,1,0:T(8,128)(2,1)} collective-permute-done((bf16[4,4,40,512]{3,2,1,0:T(8,128)(2,1)}, bf16[4,4,40,512]{3,2,1,0:T(8,128)(2,1)}, u32[]{:S(2)}, u32[]{:S(2)}) %collective-permute-start.38) | collective-permute-done | bytes 655392 | tf_op jit(solution)/shard_map/ppermute | solution.py:88
  624.8 3.4 fusion.88
  634.2 27.6 %collective-permute-done.36.__1_ = bf16[4,40,768]{2,1,0:T(8,128)(2,1)S(1)} collective-permute-done((bf16[4,40,768]{2,1,0:T(8,128)(2,1)}, bf16[4,40,768]{2,1,0:T(8,128)(2,1)S(1)}, u32[]{:S(2)}, u32[]{:S(2)}) %collective-permute-start.36) | collective-permute-done | bytes 245792 | tf_op jit(solution)/shard_map/ppermute | solution.py:93
  680.8 6.7 all-to-all-start.4
  689.5 6.4 collective-permute-done.41.__1_
  705.7 3.3 fusion.86
  712.3 17.9 %fusion.78 = (bf16[2,3,320,896]{3,2,1,0:T(8,128)(2,1)}, f32[2,3,320,896]{3,2,1,0:T(8,128)}, f32[2,3,320,896]{3,2,1,0:T(8,128)}, f32[2,3,320,896]{3,2,1,0:T(8,128)}) fusion(f32[2,3,320,896]{3,2,1,0:T(8,128)} %param.39, f32[]{:T(128)S(6)} %min.3, f32[1,3,320,896]{3,2,1,0:T(8,128)S(1)} %copy-done.11, f32[1,3,320,896]{3,2,1,0:T(8,128)S(1)} %copy-done.10, ...), kind=kLoop, calls=%fused_computation.204 | loop fusion | flops 30965760 | bytes 51609604 | tf_op jit(solution)/shard_map/convert_element_type | solution.py:1068
  (415 shorter events, 164.7 us)
Async XLA Ops:
  7.2 43.9 %all-gather.9.cloned.1.call-start = ((), (), s32[]{:S(2)}) async-start(), calls=%async_computation.11 | async-start | bytes 2048000 | tf_op jit(solution)/shard_map/all_gather | solution.py:749
  9.3 112.6 %all-gather.11.cloned.1.call-start = ((), (), s32[]{:S(2)}) async-start(), calls=%async_computation.12 | async-start | bytes 4403200 | tf_op jit(solution)/shard_map/all_gather | solution.py:754
  51.1 217.2 %all-gather.13.cloned.1.call-start = ((), (), s32[]{:S(2)}) async-start(), calls=%async_computation.13 | async-start | bytes 8601600 | tf_op jit(solution)/shard_map/all_gather | solution.py:765
  52.5 30.9 %collective-permute-start.2 = (bf16[4,3,40,1280]{3,2,1,0:T(8,128)(2,1)S(1)}, bf16[4,3,40,1280]{3,2,1,0:T(8,128)(2,1)S(1)}, u32[]{:S(2)}, u32[]{:S(2)}) collective-permute-start(bf16[4,3,40,1280]{3,2,1,0:T(8,128)(2,1)S(1)} %slice.143), channel_id=1, source_target_pairs={{0,6},{1,7},{2,4},{3,5},{4,2},{5,3},{6,0},{7,1},{8,14},{9,15},{10,... | collective-permute-start | bytes 3686408 | tf_op jit(solution)/shard_map/ppermute | solution.py:88
  55.0 53.5 %collective-permute-start.1 = (bf16[4,3,40,1280]{3,2,1,0:T(8,128)(2,1)S(1)}, bf16[4,3,40,1280]{3,2,1,0:T(8,128)(2,1)S(1)}, u32[]{:S(2)}, u32[]{:S(2)}) collective-permute-start(bf16[4,3,40,1280]{3,2,1,0:T(8,128)(2,1)S(1)} %slice.143), channel_id=1, source_target_pairs={{0,4},{1,5},{2,6},{3,7},{4,0},{5,1},{6,2},{7,3},{8,12},{9,13},{10,... | collective-permute-start | bytes 3686408 | tf_op jit(solution)/shard_map/ppermute | solution.py:88
  55.5 54.0 %collective-permute-start = (bf16[4,3,40,1280]{3,2,1,0:T(8,128)(2,1)S(1)}, bf16[4,3,40,1280]{3,2,1,0:T(8,128)(2,1)}, u32[]{:S(2)}, u32[]{:S(2)}) collective-permute-start(bf16[4,3,40,1280]{3,2,1,0:T(8,128)(2,1)S(1)} %slice.143), channel_id=1, source_target_pairs={{0,2},{1,3},{2,0},{3,1},{4,6},{5,7},{6,4},{7,5},{8,10},{9,11},{10,... | collective-permute-start | bytes 3686408 | tf_op jit(solution)/shard_map/ppermute | solution.py:88
  134.7 242.0 %all-gather.15.cloned.1.call-start = ((), (), s32[]{:S(2)}) async-start(), calls=%async_computation.14 | async-start | bytes 8601600 | tf_op jit(solution)/shard_map/all_gather | solution.py:771
  148.2 20.1 %collective-permute-start.8 = (bf16[4,1,40,1280]{3,2,0,1:T(8,128)(2,1)S(1)}, bf16[4,1,40,1280]{3,2,0,1:T(8,128)(2,1)S(1)}, u32[]{:S(2)}, u32[]{:S(2)}) collective-permute-start(bf16[4,1,40,1280]{3,2,0,1:T(8,128)(2,1)S(1)} %slice_bitcast_fusion.3), channel_id=1, source_target_pairs={{0,4},{1,5},{2,6},{3,7},{4,0},{5,1},{6,2},{7,3},{8,12},{9,13},{10,... | collective-permute-start | bytes 1228808 | tf_op jit(solution)/shard_map/ppermute | solution.py:88
  149.4 18.9 %collective-permute-start.7 = (bf16[4,1,40,1280]{3,2,0,1:T(8,128)(2,1)S(1)}, bf16[4,1,40,1280]{3,2,0,1:T(8,128)(2,1)S(1)}, u32[]{:S(2)}, u32[]{:S(2)}) collective-permute-start(bf16[4,1,40,1280]{3,2,0,1:T(8,128)(2,1)S(1)} %slice_bitcast_fusion.3), channel_id=1, source_target_pairs={{0,2},{1,3},{2,0},{3,1},{4,6},{5,7},{6,4},{7,5},{8,10},{9,11},{10,... | collective-permute-start | bytes 1228808 | tf_op jit(solution)/shard_map/ppermute | solution.py:88
  169.7 22.3 %collective-permute-start.10 = (bf16[4,4,1,40,1280]{4,3,2,1,0:T(8,128)(2,1)}, bf16[4,4,1,40,1280]{4,3,2,1,0:T(8,128)(2,1)}, u32[]{:S(2)}, u32[]{:S(2)}) collective-permute-start(bf16[4,4,1,40,1280]{4,3,2,1,0:T(8,128)(2,1)} %pad_maximum_fusion.4.even), channel_id=1, source_target_pairs={{0,1},{1,0},{2,3},{3,2},{4,5},{5,4},{6,7},{7,6},{8,9},{9,8},{10,11... | collective-permute-start | bytes 4915208 | tf_op jit(solution)/shard_map/ppermute | solution.py:88
  183.1 32.7 %collective-permute-start.6 = (bf16[256,1280]{1,0:T(8,128)(2,1)}, bf16[256,1280]{1,0:T(8,128)(2,1)}, u32[]{:S(2)}, u32[]{:S(2)}) collective-permute-start(bf16[256,1280]{1,0:T(8,128)(2,1)} %hold.22), channel_id=1, source_target_pairs={{0,6},{1,7},{2,4},{3,5},{4,2},{5,3},{6,0},{7,1},{8,14},{9,15},{10,... | collective-permute-start | bytes 1966088 | tf_op jit(solution)/shard_map/ppermute | solution.py:88
  184.3 31.5 %collective-permute-start.5 = (bf16[256,1280]{1,0:T(8,128)(2,1)}, bf16[256,1280]{1,0:T(8,128)(2,1)}, u32[]{:S(2)}, u32[]{:S(2)}) collective-permute-start(bf16[256,1280]{1,0:T(8,128)(2,1)} %hold.22), channel_id=1, source_target_pairs={{0,4},{1,5},{2,6},{3,7},{4,0},{5,1},{6,2},{7,3},{8,12},{9,13},{10,... | collective-permute-start | bytes 1966088 | tf_op jit(solution)/shard_map/ppermute | solution.py:88
  185.4 30.4 %collective-permute-start.4 = (bf16[256,1280]{1,0:T(8,128)(2,1)}, bf16[256,1280]{1,0:T(8,128)(2,1)}, u32[]{:S(2)}, u32[]{:S(2)}) collective-permute-start(bf16[256,1280]{1,0:T(8,128)(2,1)} %hold.22), channel_id=1, source_target_pairs={{0,2},{1,3},{2,0},{3,1},{4,6},{5,7},{6,4},{7,5},{8,10},{9,11},{10,... | collective-permute-start | bytes 1966088 | tf_op jit(solution)/shard_map/ppermute | solution.py:88
  219.3 18.8 %collective-permute-start.13 = (bf16[256,1280]{1,0:T(8,128)(2,1)S(1)}, bf16[256,1280]{1,0:T(8,128)(2,1)}, u32[]{:S(2)}, u32[]{:S(2)}) collective-permute-start(bf16[256,1280]{1,0:T(8,128)(2,1)S(1)} %multiply_convert_fusion.1.tokens_ref), channel_id=1, source_target_pairs={{0,6},{1,7},{2,4},{3,5},{4,2},{5,3},{6,0},{7,1},{8,14},{9,15},{10,... | collective-permute-start | bytes 1966088 | tf_op jit(solution)/shard_map/ppermute | solution.py:88
  220.6 30.1 %collective-permute-start.12 = (bf16[256,1280]{1,0:T(8,128)(2,1)S(1)}, bf16[256,1280]{1,0:T(8,128)(2,1)}, u32[]{:S(2)}, u32[]{:S(2)}) collective-permute-start(bf16[256,1280]{1,0:T(8,128)(2,1)S(1)} %multiply_convert_fusion.1.tokens_ref), channel_id=1, source_target_pairs={{0,4},{1,5},{2,6},{3,7},{4,0},{5,1},{6,2},{7,3},{8,12},{9,13},{10,... | collective-permute-start | bytes 1966088 | tf_op jit(solution)/shard_map/ppermute | solution.py:88
  221.7 29.0 %collective-permute-start.11 = (bf16[256,1280]{1,0:T(8,128)(2,1)S(1)}, bf16[256,1280]{1,0:T(8,128)(2,1)}, u32[]{:S(2)}, u32[]{:S(2)}) collective-permute-start(bf16[256,1280]{1,0:T(8,128)(2,1)S(1)} %multiply_convert_fusion.1.tokens_ref), channel_id=1, source_target_pairs={{0,2},{1,3},{2,0},{3,1},{4,6},{5,7},{6,4},{7,5},{8,10},{9,11},{10,... | collective-permute-start | bytes 1966088 | tf_op jit(solution)/shard_map/ppermute | solution.py:88
  227.3 41.0 %collective-permute-start.15 = (bf16[4,256,1280]{2,1,0:T(8,128)(2,1)S(1)}, bf16[4,256,1280]{2,1,0:T(8,128)(2,1)}, u32[]{:S(2)}, u32[]{:S(2)}) collective-permute-start(bf16[4,256,1280]{2,1,0:T(8,128)(2,1)S(1)} %pad_maximum_fusion.3.refs_3_.even_c), channel_id=1, source_target_pairs={{0,1},{1,0},{2,3},{3,2},{4,5},{5,4},{6,7},{7,6},{8,9},{9,8},{10,11... | collective-permute-start | bytes 7864328 | tf_op jit(solution)/shard_map/ppermute | solution.py:88
  261.7 257.9 %reduce-scatter.4.cloned.1.call-start = ((), (), s32[]{:S(2)}) async-start(), calls=%async_computation.8 | async-start | bytes 8601600 | tf_op jit(solution)/shard_map/reduce_scatter | solution.py:889
  268.3 50.0 %collective-permute-start.18 = (bf16[4,3,40,896]{3,2,1,0:T(8,128)(2,1)}, bf16[4,3,40,896]{3,2,1,0:T(8,128)(2,1)S(1)}, u32[]{:S(2)}, u32[]{:S(2)}) collective-permute-start(bf16[4,3,40,896]{3,2,1,0:T(8,128)(2,1)} %hold.25), channel_id=1, source_target_pairs={{0,6},{1,7},{2,4},{3,5},{4,2},{5,3},{6,0},{7,1},{8,14},{9,15},{10,... | collective-permute-start | bytes 2580488 | tf_op jit(solution)/shard_map/ppermute | solution.py:88
  269.0 49.4 %collective-permute-start.17 = (bf16[4,3,40,896]{3,2,1,0:T(8,128)(2,1)}, bf16[4,3,40,896]{3,2,1,0:T(8,128)(2,1)S(1)}, u32[]{:S(2)}, u32[]{:S(2)}) collective-permute-start(bf16[4,3,40,896]{3,2,1,0:T(8,128)(2,1)} %hold.25), channel_id=1, source_target_pairs={{0,4},{1,5},{2,6},{3,7},{4,0},{5,1},{6,2},{7,3},{8,12},{9,13},{10,... | collective-permute-start | bytes 2580488 | tf_op jit(solution)/shard_map/ppermute | solution.py:88
  270.4 47.9 %collective-permute-start.16 = (bf16[4,3,40,896]{3,2,1,0:T(8,128)(2,1)}, bf16[4,3,40,896]{3,2,1,0:T(8,128)(2,1)}, u32[]{:S(2)}, u32[]{:S(2)}) collective-permute-start(bf16[4,3,40,896]{3,2,1,0:T(8,128)(2,1)} %hold.25), channel_id=1, source_target_pairs={{0,2},{1,3},{2,0},{3,1},{4,6},{5,7},{6,4},{7,5},{8,10},{9,11},{10,... | collective-permute-start | bytes 2580488 | tf_op jit(solution)/shard_map/ppermute | solution.py:88
  321.7 22.6 %collective-permute-start.19 = (bf16[4,4,3,40,896]{4,3,2,1,0:T(8,128)(2,1)}, bf16[4,4,3,40,896]{4,3,2,1,0:T(8,128)(2,1)S(1)}, u32[]{:S(2)}, u32[]{:S(2)}) collective-permute-start(bf16[4,4,3,40,896]{4,3,2,1,0:T(8,128)(2,1)} %hold.26.even), channel_id=1, source_target_pairs={{0,1},{1,0},{2,3},{3,2},{4,5},{5,4},{6,7},{7,6},{8,9},{9,8},{10,11... | collective-permute-start | bytes 10321928 | tf_op jit(solution)/shard_map/ppermute | solution.py:88
  376.7 52.6 %collective-permute-start.21 = (bf16[3,4,40,896]{3,2,1,0:T(8,128)(2,1)}, bf16[3,4,40,896]{3,2,1,0:T(8,128)(2,1)S(1)}, u32[]{:S(2)}, u32[]{:S(2)}) collective-permute-start(bf16[3,4,40,896]{3,2,1,0:T(8,128)(2,1)} %get-tuple-element.121), channel_id=1, source_target_pairs={{0,2},{1,3},{2,0},{3,1},{4,6},{5,7},{6,4},{7,5},{8,10},{9,11},{10,... | collective-permute-start | bytes 2580488 | tf_op jit(solution)/shard_map/ppermute | solution.py:88
  377.3 52.1 %collective-permute-start.22 = (bf16[3,4,40,896]{3,2,1,0:T(8,128)(2,1)}, bf16[3,4,40,896]{3,2,1,0:T(8,128)(2,1)S(1)}, u32[]{:S(2)}, u32[]{:S(2)}) collective-permute-start(bf16[3,4,40,896]{3,2,1,0:T(8,128)(2,1)} %get-tuple-element.122), channel_id=1, source_target_pairs={{0,4},{1,5},{2,6},{3,7},{4,0},{5,1},{6,2},{7,3},{8,12},{9,13},{10,... | collective-permute-start | bytes 2580488 | tf_op jit(solution)/shard_map/ppermute | solution.py:88
  378.0 51.4 %collective-permute-start.23 = (bf16[3,4,40,896]{3,2,1,0:T(8,128)(2,1)}, bf16[3,4,40,896]{3,2,1,0:T(8,128)(2,1)S(1)}, u32[]{:S(2)}, u32[]{:S(2)}) collective-permute-start(bf16[3,4,40,896]{3,2,1,0:T(8,128)(2,1)} %get-tuple-element.123), channel_id=1, source_target_pairs={{0,6},{1,7},{2,4},{3,5},{4,2},{5,3},{6,0},{7,1},{8,14},{9,15},{10,... | collective-permute-start | bytes 2580488 | tf_op jit(solution)/shard_map/ppermute | solution.py:88
  445.8 47.1 %collective-permute-start.28 = (bf16[256,1280]{1,0:T(8,128)(2,1)}, bf16[256,1280]{1,0:T(8,128)(2,1)S(1)}, u32[]{:S(2)}, u32[]{:S(2)}) collective-permute-start(bf16[256,1280]{1,0:T(8,128)(2,1)} %get-tuple-element.298.__3_), channel_id=1, source_target_pairs={{0,6},{1,7},{2,4},{3,5},{4,2},{5,3},{6,0},{7,1},{8,14},{9,15},{10,... | collective-permute-start | bytes 1966088 | tf_op jit(solution)/shard_map/ppermute | solution.py:88
  446.5 46.4 %collective-permute-start.27 = (bf16[256,1280]{1,0:T(8,128)(2,1)}, bf16[256,1280]{1,0:T(8,128)(2,1)}, u32[]{:S(2)}, u32[]{:S(2)}) collective-permute-start(bf16[256,1280]{1,0:T(8,128)(2,1)} %get-tuple-element.299.__2_), channel_id=1, source_target_pairs={{0,4},{1,5},{2,6},{3,7},{4,0},{5,1},{6,2},{7,3},{8,12},{9,13},{10,... | collective-permute-start | bytes 1966088 | tf_op jit(solution)/shard_map/ppermute | solution.py:88
  471.7 21.2 %collective-permute-start.26 = (bf16[256,1280]{1,0:T(8,128)(2,1)}, bf16[256,1280]{1,0:T(8,128)(2,1)}, u32[]{:S(2)}, u32[]{:S(2)}) collective-permute-start(bf16[256,1280]{1,0:T(8,128)(2,1)} %get-tuple-element.300.__1_), channel_id=1, source_target_pairs={{0,2},{1,3},{2,0},{3,1},{4,6},{5,7},{6,4},{7,5},{8,10},{9,11},{10,... | collective-permute-start | bytes 1966088 | tf_op jit(solution)/shard_map/ppermute | solution.py:88
  478.7 188.3 %reduce-scatter.6.cloned.1.call-start = ((), (), s32[]{:S(2)}) async-start(), calls=%async_computation.9 | async-start | bytes 9891840 | tf_op jit(solution)/shard_map/reduce_scatter | solution.py:889
  519.2 20.5 %collective-permute-start.29 = (bf16[4,16,40,768]{3,2,1,0:T(8,128)(2,1)}, bf16[4,16,40,768]{3,2,1,0:T(8,128)(2,1)}, u32[]{:S(2)}, u32[]{:S(2)}) collective-permute-start(bf16[4,16,40,768]{3,2,1,0:T(8,128)(2,1)} %get-tuple-element.137.refs_0_), channel_id=1, source_target_pairs={{0,1},{1,0},{2,3},{3,2},{4,5},{5,4},{6,7},{7,6},{8,9},{9,8},{10,11... | collective-permute-start | bytes 11796488 | tf_op jit(solution)/shard_map/ppermute | solution.py:88
  534.2 30.3 %collective-permute-start.34 = (bf16[4,16,40,512]{3,2,1,0:T(8,128)(2,1)}, bf16[4,16,40,512]{3,2,1,0:T(8,128)(2,1)S(1)}, u32[]{:S(2)}, u32[]{:S(2)}) collective-permute-start(bf16[4,16,40,512]{3,2,1,0:T(8,128)(2,1)} %get-tuple-element.149), channel_id=1, source_target_pairs={{0,1},{1,0},{2,3},{3,2},{4,5},{5,4},{6,7},{7,6},{8,9},{9,8},{10,11... | collective-permute-start | bytes 7864328 | tf_op jit(solution)/shard_map/ppermute | solution.py:88
  545.0 25.9 %collective-permute-start.32 = (bf16[4,4,40,768]{3,2,1,0:T(8,128)(2,1)}, bf16[4,4,40,768]{3,2,1,0:T(8,128)(2,1)}, u32[]{:S(2)}, u32[]{:S(2)}) collective-permute-start(bf16[4,4,40,768]{3,2,1,0:T(8,128)(2,1)} %get-tuple-element.286), channel_id=1, source_target_pairs={{0,6},{1,7},{2,4},{3,5},{4,2},{5,3},{6,0},{7,1},{8,14},{9,15},{10,... | collective-permute-start | bytes 2949128 | tf_op jit(solution)/shard_map/ppermute | solution.py:88
  547.7 43.5 %collective-permute-start.31 = (bf16[4,4,40,768]{3,2,1,0:T(8,128)(2,1)}, bf16[4,4,40,768]{3,2,1,0:T(8,128)(2,1)}, u32[]{:S(2)}, u32[]{:S(2)}) collective-permute-start(bf16[4,4,40,768]{3,2,1,0:T(8,128)(2,1)} %get-tuple-element.287), channel_id=1, source_target_pairs={{0,4},{1,5},{2,6},{3,7},{4,0},{5,1},{6,2},{7,3},{8,12},{9,13},{10,... | collective-permute-start | bytes 2949128 | tf_op jit(solution)/shard_map/ppermute | solution.py:88
  548.2 43.2 %collective-permute-start.30 = (bf16[4,4,40,768]{3,2,1,0:T(8,128)(2,1)}, bf16[4,4,40,768]{3,2,1,0:T(8,128)(2,1)}, u32[]{:S(2)}, u32[]{:S(2)}) collective-permute-start(bf16[4,4,40,768]{3,2,1,0:T(8,128)(2,1)} %get-tuple-element.288.refs_9_.__1_), channel_id=1, source_target_pairs={{0,2},{1,3},{2,0},{3,1},{4,6},{5,7},{6,4},{7,5},{8,10},{9,11},{10,... | collective-permute-start | bytes 2949128 | tf_op jit(solution)/shard_map/ppermute | solution.py:88
  591.3 18.9 %collective-permute-start.35 = (bf16[4,4,40,512]{3,2,1,0:T(8,128)(2,1)}, bf16[4,4,40,512]{3,2,1,0:T(8,128)(2,1)S(1)}, u32[]{:S(2)}, u32[]{:S(2)}) collective-permute-start(bf16[4,4,40,512]{3,2,1,0:T(8,128)(2,1)} %get-tuple-element.150), channel_id=1, source_target_pairs={{0,2},{1,3},{2,0},{3,1},{4,6},{5,7},{6,4},{7,5},{8,10},{9,11},{10,... | collective-permute-start | bytes 1966088 | tf_op jit(solution)/shard_map/ppermute | solution.py:88
  592.8 31.9 %collective-permute-start.38 = (bf16[4,4,40,512]{3,2,1,0:T(8,128)(2,1)}, bf16[4,4,40,512]{3,2,1,0:T(8,128)(2,1)}, u32[]{:S(2)}, u32[]{:S(2)}) collective-permute-start(bf16[4,4,40,512]{3,2,1,0:T(8,128)(2,1)} %get-tuple-element.151), channel_id=1, source_target_pairs={{0,4},{1,5},{2,6},{3,7},{4,0},{5,1},{6,2},{7,3},{8,12},{9,13},{10,... | collective-permute-start | bytes 1966088 | tf_op jit(solution)/shard_map/ppermute | solution.py:88
  593.4 31.3 %collective-permute-start.39 = (bf16[4,4,40,512]{3,2,1,0:T(8,128)(2,1)}, bf16[4,4,40,512]{3,2,1,0:T(8,128)(2,1)}, u32[]{:S(2)}, u32[]{:S(2)}) collective-permute-start(bf16[4,4,40,512]{3,2,1,0:T(8,128)(2,1)} %get-tuple-element.152), channel_id=1, source_target_pairs={{0,6},{1,7},{2,4},{3,5},{4,2},{5,3},{6,0},{7,1},{8,14},{9,15},{10,... | collective-permute-start | bytes 1966088 | tf_op jit(solution)/shard_map/ppermute | solution.py:88
  595.6 35.3 %all-to-all-start.3 = ((f32[32,8,128]{2,1,0:T(8,128)}), f32[32,8,128]{2,1,0:T(8,128)S(1)}, u32[]{:S(2)}, u32[]{:S(2)}) async-start(f32[32,8,128]{2,1,0:T(8,128)} %bitcast.140), calls=%async_computation.5 | async-start | bytes 262144 | tf_op jit(solution)/shard_map/all_to_all | solution.py:968
  598.2 132.0 %reduce-scatter.8.cloned.1.call-start = ((), (), s32[]{:S(2)}) async-start(), calls=%async_computation.10 | async-start | bytes 3276800 | tf_op jit(solution)/shard_map/reduce_scatter | solution.py:981
  604.8 28.9 %collective-permute-start.37 = (bf16[4,40,768]{2,1,0:T(8,128)(2,1)S(1)}, bf16[4,40,768]{2,1,0:T(8,128)(2,1)S(1)}, u32[]{:S(2)}, u32[]{:S(2)}) collective-permute-start(bf16[4,40,768]{2,1,0:T(8,128)(2,1)S(1)} %get-tuple-element.305), channel_id=1, source_target_pairs={{0,24},{8,0},{16,8},{24,16},{1,25},{9,1},{17,9},{25,17},{2,26},{10... | collective-permute-start | bytes 737288 | tf_op jit(solution)/shard_map/ppermute | solution.py:93
  608.4 25.8 %collective-permute-start.33 = (bf16[4,40,768]{2,1,0:T(8,128)(2,1)S(1)}, bf16[4,40,768]{2,1,0:T(8,128)(2,1)S(1)}, u32[]{:S(2)}, u32[]{:S(2)}) collective-permute-start(bf16[4,40,768]{2,1,0:T(8,128)(2,1)S(1)} %get-tuple-element.307), channel_id=1, source_target_pairs={{0,8},{8,16},{16,24},{24,0},{1,9},{9,17},{17,25},{25,1},{2,10},{10... | collective-permute-start | bytes 737288 | tf_op jit(solution)/shard_map/ppermute | solution.py:93
  611.0 50.8 %collective-permute-start.36 = (bf16[4,40,768]{2,1,0:T(8,128)(2,1)}, bf16[4,40,768]{2,1,0:T(8,128)(2,1)S(1)}, u32[]{:S(2)}, u32[]{:S(2)}) collective-permute-start(bf16[4,40,768]{2,1,0:T(8,128)(2,1)} %hold.36), channel_id=1, source_target_pairs={{0,16},{8,24},{16,0},{24,8},{1,17},{9,25},{17,1},{25,9},{2,18},{10... | collective-permute-start | bytes 737288 | tf_op jit(solution)/shard_map/ppermute | solution.py:93
  629.0 42.4 %collective-permute-start.45 = (bf16[4,40,512]{2,1,0:T(8,128)(2,1)}, bf16[4,40,512]{2,1,0:T(8,128)(2,1)}, u32[]{:S(2)}, u32[]{:S(2)}) collective-permute-start(bf16[4,40,512]{2,1,0:T(8,128)(2,1)} %get-tuple-element.308), channel_id=1, source_target_pairs={{0,24},{8,0},{16,8},{24,16},{1,25},{9,1},{17,9},{25,17},{2,26},{10... | collective-permute-start | bytes 491528 | tf_op jit(solution)/shard_map/ppermute | solution.py:93
  629.4 43.9 %collective-permute-start.44 = (bf16[4,40,512]{2,1,0:T(8,128)(2,1)}, bf16[4,40,512]{2,1,0:T(8,128)(2,1)}, u32[]{:S(2)}, u32[]{:S(2)}) collective-permute-start(bf16[4,40,512]{2,1,0:T(8,128)(2,1)} %get-tuple-element.309), channel_id=1, source_target_pairs={{0,16},{8,24},{16,0},{24,8},{1,17},{9,25},{17,1},{25,9},{2,18},{10... | collective-permute-start | bytes 491528 | tf_op jit(solution)/shard_map/ppermute | solution.py:93
  633.7 39.6 %collective-permute-start.43 = (bf16[4,40,512]{2,1,0:T(8,128)(2,1)}, bf16[4,40,512]{2,1,0:T(8,128)(2,1)S(1)}, u32[]{:S(2)}, u32[]{:S(2)}) collective-permute-start(bf16[4,40,512]{2,1,0:T(8,128)(2,1)} %get-tuple-element.310), channel_id=1, source_target_pairs={{0,8},{8,16},{16,24},{24,0},{1,9},{9,17},{17,25},{25,1},{2,10},{10... | collective-permute-start | bytes 491528 | tf_op jit(solution)/shard_map/ppermute | solution.py:93
  662.5 27.0 %collective-permute-start.40 = (bf16[256,1280]{1,0:T(8,128)(2,1)}, bf16[256,1280]{1,0:T(8,128)(2,1)S(1)}, u32[]{:S(2)}, u32[]{:S(2)}) collective-permute-start(bf16[256,1280]{1,0:T(8,128)(2,1)} %get-tuple-element.156), channel_id=1, source_target_pairs={{0,2},{1,3},{2,0},{3,1},{4,6},{5,7},{6,4},{7,5},{8,10},{9,11},{10,... | collective-permute-start | bytes 1966088 | tf_op jit(solution)/shard_map/ppermute | solution.py:88
  664.0 31.8 %collective-permute-start.41 = (bf16[256,1280]{1,0:T(8,128)(2,1)}, bf16[256,1280]{1,0:T(8,128)(2,1)}, u32[]{:S(2)}, u32[]{:S(2)}) collective-permute-start(bf16[256,1280]{1,0:T(8,128)(2,1)} %get-tuple-element.157), channel_id=1, source_target_pairs={{0,4},{1,5},{2,6},{3,7},{4,0},{5,1},{6,2},{7,3},{8,12},{9,13},{10,... | collective-permute-start | bytes 1966088 | tf_op jit(solution)/shard_map/ppermute | solution.py:88
  671.4 24.5 %collective-permute-start.42 = (bf16[256,1280]{1,0:T(8,128)(2,1)}, bf16[256,1280]{1,0:T(8,128)(2,1)}, u32[]{:S(2)}, u32[]{:S(2)}) collective-permute-start(bf16[256,1280]{1,0:T(8,128)(2,1)} %get-tuple-element.158), channel_id=1, source_target_pairs={{0,6},{1,7},{2,4},{3,5},{4,2},{5,3},{6,0},{7,1},{8,14},{9,15},{10,... | collective-permute-start | bytes 1966088 | tf_op jit(solution)/shard_map/ppermute | solution.py:88
  (93 other events, 1365.8 us)
Sparse Core Ops, SparseCore 0:
  10.2 40.8 all-gather.8
  53.2 68.5 all-gather.10
  125.4 124.9 all-gather.12
  251.8 123.1 all-gather.14
  377.7 118.5 reduce-scatter.3
  498.7 164.0 reduce-scatter.5
  667.2 59.3 reduce-scatter.7

commit v5 on v4

--- a/solution.py
+++ b/solution.py
@@ -972,7 +972,7 @@
     first_total = add_up(first_sums[0], hold(first_parts, grad_normed))
     last_total = add_up(last_sums[0], last_parts)
     first_sum, first_column = column_sum(
-        first_total, 1, last_parts[0], last_total.astype(BF16)
+        first_total, 1, None, last_total.astype(BF16)
     )
     expert_squares = sum(jnp.sum(part * part) for part in expert_sums)
     last_sum, _ = column_sum(last_total, 1, None, jnp.broadcast_to(expert_squares, (8, 128)))

time: 752 us -> 752 us (level)
    unnamed x175 -> x173, local copies, waits for them, and re-layouts: 23.1 us -> 22.9 us
  transfers between devices with their start and end apart: 58 -> 58, of which waited for: 21 -> 20; matrix products, arithmetic and copies ran while one was open for 22% -> 22% of each run, Pallas kernels for 32% -> 32%
where the time goes in v5:
time: 752 us; the launch traced here: 744 us
  Pallas kernels  240 us (32%)
  waiting for transfers between devices  231 us (31%)
  other arithmetic  126 us (17%)
  starting transfers between devices  64 us (9%)
  local copies, waits for them, and re-layouts  55.8 us (7%)
  between operations  21.6 us (3%)
    ppermute x40, waiting for transfers between devices, swap(): return lax.ppermute(value, 'expert', [(i, i ^ mask) for i in range(size)])  141 us
    pallas_call x2, Pallas kernels, expert_pass(): pl.pallas_call(functools.partial(expert_kernel, before is not None, split...  93.9 us
    pallas_call x2, Pallas kernels, expert_grad(): pl.pallas_call(expert_grad_kernel, grid=(width // span,), in_specs=[stack...  44.9 us
    all_gather x1, waiting for transfers between devices, body(): attn_column = lax.all_gather(attn_own, 'dp')  39.2 us
    ppermute x40, starting transfers between devices, swap(): return lax.ppermute(value, 'expert', [(i, i ^ mask) for i in range(size)])  36.7 us
    pallas_call x2, Pallas kernels, attention_grad(): pl.pallas_call(attention_grad_kernel, grid_spec=pltpu.PrefetchScalarGridS...  33.5 us
    ppermute x6, waiting for transfers between devices, rotate(): lax.ppermute(value, 'dp', [(i, (i + step) % size) for i in range(size)])  27.4 us
    unnamed x173, local copies, waits for them, and re-layouts  22.9 us
  transfers between devices with their start and end apart: 58, of which 20 were waited for; matrix products, arithmetic and copies ran while one was open for 22% of the time, Pallas kernels for 32%

profile of v5, /device:TPU:0, one launch (start us, length us, event | category | flops | bytes accessed | tf_op | source)
XLA Modules:
  0.0 744.4 jit_solution(16525832195452584477)
XLA Ops:
  11.9 39.2 %all-gather.9.cloned.1.call-done = bf16[16,40,1280]{2,1,0:T(8,128)(2,1)} async-done(((bf16[4,40,1280]{2,1,0:T(8,128)(2,1)}), bf16[16,40,1280]{2,1,0:T(8,128)(2,1)}) %all-gather.9.cloned.1.call-update) | async-done | bytes 1638416 | tf_op jit(solution)/shard_map/all_gather | solution.py:749
  56.1 3.6 convert_element_type.452
  61.8 21.7 %collective-permute-done.2 = bf16[4,3,40,1280]{3,2,1,0:T(8,128)(2,1)S(1)} collective-permute-done((bf16[4,3,40,1280]{3,2,1,0:T(8,128)(2,1)S(1)}, bf16[4,3,40,1280]{3,2,1,0:T(8,128)(2,1)S(1)}, u32[]{:S(2)}, u32[]{:S(2)}) %collective-permute-start.2) | collective-permute-done | bytes 1228832 | tf_op jit(solution)/shard_map/ppermute | solution.py:88
  83.5 25.1 %collective-permute-done.1 = bf16[4,3,40,1280]{3,2,1,0:T(8,128)(2,1)S(1)} collective-permute-done((bf16[4,3,40,1280]{3,2,1,0:T(8,128)(2,1)S(1)}, bf16[4,3,40,1280]{3,2,1,0:T(8,128)(2,1)S(1)}, u32[]{:S(2)}, u32[]{:S(2)}) %collective-permute-start.1) | collective-permute-done | bytes 1228832 | tf_op jit(solution)/shard_map/ppermute | solution.py:88
  109.6 12.3 %all-gather.11.cloned.1.call-done = bf16[1376,1280]{1,0:T(8,128)(2,1)} async-done(((bf16[344,1280]{1,0:T(8,128)(2,1)}), bf16[1376,1280]{1,0:T(8,128)(2,1)}) %all-gather.11.cloned.1.call-update) | async-done | bytes 3522576 | tf_op jit(solution)/shard_map/all_gather | solution.py:754
  121.8 3.4 slice.106
  125.3 5.1 pad_maximum_fusion.even
  131.4 3.3 all-to-all-start
  140.6 5.1 all-to-all-done
  152.1 8.5 %collective-permute-done.9 = bf16[4,1,40,1280]{3,2,0,1:T(8,128)(2,1)S(1)} collective-permute-done((bf16[4,1,40,1280]{3,2,0,1:T(8,128)(2,1)S(1)}, bf16[4,1,40,1280]{3,2,0,1:T(8,128)(2,1)S(1)}, u32[]{:S(2)}, u32[]{:S(2)}) %collective-permute-start.9) | collective-permute-done | bytes 409632 | tf_op jit(solution)/shard_map/ppermute | solution.py:88
  160.5 7.8 %collective-permute-done.8 = bf16[4,1,40,1280]{3,2,0,1:T(8,128)(2,1)S(1)} collective-permute-done((bf16[4,1,40,1280]{3,2,0,1:T(8,128)(2,1)S(1)}, bf16[4,1,40,1280]{3,2,0,1:T(8,128)(2,1)S(1)}, u32[]{:S(2)}, u32[]{:S(2)}) %collective-permute-start.8) | collective-permute-done | bytes 409632 | tf_op jit(solution)/shard_map/ppermute | solution.py:88
  175.0 8.0 %assemble.3 = bf16[3,4,8,40,1280]{4,3,2,1,0:T(8,128)(2,1)} custom-call(s32[1]{0:T(128)} %bitcast.7.place_ref, bf16[4,4,3,40,1280]{4,3,2,1,0:T(8,128)(2,1)} %pad_maximum_fusion.even, bf16[4,4,3,40,1280]{4,3,2,1,0:T(8,128)(2,1)} %collective-permute-done.3.odd), custom_call_target="tpu_custom_call" | custom-call | flops 1 | bytes 1 | tf_op jit(solution)/shard_map/assemble/pallas_call | solution.py:205
  192.0 4.3 assemble.4
  196.3 19.5 %attention_forward.1 = (bf16[256,1280]{1,0:T(8,128)(2,1)}, bf16[1024,1280]{1,0:T(8,128)(2,1)}, bf16[1024,1280]{1,0:T(8,128)(2,1)}, f32[256,1280]{1,0:T(8,128)}, bf16[256,1280]{1,0:T(8,128)(2,1)}) custom-call(s32[1]{0:T(128)} %bitcast.1.place_ref, bf16[1024,1280]{1,0:T(8,128)(2,1)} %copy-done.4, bf16[3,1280,1280]{2,1,0:T(8,128)(2,1)} %bitcast.290, ...), custom_call_target="tpu_custom_call" | custom-call | flops 1 | bytes 1 | tf_op jit(solution)/shard_map/attention_forward/pallas_call | solution.py:273
  229.7 8.4 %collective-permute-done.13.__2_ = bf16[256,1280]{1,0:T(8,128)(2,1)} collective-permute-done((bf16[256,1280]{1,0:T(8,128)(2,1)S(1)}, bf16[256,1280]{1,0:T(8,128)(2,1)}, u32[]{:S(2)}, u32[]{:S(2)}) %collective-permute-start.13) | collective-permute-done | bytes 655392 | tf_op jit(solution)/shard_map/ppermute | solution.py:88
  238.0 12.6 %collective-permute-done.12.__1_ = bf16[256,1280]{1,0:T(8,128)(2,1)} collective-permute-done((bf16[256,1280]{1,0:T(8,128)(2,1)S(1)}, bf16[256,1280]{1,0:T(8,128)(2,1)}, u32[]{:S(2)}, u32[]{:S(2)}) %collective-permute-start.12) | collective-permute-done | bytes 655392 | tf_op jit(solution)/shard_map/ppermute | solution.py:88
  250.7 3.5 pad_maximum_fusion.2.refs_1_.even_n
  258.3 3.3 all-to-all-start.1
  261.7 4.6 all-to-all-done.1
  273.6 44.8 %expert_pass.2 = (f32[2048,1280]{1,0:T(8,128)}, f32[2048,1280]{1,0:T(8,128)}, f32[2048,1]{1,0:T(8,128)}, bf16[2048,896]{1,0:T(8,128)(2,1)}, bf16[2048,1792]{1,0:T(8,128)(2,1)}) custom-call(bf16[4,256,1280]{2,1,0:T(8,128)(2,1)} %collective-permute-done.14.__1_.refs_0_.odd_n, bf16[4,256,1280]{2,1,0:T(8,128)(2,1)} %pad_maximum_fusion.2.refs_1_.even_n, ...), custom_call_target="tpu_custom_call" | custom-call | flops 1 | bytes 1 | tf_op jit(solution)/shard_map/expert_pass/pallas_call | solution.py:586
  318.4 3.3 pad_maximum_fusion.1.__0_
  321.8 22.5 %expert_weight_grad.2.__1_ = bf16[3,1280,896]{2,1,0:T(8,128)(2,1)} custom-call(bf16[4,256,1280]{2,1,0:T(8,128)(2,1)} %collective-permute-done.14.__1_.refs_0_.odd_n, bf16[4,256,1280]{2,1,0:T(8,128)(2,1)} %pad_maximum_fusion.2.refs_1_.even_n, bf16[4,256,1280]{2,1,0:T(8,128)(2,1)} %collective-permute-done.15.refs_2_.odd_c, bf16[4,256,1280]{2,1,0:T(8,128)(2,1)} %copy-done, ...), custom_call_target="tpu_custom_call" | custom-call | flops 1 | bytes 1 | tf_op jit(solution)/shard_map/expert_weight_grad/pallas_call | solution.py:667
  346.1 6.7 assemble.5
  352.8 12.7 %shared_pass.1 = (f32[256,1280]{1,0:T(8,128)}, f32[256,1280]{1,0:T(8,128)}, bf16[3,16,40,896]{3,2,1,0:T(8,128)(2,1)}, bf16[3,16,40,896]{3,2,1,0:T(8,128)(2,1)}) custom-call(s32[1]{0:T(128)S(6)} %select_n.165.place_ref, bf16[256,1280]{1,0:T(8,128)(2,1)} %copy-done.18, bf16[256,1280]{1,0:T(8,128)(2,1)} %bitcast.310, bf16[3,1280,896]{2,1,0:T(8,128)(2,1)} %bitcast.301), custom_call_target="tpu_custom_call" | custom-call | flops 1 | bytes 1 | tf_op jit(solution)/shard_map/shared_pass/pallas_call | solution.py:627
  366.0 5.9 collective-permute-done.20
  371.9 4.8 fusion.38
  380.2 49.1 %expert_pass.3 = (bf16[4,256,1280]{2,1,0:T(8,128)(2,1)}, bf16[4,256,1280]{2,1,0:T(8,128)(2,1)}, bf16[4,256,1280]{2,1,0:T(8,128)(2,1)}, bf16[4,256,1280]{2,1,0:T(...) custom-call(bf16[4,256,1280]{2,1,0:T(8,128)(2,1)} %collective-permute-done.14.__1_.refs_0_.odd, ...), custom_call_target="tpu_custom_call" | custom-call | flops 1 | bytes 1 | tf_op jit(solution)/shard_map/expert_pass/pallas_call | solution.py:586
  430.8 5.1 collective-permute-done.24
  435.9 4.0 fusion.42
  449.4 22.4 %expert_weight_grad.3.__3_.__1_ = bf16[3,1280,896]{2,1,0:T(8,128)(2,1)} custom-call(bf16[4,256,1280]{2,1,0:T(8,128)(2,1)} %collective-permute-done.14.__1_.refs_0_.odd_n, bf16[4,256,1280]{2,1,0:T(8,128)(2,1)} %pad_maximum_fusion.2.refs_1_.even_n, bf16[4,256,1280]{2,1,0:T(8,128)(2,1)} %collective-permute-done.15.refs_2_.odd_c, bf16[4,256,1280]{2,1,0:T(8,128)(2,1)} %copy-done, ...), custom_call_target="tpu_custom_call" | custom-call | flops 1 | bytes 1 | tf_op jit(solution)/shard_map/expert_weight_grad/pallas_call | solution.py:667
  475.4 3.3 all-to-all-start.2
  481.5 6.6 fusion.1
  495.1 3.3 multiply_reduce_fusion.1
  499.6 18.9 %attention_backward.2 = (bf16[4,16,40,768]{3,2,1,0:T(8,128)(2,1)}, bf16[4,16,40,768]{3,2,1,0:T(8,128)(2,1)}, bf16[256,768]{1,0:T(8,128)(2,1)}, bf16[1024,768]{1,0:T(8,128)(2,1)}, bf16[1024,768]{1,0:T(8,128)(2,1)}) custom-call(s32[2]{0:T(128)} %pad_add_fusion.place_ref, bf16[1280,1024]{1,0:T(8,128)(2,1)} %copy.327.__4_.turned_normed, ...), custom_call_target="tpu_custom_call" | custom-call | flops 64424509440 | bytes 1 | tf_op jit(solution)/shard_map/attention_backward/pallas_call | solution.py:371
  519.6 14.6 %attention_backward.3 = (bf16[4,16,40,512]{3,2,1,0:T(8,128)(2,1)}, bf16[4,16,40,512]{3,2,1,0:T(8,128)(2,1)}, bf16[256,512]{1,0:T(8,128)(2,1)}, bf16[1024,512]{1,0:T(8,128)(2,1)}, bf16[1024,512]{1,0:T(8,128)(2,1)}) custom-call(s32[2]{0:T(128)} %pad_add_fusion.place_ref, bf16[1280,1024]{1,0:T(8,128)(2,1)} %copy.327.__4_.turned_normed, ...), custom_call_target="tpu_custom_call" | custom-call | flops 42949672960 | bytes 1 | tf_op jit(solution)/shard_map/attention_backward/pallas_call | solution.py:371
  541.1 4.0 fusion.35
  548.5 16.0 %normed_grad.1 = (bf16[4,256,1280]{2,1,0:T(8,128)(2,1)}, f32[256,1280]{1,0:T(8,128)}, f32[1,1280]{1,0:T(1,128)}) custom-call(s32[1]{0:T(128)} %bitcast.72.refs_0_, bf16[1024,1280]{1,0:T(8,128)(2,1)} %bitcast.312, bf16[3,1280,1280]{2,1,0:T(8,128)(2,1)} %bitcast.293, bf16[256,768]{1,0:T(8,128)(2,1)} %get-tuple-element.138.refs_3_, ...), custom_call_target="tpu_custom_call" | custom-call | flops 80530636800 | bytes 1 | tf_op jit(solution)/shard_map/normed_grad/pallas_call | solution.py:457
  566.2 3.7 fusion.48
  570.9 20.3 %collective-permute-done.31.__1_.__4_ = bf16[4,4,40,768]{3,2,1,0:T(8,128)(2,1)} collective-permute-done((bf16[4,4,40,768]{3,2,1,0:T(8,128)(2,1)}, bf16[4,4,40,768]{3,2,1,0:T(8,128)(2,1)}, u32[]{:S(2)}, u32[]{:S(2)}) %collective-permute-start.31) | collective-permute-done | bytes 983072 | tf_op jit(solution)/shard_map/ppermute | solution.py:88
  599.8 4.3 fusion.90
  604.1 3.7 collective-permute-start.35
  610.6 14.2 %collective-permute-done.38.__2_ = bf16[4,4,40,512]{3,2,1,0:T(8,128)(2,1)} collective-permute-done((bf16[4,4,40,512]{3,2,1,0:T(8,128)(2,1)}, bf16[4,4,40,512]{3,2,1,0:T(8,128)(2,1)}, u32[]{:S(2)}, u32[]{:S(2)}) %collective-permute-start.38) | collective-permute-done | bytes 655392 | tf_op jit(solution)/shard_map/ppermute | solution.py:88
  630.7 4.0 collective-permute-start.43
  634.7 27.4 %collective-permute-done.34.__1_ = bf16[4,40,768]{2,1,0:T(8,128)(2,1)S(1)} collective-permute-done((bf16[4,40,768]{2,1,0:T(8,128)(2,1)S(1)}, bf16[4,40,768]{2,1,0:T(8,128)(2,1)S(1)}, u32[]{:S(2)}, u32[]{:S(2)}) %collective-permute-start.34) | collective-permute-done | bytes 245792 | tf_op jit(solution)/shard_map/ppermute | solution.py:93
  682.9 4.5 all-to-all-start.4
  689.5 7.7 %collective-permute-done.41.__1_ = bf16[256,1280]{1,0:T(8,128)(2,1)} collective-permute-done((bf16[256,1280]{1,0:T(8,128)(2,1)}, bf16[256,1280]{1,0:T(8,128)(2,1)}, u32[]{:S(2)}, u32[]{:S(2)}) %collective-permute-start.41) | collective-permute-done | bytes 655392 | tf_op jit(solution)/shard_map/ppermute | solution.py:88
  705.6 3.3 fusion.86
  712.2 17.9 %fusion.78 = (bf16[2,3,320,896]{3,2,1,0:T(8,128)(2,1)}, f32[2,3,320,896]{3,2,1,0:T(8,128)}, f32[2,3,320,896]{3,2,1,0:T(8,128)}, f32[2,3,320,896]{3,2,1,0:T(8,128)}) fusion(f32[2,3,320,896]{3,2,1,0:T(8,128)} %param.39, f32[]{:T(128)S(6)} %min.3, f32[1,3,320,896]{3,2,1,0:T(8,128)S(1)} %copy-done.11, f32[1,3,320,896]{3,2,1,0:T(8,128)S(1)} %copy-done.10, ...), kind=kLoop, calls=%fused_computation.204 | loop fusion | flops 30965760 | bytes 51609604 | tf_op jit(solution)/shard_map/convert_element_type | solution.py:1068
  (412 shorter events, 164.4 us)
Async XLA Ops:
  7.2 43.9 %all-gather.9.cloned.1.call-start = ((), (), s32[]{:S(2)}) async-start(), calls=%async_computation.11 | async-start | bytes 2048000 | tf_op jit(solution)/shard_map/all_gather | solution.py:749
  9.3 112.6 %all-gather.11.cloned.1.call-start = ((), (), s32[]{:S(2)}) async-start(), calls=%async_computation.12 | async-start | bytes 4403200 | tf_op jit(solution)/shard_map/all_gather | solution.py:754
  51.1 217.2 %all-gather.13.cloned.1.call-start = ((), (), s32[]{:S(2)}) async-start(), calls=%async_computation.13 | async-start | bytes 8601600 | tf_op jit(solution)/shard_map/all_gather | solution.py:765
  52.5 30.9 %collective-permute-start.2 = (bf16[4,3,40,1280]{3,2,1,0:T(8,128)(2,1)S(1)}, bf16[4,3,40,1280]{3,2,1,0:T(8,128)(2,1)S(1)}, u32[]{:S(2)}, u32[]{:S(2)}) collective-permute-start(bf16[4,3,40,1280]{3,2,1,0:T(8,128)(2,1)S(1)} %slice.143), channel_id=1, source_target_pairs={{0,6},{1,7},{2,4},{3,5},{4,2},{5,3},{6,0},{7,1},{8,14},{9,15},{10,... | collective-permute-start | bytes 3686408 | tf_op jit(solution)/shard_map/ppermute | solution.py:88
  55.0 53.5 %collective-permute-start.1 = (bf16[4,3,40,1280]{3,2,1,0:T(8,128)(2,1)S(1)}, bf16[4,3,40,1280]{3,2,1,0:T(8,128)(2,1)S(1)}, u32[]{:S(2)}, u32[]{:S(2)}) collective-permute-start(bf16[4,3,40,1280]{3,2,1,0:T(8,128)(2,1)S(1)} %slice.143), channel_id=1, source_target_pairs={{0,4},{1,5},{2,6},{3,7},{4,0},{5,1},{6,2},{7,3},{8,12},{9,13},{10,... | collective-permute-start | bytes 3686408 | tf_op jit(solution)/shard_map/ppermute | solution.py:88
  55.5 54.0 %collective-permute-start = (bf16[4,3,40,1280]{3,2,1,0:T(8,128)(2,1)S(1)}, bf16[4,3,40,1280]{3,2,1,0:T(8,128)(2,1)}, u32[]{:S(2)}, u32[]{:S(2)}) collective-permute-start(bf16[4,3,40,1280]{3,2,1,0:T(8,128)(2,1)S(1)} %slice.143), channel_id=1, source_target_pairs={{0,2},{1,3},{2,0},{3,1},{4,6},{5,7},{6,4},{7,5},{8,10},{9,11},{10,... | collective-permute-start | bytes 3686408 | tf_op jit(solution)/shard_map/ppermute | solution.py:88
  134.7 242.0 %all-gather.15.cloned.1.call-start = ((), (), s32[]{:S(2)}) async-start(), calls=%async_computation.14 | async-start | bytes 8601600 | tf_op jit(solution)/shard_map/all_gather | solution.py:771
  148.2 20.1 %collective-permute-start.8 = (bf16[4,1,40,1280]{3,2,0,1:T(8,128)(2,1)S(1)}, bf16[4,1,40,1280]{3,2,0,1:T(8,128)(2,1)S(1)}, u32[]{:S(2)}, u32[]{:S(2)}) collective-permute-start(bf16[4,1,40,1280]{3,2,0,1:T(8,128)(2,1)S(1)} %slice_bitcast_fusion.3), channel_id=1, source_target_pairs={{0,4},{1,5},{2,6},{3,7},{4,0},{5,1},{6,2},{7,3},{8,12},{9,13},{10,... | collective-permute-start | bytes 1228808 | tf_op jit(solution)/shard_map/ppermute | solution.py:88
  149.4 18.9 %collective-permute-start.7 = (bf16[4,1,40,1280]{3,2,0,1:T(8,128)(2,1)S(1)}, bf16[4,1,40,1280]{3,2,0,1:T(8,128)(2,1)S(1)}, u32[]{:S(2)}, u32[]{:S(2)}) collective-permute-start(bf16[4,1,40,1280]{3,2,0,1:T(8,128)(2,1)S(1)} %slice_bitcast_fusion.3), channel_id=1, source_target_pairs={{0,2},{1,3},{2,0},{3,1},{4,6},{5,7},{6,4},{7,5},{8,10},{9,11},{10,... | collective-permute-start | bytes 1228808 | tf_op jit(solution)/shard_map/ppermute | solution.py:88
  169.7 22.3 %collective-permute-start.10 = (bf16[4,4,1,40,1280]{4,3,2,1,0:T(8,128)(2,1)}, bf16[4,4,1,40,1280]{4,3,2,1,0:T(8,128)(2,1)}, u32[]{:S(2)}, u32[]{:S(2)}) collective-permute-start(bf16[4,4,1,40,1280]{4,3,2,1,0:T(8,128)(2,1)} %pad_maximum_fusion.4.even), channel_id=1, source_target_pairs={{0,1},{1,0},{2,3},{3,2},{4,5},{5,4},{6,7},{7,6},{8,9},{9,8},{10,11... | collective-permute-start | bytes 4915208 | tf_op jit(solution)/shard_map/ppermute | solution.py:88
  183.1 32.7 %collective-permute-start.6 = (bf16[256,1280]{1,0:T(8,128)(2,1)}, bf16[256,1280]{1,0:T(8,128)(2,1)}, u32[]{:S(2)}, u32[]{:S(2)}) collective-permute-start(bf16[256,1280]{1,0:T(8,128)(2,1)} %hold.21), channel_id=1, source_target_pairs={{0,6},{1,7},{2,4},{3,5},{4,2},{5,3},{6,0},{7,1},{8,14},{9,15},{10,... | collective-permute-start | bytes 1966088 | tf_op jit(solution)/shard_map/ppermute | solution.py:88
  184.2 31.6 %collective-permute-start.5 = (bf16[256,1280]{1,0:T(8,128)(2,1)}, bf16[256,1280]{1,0:T(8,128)(2,1)}, u32[]{:S(2)}, u32[]{:S(2)}) collective-permute-start(bf16[256,1280]{1,0:T(8,128)(2,1)} %hold.21), channel_id=1, source_target_pairs={{0,4},{1,5},{2,6},{3,7},{4,0},{5,1},{6,2},{7,3},{8,12},{9,13},{10,... | collective-permute-start | bytes 1966088 | tf_op jit(solution)/shard_map/ppermute | solution.py:88
  185.4 30.4 %collective-permute-start.4 = (bf16[256,1280]{1,0:T(8,128)(2,1)}, bf16[256,1280]{1,0:T(8,128)(2,1)}, u32[]{:S(2)}, u32[]{:S(2)}) collective-permute-start(bf16[256,1280]{1,0:T(8,128)(2,1)} %hold.21), channel_id=1, source_target_pairs={{0,2},{1,3},{2,0},{3,1},{4,6},{5,7},{6,4},{7,5},{8,10},{9,11},{10,... | collective-permute-start | bytes 1966088 | tf_op jit(solution)/shard_map/ppermute | solution.py:88
  219.3 18.7 %collective-permute-start.13 = (bf16[256,1280]{1,0:T(8,128)(2,1)S(1)}, bf16[256,1280]{1,0:T(8,128)(2,1)}, u32[]{:S(2)}, u32[]{:S(2)}) collective-permute-start(bf16[256,1280]{1,0:T(8,128)(2,1)S(1)} %multiply_convert_fusion.1.tokens_ref), channel_id=1, source_target_pairs={{0,6},{1,7},{2,4},{3,5},{4,2},{5,3},{6,0},{7,1},{8,14},{9,15},{10,... | collective-permute-start | bytes 1966088 | tf_op jit(solution)/shard_map/ppermute | solution.py:88
  220.6 30.1 %collective-permute-start.12 = (bf16[256,1280]{1,0:T(8,128)(2,1)S(1)}, bf16[256,1280]{1,0:T(8,128)(2,1)}, u32[]{:S(2)}, u32[]{:S(2)}) collective-permute-start(bf16[256,1280]{1,0:T(8,128)(2,1)S(1)} %multiply_convert_fusion.1.tokens_ref), channel_id=1, source_target_pairs={{0,4},{1,5},{2,6},{3,7},{4,0},{5,1},{6,2},{7,3},{8,12},{9,13},{10,... | collective-permute-start | bytes 1966088 | tf_op jit(solution)/shard_map/ppermute | solution.py:88
  221.7 29.0 %collective-permute-start.11 = (bf16[256,1280]{1,0:T(8,128)(2,1)S(1)}, bf16[256,1280]{1,0:T(8,128)(2,1)}, u32[]{:S(2)}, u32[]{:S(2)}) collective-permute-start(bf16[256,1280]{1,0:T(8,128)(2,1)S(1)} %multiply_convert_fusion.1.tokens_ref), channel_id=1, source_target_pairs={{0,2},{1,3},{2,0},{3,1},{4,6},{5,7},{6,4},{7,5},{8,10},{9,11},{10,... | collective-permute-start | bytes 1966088 | tf_op jit(solution)/shard_map/ppermute | solution.py:88
  227.3 40.9 %collective-permute-start.15 = (bf16[4,256,1280]{2,1,0:T(8,128)(2,1)S(1)}, bf16[4,256,1280]{2,1,0:T(8,128)(2,1)}, u32[]{:S(2)}, u32[]{:S(2)}) collective-permute-start(bf16[4,256,1280]{2,1,0:T(8,128)(2,1)S(1)} %pad_maximum_fusion.3.refs_3_.even_c), channel_id=1, source_target_pairs={{0,1},{1,0},{2,3},{3,2},{4,5},{5,4},{6,7},{7,6},{8,9},{9,8},{10,11... | collective-permute-start | bytes 7864328 | tf_op jit(solution)/shard_map/ppermute | solution.py:88
  261.7 257.9 %reduce-scatter.4.cloned.1.call-start = ((), (), s32[]{:S(2)}) async-start(), calls=%async_computation.8 | async-start | bytes 8601600 | tf_op jit(solution)/shard_map/reduce_scatter | solution.py:889
  268.3 50.0 %collective-permute-start.18 = (bf16[4,3,40,896]{3,2,1,0:T(8,128)(2,1)}, bf16[4,3,40,896]{3,2,1,0:T(8,128)(2,1)S(1)}, u32[]{:S(2)}, u32[]{:S(2)}) collective-permute-start(bf16[4,3,40,896]{3,2,1,0:T(8,128)(2,1)} %hold.24), channel_id=1, source_target_pairs={{0,6},{1,7},{2,4},{3,5},{4,2},{5,3},{6,0},{7,1},{8,14},{9,15},{10,... | collective-permute-start | bytes 2580488 | tf_op jit(solution)/shard_map/ppermute | solution.py:88
  268.9 49.4 %collective-permute-start.17 = (bf16[4,3,40,896]{3,2,1,0:T(8,128)(2,1)}, bf16[4,3,40,896]{3,2,1,0:T(8,128)(2,1)S(1)}, u32[]{:S(2)}, u32[]{:S(2)}) collective-permute-start(bf16[4,3,40,896]{3,2,1,0:T(8,128)(2,1)} %hold.24), channel_id=1, source_target_pairs={{0,4},{1,5},{2,6},{3,7},{4,0},{5,1},{6,2},{7,3},{8,12},{9,13},{10,... | collective-permute-start | bytes 2580488 | tf_op jit(solution)/shard_map/ppermute | solution.py:88
  270.4 48.0 %collective-permute-start.16 = (bf16[4,3,40,896]{3,2,1,0:T(8,128)(2,1)}, bf16[4,3,40,896]{3,2,1,0:T(8,128)(2,1)}, u32[]{:S(2)}, u32[]{:S(2)}) collective-permute-start(bf16[4,3,40,896]{3,2,1,0:T(8,128)(2,1)} %hold.24), channel_id=1, source_target_pairs={{0,2},{1,3},{2,0},{3,1},{4,6},{5,7},{6,4},{7,5},{8,10},{9,11},{10,... | collective-permute-start | bytes 2580488 | tf_op jit(solution)/shard_map/ppermute | solution.py:88
  321.7 22.6 %collective-permute-start.19 = (bf16[4,4,3,40,896]{4,3,2,1,0:T(8,128)(2,1)}, bf16[4,4,3,40,896]{4,3,2,1,0:T(8,128)(2,1)S(1)}, u32[]{:S(2)}, u32[]{:S(2)}) collective-permute-start(bf16[4,4,3,40,896]{4,3,2,1,0:T(8,128)(2,1)} %hold.25.even), channel_id=1, source_target_pairs={{0,1},{1,0},{2,3},{3,2},{4,5},{5,4},{6,7},{7,6},{8,9},{9,8},{10,11... | collective-permute-start | bytes 10321928 | tf_op jit(solution)/shard_map/ppermute | solution.py:88
  376.7 52.6 %collective-permute-start.21 = (bf16[3,4,40,896]{3,2,1,0:T(8,128)(2,1)}, bf16[3,4,40,896]{3,2,1,0:T(8,128)(2,1)S(1)}, u32[]{:S(2)}, u32[]{:S(2)}) collective-permute-start(bf16[3,4,40,896]{3,2,1,0:T(8,128)(2,1)} %get-tuple-element.121), channel_id=1, source_target_pairs={{0,2},{1,3},{2,0},{3,1},{4,6},{5,7},{6,4},{7,5},{8,10},{9,11},{10,... | collective-permute-start | bytes 2580488 | tf_op jit(solution)/shard_map/ppermute | solution.py:88
  377.3 52.1 %collective-permute-start.22 = (bf16[3,4,40,896]{3,2,1,0:T(8,128)(2,1)}, bf16[3,4,40,896]{3,2,1,0:T(8,128)(2,1)S(1)}, u32[]{:S(2)}, u32[]{:S(2)}) collective-permute-start(bf16[3,4,40,896]{3,2,1,0:T(8,128)(2,1)} %get-tuple-element.122), channel_id=1, source_target_pairs={{0,4},{1,5},{2,6},{3,7},{4,0},{5,1},{6,2},{7,3},{8,12},{9,13},{10,... | collective-permute-start | bytes 2580488 | tf_op jit(solution)/shard_map/ppermute | solution.py:88
  377.9 51.4 %collective-permute-start.23 = (bf16[3,4,40,896]{3,2,1,0:T(8,128)(2,1)}, bf16[3,4,40,896]{3,2,1,0:T(8,128)(2,1)S(1)}, u32[]{:S(2)}, u32[]{:S(2)}) collective-permute-start(bf16[3,4,40,896]{3,2,1,0:T(8,128)(2,1)} %get-tuple-element.123), channel_id=1, source_target_pairs={{0,6},{1,7},{2,4},{3,5},{4,2},{5,3},{6,0},{7,1},{8,14},{9,15},{10,... | collective-permute-start | bytes 2580488 | tf_op jit(solution)/shard_map/ppermute | solution.py:88
  445.8 47.1 %collective-permute-start.28 = (bf16[256,1280]{1,0:T(8,128)(2,1)}, bf16[256,1280]{1,0:T(8,128)(2,1)S(1)}, u32[]{:S(2)}, u32[]{:S(2)}) collective-permute-start(bf16[256,1280]{1,0:T(8,128)(2,1)} %get-tuple-element.298.__3_), channel_id=1, source_target_pairs={{0,6},{1,7},{2,4},{3,5},{4,2},{5,3},{6,0},{7,1},{8,14},{9,15},{10,... | collective-permute-start | bytes 1966088 | tf_op jit(solution)/shard_map/ppermute | solution.py:88
  446.5 46.4 %collective-permute-start.27 = (bf16[256,1280]{1,0:T(8,128)(2,1)}, bf16[256,1280]{1,0:T(8,128)(2,1)}, u32[]{:S(2)}, u32[]{:S(2)}) collective-permute-start(bf16[256,1280]{1,0:T(8,128)(2,1)} %get-tuple-element.299.__2_), channel_id=1, source_target_pairs={{0,4},{1,5},{2,6},{3,7},{4,0},{5,1},{6,2},{7,3},{8,12},{9,13},{10,... | collective-permute-start | bytes 1966088 | tf_op jit(solution)/shard_map/ppermute | solution.py:88
  471.8 21.1 %collective-permute-start.26 = (bf16[256,1280]{1,0:T(8,128)(2,1)}, bf16[256,1280]{1,0:T(8,128)(2,1)}, u32[]{:S(2)}, u32[]{:S(2)}) collective-permute-start(bf16[256,1280]{1,0:T(8,128)(2,1)} %get-tuple-element.300.__1_), channel_id=1, source_target_pairs={{0,2},{1,3},{2,0},{3,1},{4,6},{5,7},{6,4},{7,5},{8,10},{9,11},{10,... | collective-permute-start | bytes 1966088 | tf_op jit(solution)/shard_map/ppermute | solution.py:88
  478.7 191.8 %reduce-scatter.6.cloned.1.call-start = ((), (), s32[]{:S(2)}) async-start(), calls=%async_computation.9 | async-start | bytes 9891840 | tf_op jit(solution)/shard_map/reduce_scatter | solution.py:889
  519.2 20.5 %collective-permute-start.29 = (bf16[4,16,40,768]{3,2,1,0:T(8,128)(2,1)}, bf16[4,16,40,768]{3,2,1,0:T(8,128)(2,1)}, u32[]{:S(2)}, u32[]{:S(2)}) collective-permute-start(bf16[4,16,40,768]{3,2,1,0:T(8,128)(2,1)} %get-tuple-element.137.refs_0_), channel_id=1, source_target_pairs={{0,1},{1,0},{2,3},{3,2},{4,5},{5,4},{6,7},{7,6},{8,9},{9,8},{10,11... | collective-permute-start | bytes 11796488 | tf_op jit(solution)/shard_map/ppermute | solution.py:88
  534.2 30.3 %collective-permute-start.36 = (bf16[4,16,40,512]{3,2,1,0:T(8,128)(2,1)}, bf16[4,16,40,512]{3,2,1,0:T(8,128)(2,1)S(1)}, u32[]{:S(2)}, u32[]{:S(2)}) collective-permute-start(bf16[4,16,40,512]{3,2,1,0:T(8,128)(2,1)} %get-tuple-element.149), channel_id=1, source_target_pairs={{0,1},{1,0},{2,3},{3,2},{4,5},{5,4},{6,7},{7,6},{8,9},{9,8},{10,11... | collective-permute-start | bytes 7864328 | tf_op jit(solution)/shard_map/ppermute | solution.py:88
  545.0 25.9 %collective-permute-start.32 = (bf16[4,4,40,768]{3,2,1,0:T(8,128)(2,1)}, bf16[4,4,40,768]{3,2,1,0:T(8,128)(2,1)}, u32[]{:S(2)}, u32[]{:S(2)}) collective-permute-start(bf16[4,4,40,768]{3,2,1,0:T(8,128)(2,1)} %get-tuple-element.286), channel_id=1, source_target_pairs={{0,6},{1,7},{2,4},{3,5},{4,2},{5,3},{6,0},{7,1},{8,14},{9,15},{10,... | collective-permute-start | bytes 2949128 | tf_op jit(solution)/shard_map/ppermute | solution.py:88
  547.7 43.5 %collective-permute-start.31 = (bf16[4,4,40,768]{3,2,1,0:T(8,128)(2,1)}, bf16[4,4,40,768]{3,2,1,0:T(8,128)(2,1)}, u32[]{:S(2)}, u32[]{:S(2)}) collective-permute-start(bf16[4,4,40,768]{3,2,1,0:T(8,128)(2,1)} %get-tuple-element.287), channel_id=1, source_target_pairs={{0,4},{1,5},{2,6},{3,7},{4,0},{5,1},{6,2},{7,3},{8,12},{9,13},{10,... | collective-permute-start | bytes 2949128 | tf_op jit(solution)/shard_map/ppermute | solution.py:88
  548.2 43.2 %collective-permute-start.30 = (bf16[4,4,40,768]{3,2,1,0:T(8,128)(2,1)}, bf16[4,4,40,768]{3,2,1,0:T(8,128)(2,1)}, u32[]{:S(2)}, u32[]{:S(2)}) collective-permute-start(bf16[4,4,40,768]{3,2,1,0:T(8,128)(2,1)} %get-tuple-element.288.refs_9_.__1_), channel_id=1, source_target_pairs={{0,2},{1,3},{2,0},{3,1},{4,6},{5,7},{6,4},{7,5},{8,10},{9,11},{10,... | collective-permute-start | bytes 2949128 | tf_op jit(solution)/shard_map/ppermute | solution.py:88
  591.3 18.9 %collective-permute-start.37 = (bf16[4,4,40,512]{3,2,1,0:T(8,128)(2,1)}, bf16[4,4,40,512]{3,2,1,0:T(8,128)(2,1)S(1)}, u32[]{:S(2)}, u32[]{:S(2)}) collective-permute-start(bf16[4,4,40,512]{3,2,1,0:T(8,128)(2,1)} %get-tuple-element.150), channel_id=1, source_target_pairs={{0,2},{1,3},{2,0},{3,1},{4,6},{5,7},{6,4},{7,5},{8,10},{9,11},{10,... | collective-permute-start | bytes 1966088 | tf_op jit(solution)/shard_map/ppermute | solution.py:88
  592.8 31.9 %collective-permute-start.38 = (bf16[4,4,40,512]{3,2,1,0:T(8,128)(2,1)}, bf16[4,4,40,512]{3,2,1,0:T(8,128)(2,1)}, u32[]{:S(2)}, u32[]{:S(2)}) collective-permute-start(bf16[4,4,40,512]{3,2,1,0:T(8,128)(2,1)} %get-tuple-element.151), channel_id=1, source_target_pairs={{0,4},{1,5},{2,6},{3,7},{4,0},{5,1},{6,2},{7,3},{8,12},{9,13},{10,... | collective-permute-start | bytes 1966088 | tf_op jit(solution)/shard_map/ppermute | solution.py:88
  593.5 31.3 %collective-permute-start.39 = (bf16[4,4,40,512]{3,2,1,0:T(8,128)(2,1)}, bf16[4,4,40,512]{3,2,1,0:T(8,128)(2,1)}, u32[]{:S(2)}, u32[]{:S(2)}) collective-permute-start(bf16[4,4,40,512]{3,2,1,0:T(8,128)(2,1)} %get-tuple-element.152), channel_id=1, source_target_pairs={{0,6},{1,7},{2,4},{3,5},{4,2},{5,3},{6,0},{7,1},{8,14},{9,15},{10,... | collective-permute-start | bytes 1966088 | tf_op jit(solution)/shard_map/ppermute | solution.py:88
  595.6 70.9 %all-to-all-start.3 = ((f32[32,8,128]{2,1,0:T(8,128)}), f32[32,8,128]{2,1,0:T(8,128)S(1)}, u32[]{:S(2)}, u32[]{:S(2)}) async-start(f32[32,8,128]{2,1,0:T(8,128)} %bitcast.140), calls=%async_computation.5 | async-start | bytes 262144 | tf_op jit(solution)/shard_map/all_to_all | solution.py:968
  598.2 131.9 %reduce-scatter.8.cloned.1.call-start = ((), (), s32[]{:S(2)}) async-start(), calls=%async_computation.10 | async-start | bytes 3276800 | tf_op jit(solution)/shard_map/reduce_scatter | solution.py:981
  604.1 26.6 %collective-permute-start.35 = (bf16[4,40,768]{2,1,0:T(8,128)(2,1)S(1)}, bf16[4,40,768]{2,1,0:T(8,128)(2,1)S(1)}, u32[]{:S(2)}, u32[]{:S(2)}) collective-permute-start(bf16[4,40,768]{2,1,0:T(8,128)(2,1)S(1)} %get-tuple-element.305), channel_id=1, source_target_pairs={{0,24},{8,0},{16,8},{24,16},{1,25},{9,1},{17,9},{25,17},{2,26},{10... | collective-permute-start | bytes 737288 | tf_op jit(solution)/shard_map/ppermute | solution.py:93
  607.8 54.4 %collective-permute-start.34 = (bf16[4,40,768]{2,1,0:T(8,128)(2,1)S(1)}, bf16[4,40,768]{2,1,0:T(8,128)(2,1)S(1)}, u32[]{:S(2)}, u32[]{:S(2)}) collective-permute-start(bf16[4,40,768]{2,1,0:T(8,128)(2,1)S(1)} %get-tuple-element.306), channel_id=1, source_target_pairs={{0,16},{8,24},{16,0},{24,8},{1,17},{9,25},{17,1},{25,9},{2,18},{10... | collective-permute-start | bytes 737288 | tf_op jit(solution)/shard_map/ppermute | solution.py:93
  610.2 51.9 %collective-permute-start.33 = (bf16[4,40,768]{2,1,0:T(8,128)(2,1)S(1)}, bf16[4,40,768]{2,1,0:T(8,128)(2,1)S(1)}, u32[]{:S(2)}, u32[]{:S(2)}) collective-permute-start(bf16[4,40,768]{2,1,0:T(8,128)(2,1)S(1)} %get-tuple-element.307), channel_id=1, source_target_pairs={{0,8},{8,16},{16,24},{24,0},{1,9},{9,17},{17,25},{25,1},{2,10},{10... | collective-permute-start | bytes 737288 | tf_op jit(solution)/shard_map/ppermute | solution.py:93
  628.8 46.0 %collective-permute-start.45 = (bf16[4,40,512]{2,1,0:T(8,128)(2,1)}, bf16[4,40,512]{2,1,0:T(8,128)(2,1)}, u32[]{:S(2)}, u32[]{:S(2)}) collective-permute-start(bf16[4,40,512]{2,1,0:T(8,128)(2,1)} %get-tuple-element.308), channel_id=1, source_target_pairs={{0,24},{8,0},{16,8},{24,16},{1,25},{9,1},{17,9},{25,17},{2,26},{10... | collective-permute-start | bytes 491528 | tf_op jit(solution)/shard_map/ppermute | solution.py:93
  629.1 46.4 %collective-permute-start.44 = (bf16[4,40,512]{2,1,0:T(8,128)(2,1)}, bf16[4,40,512]{2,1,0:T(8,128)(2,1)}, u32[]{:S(2)}, u32[]{:S(2)}) collective-permute-start(bf16[4,40,512]{2,1,0:T(8,128)(2,1)} %get-tuple-element.309), channel_id=1, source_target_pairs={{0,16},{8,24},{16,0},{24,8},{1,17},{9,25},{17,1},{25,9},{2,18},{10... | collective-permute-start | bytes 491528 | tf_op jit(solution)/shard_map/ppermute | solution.py:93
  630.7 44.8 %collective-permute-start.43 = (bf16[4,40,512]{2,1,0:T(8,128)(2,1)}, bf16[4,40,512]{2,1,0:T(8,128)(2,1)}, u32[]{:S(2)}, u32[]{:S(2)}) collective-permute-start(bf16[4,40,512]{2,1,0:T(8,128)(2,1)} %get-tuple-element.310), channel_id=1, source_target_pairs={{0,8},{8,16},{16,24},{24,0},{1,9},{9,17},{17,25},{25,1},{2,10},{10... | collective-permute-start | bytes 491528 | tf_op jit(solution)/shard_map/ppermute | solution.py:93
  663.5 25.9 %collective-permute-start.40 = (bf16[256,1280]{1,0:T(8,128)(2,1)}, bf16[256,1280]{1,0:T(8,128)(2,1)S(1)}, u32[]{:S(2)}, u32[]{:S(2)}) collective-permute-start(bf16[256,1280]{1,0:T(8,128)(2,1)} %get-tuple-element.156), channel_id=1, source_target_pairs={{0,2},{1,3},{2,0},{3,1},{4,6},{5,7},{6,4},{7,5},{8,10},{9,11},{10,... | collective-permute-start | bytes 1966088 | tf_op jit(solution)/shard_map/ppermute | solution.py:88
  665.1 32.1 %collective-permute-start.41 = (bf16[256,1280]{1,0:T(8,128)(2,1)}, bf16[256,1280]{1,0:T(8,128)(2,1)}, u32[]{:S(2)}, u32[]{:S(2)}) collective-permute-start(bf16[256,1280]{1,0:T(8,128)(2,1)} %get-tuple-element.157), channel_id=1, source_target_pairs={{0,4},{1,5},{2,6},{3,7},{4,0},{5,1},{6,2},{7,3},{8,12},{9,13},{10,... | collective-permute-start | bytes 1966088 | tf_op jit(solution)/shard_map/ppermute | solution.py:88
  674.9 22.3 %collective-permute-start.42 = (bf16[256,1280]{1,0:T(8,128)(2,1)}, bf16[256,1280]{1,0:T(8,128)(2,1)}, u32[]{:S(2)}, u32[]{:S(2)}) collective-permute-start(bf16[256,1280]{1,0:T(8,128)(2,1)} %get-tuple-element.158), channel_id=1, source_target_pairs={{0,6},{1,7},{2,4},{3,5},{4,2},{5,3},{6,0},{7,1},{8,14},{9,15},{10,... | collective-permute-start | bytes 1966088 | tf_op jit(solution)/shard_map/ppermute | solution.py:88
  (92 other events, 1363.5 us)
Sparse Core Ops, SparseCore 0:
  10.2 40.8 all-gather.8
  53.2 68.5 all-gather.10
  125.4 124.9 all-gather.12
  251.8 123.1 all-gather.14
  377.7 118.5 reduce-scatter.3
  498.6 164.6 reduce-scatter.5
  670.7 55.8 reduce-scatter.7
